TPU v7x, 32 devices: a whole 2x2x4 slice. The times are simulated.
32 devices in a mesh: dp: 8 (over z, core), seq: 4 (over y, x).
Axes of the slice: x: 2, y: 2, z: 4, core: 2. Of those that a mesh axis runs over, the one named last changes fastest.
Arguments:
- tokens: bfloat16 [32, 2048, 768], P('dp', 'seq'), may hold values from -6 to 6
- lengths: int32 [32], P('dp'), may hold values from 1024 to 2048, as said below
- cotangent: bfloat16 [32, 2048, 768], P('dp', 'seq'), may hold values from -6 to 6
- w_query: bfloat16 [768, 768], P(('dp', 'seq')), may hold values from -0.21875 to 0.21875
- b_query: bfloat16 [768], P(('dp', 'seq')), may hold values from -3 to 3
- w_key: bfloat16 [768, 768], P(('dp', 'seq')), may hold values from -0.21875 to 0.21875
- w_value: bfloat16 [768, 768], P(('dp', 'seq')), may hold values from -0.21875 to 0.21875
- b_value: bfloat16 [768], P(('dp', 'seq')), may hold values from -0.3125 to 0.3125
- w_out: bfloat16 [768, 768], P(('dp', 'seq')), may hold values from -3.5 to 3.5
- b_out: bfloat16 [768], P(('dp', 'seq')), may hold values from -3 to 3
- gain_one: bfloat16 [768], P(('dp', 'seq')), may hold values from 0.099609375 to 1.8984375
- shift_one: bfloat16 [768], P(('dp', 'seq')), may hold values from -1.75 to 1.75
- w_up: bfloat16 [768, 3072], P(('dp', 'seq')), may hold values from -0.21875 to 0.21875
- b_up: bfloat16 [3072], P(('dp', 'seq')), may hold values from -3 to 3
- w_down: bfloat16 [3072, 768], P(('dp', 'seq')), may hold values from -0.109375 to 0.109375
- b_down: bfloat16 [768], P(('dp', 'seq')), may hold values from -3 to 3
- gain_two: bfloat16 [768], P(('dp', 'seq')), may hold values from 0.099609375 to 1.8984375
- shift_two: bfloat16 [768], P(('dp', 'seq')), may hold values from -1.75 to 1.75
Outputs:
- output: bfloat16 [32, 2048, 768], P('dp', 'seq')
- grad_tokens: float32 [32, 2048, 768], P('dp', 'seq')
- grad_w_query: float32 [768, 768], P(('dp', 'seq'))
- grad_b_query: float32 [768], P(('dp', 'seq'))
- grad_w_key: float32 [768, 768], P(('dp', 'seq'))
- grad_w_value: float32 [768, 768], P(('dp', 'seq'))
- grad_b_value: float32 [768], P(('dp', 'seq'))
- grad_w_out: float32 [768, 768], P(('dp', 'seq'))
- output_bias_gradient: float32 [768], P(('dp', 'seq'))
- grad_gain_one: float32 [768], P(('dp', 'seq'))
- grad_shift_one: float32 [768], P(('dp', 'seq'))
- grad_w_up: float32 [768, 3072], P(('dp', 'seq'))
- grad_b_up: float32 [3072], P(('dp', 'seq'))
- grad_w_down: float32 [3072, 768], P(('dp', 'seq'))
- grad_b_down: float32 [768], P(('dp', 'seq'))
- grad_gain_two: float32 [768], P(('dp', 'seq'))
- grad_shift_two: float32 [768], P(('dp', 'seq'))
Inputs may be any that keep to these rules, and one draw needn't show every extreme that they name: lengths[s] counts the valid tokens of sequence s from its start; in every draw some sequence is full and some has exactly half of its 2048 slots.
All inputs are finite; a program needn't handle non-finite values.
Results may differ from a plain program's by a relative error of at most 0.015.
Values may be sent and summed in bfloat16 or wider, within the bound.
No kernel may reach another device: no remote copies, remote signals or barrier semaphores. Data moves between devices by JAX's collectives and lax.ppermute only.
A program may use at most 768 MiB of HBM per device.

v0:
```python
import jax
import jax.numpy as jnp
from jax import lax
from jax.sharding import PartitionSpec as P

H = 12
HD = 64
MB = 4


epsilon = 1e-06


def layer_norm(layer_input_rows, norm_gain, norm_shift):
    centre = layer_input_rows - jnp.mean(layer_input_rows, -1, keepdims=True)
    spread = jnp.mean(centre * centre, -1, keepdims=True)
    return centre * lax.rsqrt(spread + epsilon) * norm_gain + norm_shift


def gelu_exact(values):
    return jax.nn.gelu(values, approximate=False)


def matmul(former, latter):
    return jnp.dot(former, latter, preferred_element_type=jnp.float32)


def former_product(former, latter):
    return lax.dot_general(
        former, latter, (((0,), (0,)), ((), ())), preferred_element_type=jnp.float32
    )


def latter_product(former, latter):
    return lax.dot_general(
        former, latter, (((1,), (1,)), ((), ())), preferred_element_type=jnp.float32
    )


def widen(vector):
    return vector.astype(jnp.float32)


def body(
    tokens,
    lengths,
    cotangent,
    w_query,
    b_query,
    w_key,
    w_value,
    b_value,
    w_out,
    b_out,
    gain_one,
    shift_one,
    w_up,
    b_up,
    w_down,
    b_down,
    gain_two,
    shift_two,
):
    shards = (
        w_query,
        b_query,
        w_key,
        w_value,
        b_value,
        w_out,
        b_out,
        gain_one,
        shift_one,
        w_up,
        b_up,
        w_down,
        b_down,
        gain_two,
        shift_two,
    )
    per_batch = tokens.shape[0] // MB
    block_rows = tokens.shape[1]
    model_width = tokens.shape[2]
    head_count = H
    head_size = HD
    flat_rows = per_batch * block_rows
    full_length = block_rows * lax.axis_size("seq")
    offset = lax.axis_index("seq") * block_rows
    positions = jnp.arange(full_length, dtype=jnp.int32)
    own_positions = offset + jnp.arange(block_rows, dtype=jnp.int32)
    score_scale = head_size ** (-0.5)
    owners = lax.axis_size(("dp", "seq"))
    totals = [
        jnp.zeros((shard_piece.shape[0] * owners,) + shard_piece.shape[1:], jnp.float32)
        for shard_piece in shards
    ]
    outputs = []
    input_grads = []
    for micro_batch in range(MB):
        leading_row = micro_batch * per_batch
        own_tokens = tokens[leading_row : leading_row + per_batch]
        own_lengths = lengths[leading_row : leading_row + per_batch]
        own_cots = cotangent[leading_row : leading_row + per_batch]
        fore_weights = (
            lax.all_gather(shards[0], ("dp", "seq"), axis=0, tiled=True),
            lax.all_gather(shards[1], ("dp", "seq"), axis=0, tiled=True),
            lax.all_gather(shards[2], ("dp", "seq"), axis=0, tiled=True),
            lax.all_gather(shards[3], ("dp", "seq"), axis=0, tiled=True),
            lax.all_gather(shards[4], ("dp", "seq"), axis=0, tiled=True),
            lax.all_gather(shards[5], ("dp", "seq"), axis=0, tiled=True),
            lax.all_gather(shards[6], ("dp", "seq"), axis=0, tiled=True),
            lax.all_gather(shards[7], ("dp", "seq"), axis=0, tiled=True),
            lax.all_gather(shards[8], ("dp", "seq"), axis=0, tiled=True),
            lax.all_gather(shards[9], ("dp", "seq"), axis=0, tiled=True),
            lax.all_gather(shards[10], ("dp", "seq"), axis=0, tiled=True),
            lax.all_gather(shards[11], ("dp", "seq"), axis=0, tiled=True),
            lax.all_gather(shards[12], ("dp", "seq"), axis=0, tiled=True),
            lax.all_gather(shards[13], ("dp", "seq"), axis=0, tiled=True),
            lax.all_gather(shards[14], ("dp", "seq"), axis=0, tiled=True),
        )
        flat_tokens = own_tokens.reshape(flat_rows, model_width)
        query_low = (matmul(flat_tokens, fore_weights[0]) + widen(fore_weights[1])).astype(
            jnp.bfloat16
        )
        key_low = matmul(flat_tokens, fore_weights[2]).astype(jnp.bfloat16)
        value_low = (matmul(flat_tokens, fore_weights[3]) + widen(fore_weights[4])).astype(
            jnp.bfloat16
        )
        key_block = key_low.reshape(per_batch, block_rows, model_width)
        value_block = value_low.reshape(per_batch, block_rows, model_width)
        gathered_keys, gathered_values = (
            lax.all_gather(key_block, "seq", axis=1, tiled=True),
            lax.all_gather(value_block, "seq", axis=1, tiled=True),
        )
        query_heads = query_low.reshape(per_batch, block_rows, head_count, head_size)
        visible = (positions[None, :] < own_lengths[:, None])[:, None, None, :]

        def score_block(key_all):
            key_heads = key_all.reshape(per_batch, full_length, head_count, head_size)
            raw_scores = jnp.einsum(
                "pqhd,pkhd->phqk", query_heads, key_heads, preferred_element_type=jnp.float32
            )
            return jnp.where(visible, raw_scores * score_scale, -1e30)

        scores = score_block(gathered_keys)
        logarithm_totals = jax.nn.logsumexp(scores, axis=-1, keepdims=True)
        chances_low = jnp.exp(scores - logarithm_totals).astype(jnp.bfloat16)
        value_heads = gathered_values.reshape(per_batch, full_length, head_count, head_size)
        mixed_heads = jnp.einsum(
            "phqk,pkhd->pqhd", chances_low, value_heads, preferred_element_type=jnp.float32
        )
        mixed_low = mixed_heads.reshape(flat_rows, model_width).astype(jnp.bfloat16)
        branch = matmul(mixed_low, fore_weights[5]) + widen(fore_weights[6])
        resid_one = flat_tokens.astype(jnp.float32) + branch
        normed = layer_norm(resid_one, widen(fore_weights[7]), widen(fore_weights[8]))
        normed_low = normed.astype(jnp.bfloat16)
        hidden = matmul(normed_low, fore_weights[9]) + widen(fore_weights[10])
        active_low = gelu_exact(hidden).astype(jnp.bfloat16)
        feed_out = matmul(active_low, fore_weights[11]) + widen(fore_weights[12])
        resid_two = normed + feed_out
        result = layer_norm(resid_two, widen(fore_weights[13]), widen(fore_weights[14]))
        outputs.append(result.astype(jnp.bfloat16).reshape(per_batch, block_rows, model_width))
        back_weights = (
            lax.all_gather(shards[0], ("dp", "seq"), axis=0, tiled=True),
            lax.all_gather(shards[1], ("dp", "seq"), axis=0, tiled=True),
            lax.all_gather(shards[2], ("dp", "seq"), axis=0, tiled=True),
            lax.all_gather(shards[3], ("dp", "seq"), axis=0, tiled=True),
            lax.all_gather(shards[4], ("dp", "seq"), axis=0, tiled=True),
            lax.all_gather(shards[5], ("dp", "seq"), axis=0, tiled=True),
            lax.all_gather(shards[6], ("dp", "seq"), axis=0, tiled=True),
            lax.all_gather(shards[7], ("dp", "seq"), axis=0, tiled=True),
            lax.all_gather(shards[8], ("dp", "seq"), axis=0, tiled=True),
            lax.all_gather(shards[9], ("dp", "seq"), axis=0, tiled=True),
            lax.all_gather(shards[10], ("dp", "seq"), axis=0, tiled=True),
            lax.all_gather(shards[11], ("dp", "seq"), axis=0, tiled=True),
            lax.all_gather(shards[12], ("dp", "seq"), axis=0, tiled=True),
            lax.all_gather(shards[13], ("dp", "seq"), axis=0, tiled=True),
            lax.all_gather(shards[14], ("dp", "seq"), axis=0, tiled=True),
        )
        live_rows = (
            (own_positions[None, :] < own_lengths[:, None])
            .astype(jnp.float32)
            .reshape(flat_rows, 1)
        )
        incoming = own_cots.reshape(flat_rows, model_width).astype(jnp.float32) * live_rows
        _, second_pull = jax.vjp(
            layer_norm, resid_two, widen(back_weights[13]), widen(back_weights[14])
        )
        grad_two, grad_gain_two, grad_shift_two = second_pull(incoming)
        feed_low = grad_two.astype(jnp.bfloat16)
        totals[11] = totals[11] + former_product(active_low, feed_low)
        totals[12] = totals[12] + jnp.sum(feed_low.astype(jnp.float32), 0)
        grad_active = latter_product(feed_low, back_weights[11])
        _, gelu_pull = jax.vjp(gelu_exact, hidden)
        up_low = gelu_pull(grad_active)[0].astype(jnp.bfloat16)
        totals[9] = totals[9] + former_product(normed_low, up_low)
        totals[10] = totals[10] + jnp.sum(up_low.astype(jnp.float32), 0)
        grad_normed = latter_product(up_low, back_weights[9]) + grad_two
        _, first_pull = jax.vjp(
            layer_norm, resid_one, widen(back_weights[7]), widen(back_weights[8])
        )
        grad_one, grad_gain_one, grad_shift_one = first_pull(grad_normed)
        branch_low = grad_one.astype(jnp.bfloat16)
        totals[5] = totals[5] + former_product(mixed_low, branch_low)
        totals[6] = totals[6] + jnp.sum(branch_low.astype(jnp.float32), 0)
        dmix_low = latter_product(branch_low, back_weights[5]).astype(jnp.bfloat16)
        dmix_heads = dmix_low.reshape(per_batch, block_rows, head_count, head_size)
        back_keys, backward_value_rows = (gathered_keys, gathered_values)
        chances = jnp.exp(score_block(back_keys) - logarithm_totals)
        back_value_heads = backward_value_rows.reshape(
            per_batch, full_length, head_count, head_size
        )
        back_key_heads = back_keys.reshape(per_batch, full_length, head_count, head_size)
        grad_chances = jnp.einsum(
            "pqhd,pkhd->phqk", dmix_heads, back_value_heads, preferred_element_type=jnp.float32
        )
        row_inner = jnp.sum(grad_chances * chances, -1, keepdims=True)
        dscore_low = (score_scale * (chances * (grad_chances - row_inner))).astype(jnp.bfloat16)
        dquery_low = jnp.einsum(
            "phqk,pkhd->pqhd", dscore_low, back_key_heads, preferred_element_type=jnp.float32
        )
        dquery_low = dquery_low.reshape(flat_rows, model_width).astype(jnp.bfloat16)
        chance_low = chances.astype(jnp.bfloat16)
        value_terms = jnp.einsum(
            "phqk,pqhd->pkhd", chance_low, dmix_heads, preferred_element_type=jnp.float32
        )
        key_terms = jnp.einsum(
            "phqk,pqhd->pkhd", dscore_low, query_heads, preferred_element_type=jnp.float32
        )
        key_sums, value_sums = (
            lax.psum_scatter(
                key_terms.reshape(per_batch, full_length, model_width).astype(jnp.bfloat16),
                "seq",
                scatter_dimension=1,
                tiled=True,
            ).astype(jnp.float32),
            lax.psum_scatter(
                value_terms.reshape(per_batch, full_length, model_width).astype(jnp.bfloat16),
                "seq",
                scatter_dimension=1,
                tiled=True,
            ).astype(jnp.float32),
        )
        dkey_low = key_sums.reshape(flat_rows, model_width).astype(jnp.bfloat16)
        dvalue_low = value_sums.reshape(flat_rows, model_width).astype(jnp.bfloat16)
        totals[0] = totals[0] + former_product(flat_tokens, dquery_low)
        totals[1] = totals[1] + jnp.sum(dquery_low.astype(jnp.float32), 0)
        totals[2] = totals[2] + former_product(flat_tokens, dkey_low)
        totals[3] = totals[3] + former_product(flat_tokens, dvalue_low)
        totals[4] = totals[4] + jnp.sum(dvalue_low.astype(jnp.float32), 0)
        totals[7] = totals[7] + grad_gain_one
        totals[8] = totals[8] + grad_shift_one
        totals[13] = totals[13] + grad_gain_two
        totals[14] = totals[14] + grad_shift_two
        grad_input = (
            latter_product(dquery_low, back_weights[0])
            + latter_product(dkey_low, back_weights[2])
            + latter_product(dvalue_low, back_weights[3])
            + grad_one
        )
        input_grads.append(grad_input.reshape(per_batch, block_rows, model_width))
    owned = lax.psum_scatter(tuple(totals), ("dp", "seq"), scatter_dimension=0, tiled=True)
    output = jnp.concatenate(outputs, 0)
    grad_tokens = jnp.concatenate(input_grads, 0)
    return (
        output,
        grad_tokens,
        owned[0],
        owned[1],
        owned[2],
        owned[3],
        owned[4],
        owned[5],
        owned[6],
        owned[7],
        owned[8],
        owned[9],
        owned[10],
        owned[11],
        owned[12],
        owned[13],
        owned[14],
    )


def solution(mesh):
    in_specs = (
        P("dp", "seq", None),
        P("dp"),
        P("dp", "seq", None),
        P(("dp", "seq"), None),
        P(("dp", "seq")),
        P(("dp", "seq"), None),
        P(("dp", "seq"), None),
        P(("dp", "seq")),
        P(("dp", "seq"), None),
        P(("dp", "seq")),
        P(("dp", "seq")),
        P(("dp", "seq")),
        P(("dp", "seq"), None),
        P(("dp", "seq")),
        P(("dp", "seq"), None),
        P(("dp", "seq")),
        P(("dp", "seq")),
        P(("dp", "seq")),
    )
    out_specs = (
        P("dp", "seq", None),
        P("dp", "seq", None),
        P(("dp", "seq"), None),
        P(("dp", "seq")),
        P(("dp", "seq"), None),
        P(("dp", "seq"), None),
        P(("dp", "seq")),
        P(("dp", "seq"), None),
        P(("dp", "seq")),
        P(("dp", "seq")),
        P(("dp", "seq")),
        P(("dp", "seq"), None),
        P(("dp", "seq")),
        P(("dp", "seq"), None),
        P(("dp", "seq")),
        P(("dp", "seq")),
        P(("dp", "seq")),
    )
    return jax.shard_map(body, mesh=mesh, in_specs=in_specs, out_specs=out_specs, check_vma=False)
```

profile of v0, /device:TPU:0, one launch (start us, length us, event | category | flops | bytes accessed | tf_op | source)
XLA Modules:
  0.0 2320.9 jit_solution(17265503691682136544)
XLA Ops:
  9.6 58.3 %all-gather.27.cloned.1.call-done = bf16[768,768]{1,0:T(8,128)(2,1)} async-done(((bf16[24,768]{1,0:T(8,128)(2,1)}), bf16[768,768]{1,0:T(8,128)(2,1)}) %all-gather.27.cloned.1.call-update) | async-done | bytes 1179664 | tf_op jit(solution)/shard_map/all_gather | solution.py:107
  73.3 39.7 %all-reduce.19 = (bf16[768]{0:T(1024)(128)(2,1)S(1)}, bf16[768]{0:T(1024)(128)(2,1)S(1)}, bf16[768]{0:T(1024)(128)(2,1)S(1)}, bf16[768]{0:T(1024)(128)(2,1)S(1)}...) all-reduce(bf16[768]{0:T(1024)(128)(2,1)S(1)} %dynamic-update-slice, ...), channel_id=1, replica_groups=mesh['dp'=8,'seq'=4] {'dp','seq'}, use_global_device_ids=true, to_apply=%add | all-reduce | flops 9216 | bytes 36864
  112.9 10.8 all-gather.23.cloned.1.call-done
  158.3 21.4 all-gather.25.cloned.1.call-done
  200.7 23.7 %all-gather.49.cloned.1.call-done = bf16[2048,768]{1,0:T(8,128)(2,1)} async-done(((bf16[512,768]{1,0:T(8,128)(2,1)}), bf16[2048,768]{1,0:T(8,128)(2,1)}) %all-gather.49.cloned.1.call-update) | async-done | bytes 3145744 | tf_op jit(solution)/shard_map/all_gather | solution.py:132
  224.3 4.7 copy.100
  229.1 21.4 fusion.11
  250.5 21.6 exponential_reduce_fusion
  276.8 20.5 convolution_convert_fusion.4
  297.2 30.2 %all-gather.29.cloned.1.call-done = bf16[768,768]{1,0:T(8,128)(2,1)} async-done(((bf16[24,768]{1,0:T(8,128)(2,1)}), bf16[768,768]{1,0:T(8,128)(2,1)}) %all-gather.29.cloned.1.call-update) | async-done | bytes 1179664 | tf_op jit(solution)/shard_map/all_gather | solution.py:110
  332.0 40.3 %all-gather.45.cloned.1.call-done = bf16[2048,768]{1,0:T(8,128)(2,1)} async-done(((bf16[512,768]{1,0:T(8,128)(2,1)}), bf16[2048,768]{1,0:T(8,128)(2,1)}) %all-gather.45.cloned.1.call-update) | async-done | bytes 3145744 | tf_op jit(solution)/shard_map/all_gather | solution.py:132
  377.0 22.1 fusion.10
  399.1 21.1 exponential_reduce_fusion.1
  420.3 4.8 copy.95
  425.1 20.5 convolution_convert_fusion.5
  448.0 15.9 all-gather.41.cloned.1.call-done
  468.7 21.9 fusion.9
  490.5 21.1 exponential_reduce_fusion.2
  516.5 20.5 convolution_convert_fusion.6
  539.5 16.0 all-gather.37.cloned.1.call-done
  560.2 21.9 fusion.8
  582.1 21.1 exponential_reduce_fusion.3
  608.0 19.9 convolution_convert_fusion.7
  630.2 37.5 %all-gather.31.cloned.1.call-done = bf16[768,3072]{1,0:T(8,128)(2,1)} async-done(((bf16[24,3072]{1,0:T(8,128)(2,1)}), bf16[768,3072]{1,0:T(8,128)(2,1)}) %all-gather.31.cloned.1.call-update) | async-done | bytes 4718608 | tf_op jit(solution)/shard_map/all_gather | solution.py:114
  667.7 5.7 fusion.306
  681.8 63.8 %multiply_convert_fusion.7 = (bf16[512,3072]{1,0:T(8,128)(2,1)}, f32[512,3072]{1,0:T(8,128)}, bf16[512,3072]{1,0:T(8,128)(2,1)}, f32[512,3072]{1,0:T(8,128)}, bf...) fusion(f32[3072]{0:T(1024)S(1)} %copy-done.149, ...), kind=kOutput, calls=%fused_computation.118 | convolution fusion | flops 2833121280 | bytes 69228544 | tf_op jit(solution)/shard_map/dot_general | solution.py:25
  745.7 6.2 fusion.337
  791.8 33.8 %convert_reduce_fusion.3 = (f32[3072]{0:T(1024)}, bf16[512,3072]{1,0:T(8,128)(2,1)}, f32[3072]{0:T(1024)}, bf16[512,3072]{1,0:T(8,128)(2,1)}, f32[3072]{0:T(1024...) fusion(f32[512,3072]{1,0:T(8,128)} %get-tuple-element.158, ...), kind=kOutput, calls=%fused_computation.74 | convolution fusion | flops 2522861568 | bytes 87355392 | tf_op jit(solution)/shard_map/dot_general | solution.py:35
  825.7 7.1 multiply_reduce_fusion.4
  832.8 5.1 add_add_fusion.20
  838.0 5.2 add_add_fusion.21
  843.3 7.4 multiply_reduce_fusion.7
  860.6 20.6 fusion.355
  881.2 66.1 %fusion.91 = bf16[12,64,2048]{2,1,0:T(8,128)(2,1)} fusion(bf16[512,12,64]{0,2,1:T(8,128)(2,1)} %bitcast.409, f32[12,512,2048]{2,1,0:T(8,128)} %fusion.355, f32[12,512,2048]{2,1,0:T(8,128)} %get-tuple-element.214, f32[12,512]{1,0:T(8,128)S(1)} %copy-done.93, pred[2048]{0:T(1024)(128)(4,1)S(1)} %copy-done.88), kind=kOutput, calls=%fused_computation.136 | convolution fusion | flops 1750605824 | bytes 104622080 | tf_op jit(solution)/shard_map/phqk,pqhd->pkhd/dot_general | solution.py:227
  956.1 21.4 fusion.349
  977.4 66.3 %fusion.97 = bf16[12,64,2048]{2,1,0:T(8,128)(2,1)} fusion(bf16[512,12,64]{0,2,1:T(8,128)(2,1)} %bitcast.407, f32[12,512,2048]{2,1,0:T(8,128)} %fusion.349, f32[12,512,2048]{2,1,0:T(8,128)} %get-tuple-element.206, f32[12,512]{1,0:T(8,128)S(1)} %copy-done.98, pred[2048]{0:T(1024)(128)(4,1)S(1)} %copy-done.86), kind=kOutput, calls=%fused_computation.138 | convolution fusion | flops 1750605824 | bytes 104622080 | tf_op jit(solution)/shard_map/phqk,pqhd->pkhd/dot_general | solution.py:227
  1052.4 21.5 fusion.352
  1073.9 66.3 %fusion.94 = bf16[12,64,2048]{2,1,0:T(8,128)(2,1)} fusion(bf16[512,12,64]{0,2,1:T(8,128)(2,1)} %bitcast.405, f32[12,512,2048]{2,1,0:T(8,128)} %fusion.352, f32[12,512,2048]{2,1,0:T(8,128)} %get-tuple-element.218, f32[12,512]{1,0:T(8,128)S(1)} %copy-done.96, pred[2048]{0:T(1024)(128)(4,1)S(1)} %copy-done.84), kind=kOutput, calls=%fused_computation.137 | convolution fusion | flops 1750605824 | bytes 104622080 | tf_op jit(solution)/shard_map/phqk,pqhd->pkhd/dot_general | solution.py:227
  1149.0 21.7 fusion.358
  1170.7 66.3 %fusion.88 = bf16[12,64,2048]{2,1,0:T(8,128)(2,1)} fusion(bf16[512,12,64]{0,2,1:T(8,128)(2,1)} %bitcast.403, f32[12,512,2048]{2,1,0:T(8,128)} %fusion.358, f32[12,512,2048]{2,1,0:T(8,128)} %get-tuple-element.210, f32[12,512]{1,0:T(8,128)S(1)} %copy-done.91, pred[2048]{0:T(1024)(128)(4,1)S(1)} %copy-done.82), kind=kOutput, calls=%fused_computation.135 | convolution fusion | flops 1750605824 | bytes 104622080 | tf_op jit(solution)/shard_map/phqk,pqhd->pkhd/dot_general | solution.py:227
  1238.1 22.2 convolution_convert_fusion.1
  1261.4 22.1 convolution_convert_fusion.3
  1284.7 22.2 convolution_convert_fusion.2
  1308.1 21.8 convolution_convert_fusion
  1329.9 69.2 %convert_reduce_fusion.17 = (f32[12,64]{1,0:T(8,128)}, bf16[12,64,512]{2,1,0:T(8,128)(2,1)}) fusion(bf16[2048,12,64]{0,2,1:T(8,128)(2,1)} %bitcast.389, f32[12,512,2048]{2,1,0:T(8,128)} %fusion.355, f32[12,512,2048]{2,1,0:T(8,128)} %get-tuple-element.214, f32[12,512]{1,0:T(8,128)S(1)} %copy-done.94, pred[2048]{0:T(1024)(128)(4,1)S(1)} %copy-done.89), kind=kOutput, calls=%fused_computation.205 | convolution fusion | flops 1750211840 | bytes 104625152 | tf_op jit(solution)/shard_map/phqk,pkhd->pqhd/dot_general | solution.py:219
  1402.5 67.9 %convert_reduce_fusion.19 = (f32[12,64]{1,0:T(8,128)S(1)}, bf16[12,64,512]{2,1,0:T(8,128)(2,1)}) fusion(bf16[2048,12,64]{0,2,1:T(8,128)(2,1)} %bitcast.395, f32[12,512,2048]{2,1,0:T(8,128)} %fusion.349, f32[12,512,2048]{2,1,0:T(8,128)} %get-tuple-element.206, f32[12,512]{1,0:T(8,128)S(1)} %copy-done.98, pred[2048]{0:T(1024)(128)(4,1)S(1)} %copy-done.86), kind=kOutput, calls=%fused_computation.207 | convolution fusion | flops 1750211840 | bytes 104625152 | tf_op jit(solution)/shard_map/phqk,pkhd->pqhd/dot_general | solution.py:219
  1473.8 66.4 %convert_reduce_fusion.18 = (f32[12,64]{1,0:T(8,128)S(1)}, bf16[12,64,512]{2,1,0:T(8,128)(2,1)}) fusion(bf16[2048,12,64]{0,2,1:T(8,128)(2,1)} %bitcast.391, f32[12,512,2048]{2,1,0:T(8,128)} %fusion.352, f32[12,512,2048]{2,1,0:T(8,128)} %get-tuple-element.218, f32[12,512]{1,0:T(8,128)S(1)} %copy-done.96, pred[2048]{0:T(1024)(128)(4,1)S(1)} %copy-done.84), kind=kOutput, calls=%fused_computation.206 | convolution fusion | flops 1750211840 | bytes 104625152 | tf_op jit(solution)/shard_map/phqk,pkhd->pqhd/dot_general | solution.py:219
  1543.5 66.1 %convert_reduce_fusion.16 = (f32[12,64]{1,0:T(8,128)S(1)}, bf16[12,64,512]{2,1,0:T(8,128)(2,1)}) fusion(bf16[2048,12,64]{0,2,1:T(8,128)(2,1)} %bitcast.387, f32[12,512,2048]{2,1,0:T(8,128)} %fusion.358, f32[12,512,2048]{2,1,0:T(8,128)} %get-tuple-element.210, f32[12,512]{1,0:T(8,128)S(1)} %copy-done.91, pred[2048]{0:T(1024)(128)(4,1)S(1)} %copy-done.82), kind=kOutput, calls=%fused_computation.204 | convolution fusion | flops 1750211840 | bytes 104625152 | tf_op jit(solution)/shard_map/phqk,pkhd->pqhd/dot_general | solution.py:219
  1609.6 5.5 add_bitcast_fusion.2
  1634.7 5.6 add_bitcast_fusion.1
  1653.6 5.6 add_bitcast_fusion
  1662.5 5.0 fusion.308
  1667.6 5.6 fusion.316
  1673.3 5.5 fusion.312
  1678.8 15.1 add_add_fusion.1
  1699.8 5.1 fusion.363
  1705.0 5.2 fusion.364
  1710.1 10.6 add_add_fusion
  1734.1 41.0 %all-reduce.18 = (f32[768]{0:T(1024)S(1)}, f32[768]{0:T(1024)S(1)}, f32[768]{0:T(1024)S(1)}, f32[768]{0:T(1024)S(1)}, f32[768]{0:T(1024)S(1)}, /*index=5*/f32[30...) all-reduce(f32[768]{0:T(1024)S(1)} %add.678, ...), channel_id=19, replica_groups=mesh['dp'=8,'seq'=4] {'dp','seq'}, use_global_device_ids=true, to_apply=%region_57.58.clone | all-reduce | flops 9216 | bytes 73728
  1795.8 26.2 %reduce-scatter.37.cloned.1.call-done = f32[24,768]{1,0:T(8,128)} async-done(((f32[768,768]{1,0:T(8,128)}), f32[24,768]{1,0:T(8,128)}) %reduce-scatter.37.cloned.1.call-update) | async-done | bytes 73744 | tf_op jit(solution)/shard_map/reduce_scatter | solution.py:262
  1822.0 103.9 %reduce-scatter.45.cloned.1.call-done = f32[24,768]{1,0:T(8,128)} async-done(((f32[768,768]{1,0:T(8,128)}), f32[24,768]{1,0:T(8,128)}) %reduce-scatter.45.cloned.1.call-update) | async-done | bytes 73744
  1925.9 104.6 %reduce-scatter.47.cloned.1.call-done = f32[24,768]{1,0:T(8,128)} async-done(((f32[768,768]{1,0:T(8,128)}), f32[24,768]{1,0:T(8,128)}) %reduce-scatter.47.cloned.1.call-update) | async-done | bytes 73744
  2030.5 141.0 %reduce-scatter.39.cloned.1.call-done = f32[24,3072]{1,0:T(8,128)} async-done(((f32[768,3072]{1,0:T(8,128)}), f32[24,3072]{1,0:T(8,128)}) %reduce-scatter.39.cloned.1.call-update) | async-done | bytes 294928 | tf_op jit(solution)/shard_map/reduce_scatter | solution.py:262
  2171.5 142.1 %reduce-scatter.41.cloned.1.call-done = f32[96,768]{1,0:T(8,128)} async-done(((f32[3072,768]{1,0:T(8,128)}), f32[96,768]{1,0:T(8,128)}) %reduce-scatter.41.cloned.1.call-update) | async-done | bytes 294928 | tf_op jit(solution)/shard_map/reduce_scatter | solution.py:262
  (677 shorter events, 276.3 us)
Async XLA Ops:
  7.2 116.5 %copy-start = (bf16[4,512,768]{2,1,0:T(8,128)(2,1)S(1)}, bf16[4,512,768]{2,1,0:T(8,128)(2,1)}, u32[]{:S(2)}) copy-start(bf16[4,512,768]{2,1,0:T(8,128)(2,1)} %param.18) | copy-start | bytes 9437188
  7.2 63.9 %copy-start.185 = (bf16[24]{0:T(256)(128)(2,1)S(1)}, bf16[24]{0:T(256)(128)(2,1)}, u32[]{:S(2)}) copy-start(bf16[24]{0:T(256)(128)(2,1)} %param.25) | copy-start | bytes 148
  7.2 64.2 %copy-start.186 = (bf16[24]{0:T(256)(128)(2,1)S(1)}, bf16[24]{0:T(256)(128)(2,1)}, u32[]{:S(2)}) copy-start(bf16[24]{0:T(256)(128)(2,1)} %param.22) | copy-start | bytes 148
  7.2 64.4 %copy-start.187 = (bf16[24]{0:T(256)(128)(2,1)S(1)}, bf16[24]{0:T(256)(128)(2,1)}, u32[]{:S(2)}) copy-start(bf16[24]{0:T(256)(128)(2,1)} %param.27) | copy-start | bytes 148
  7.2 64.6 %copy-start.188 = (bf16[24]{0:T(256)(128)(2,1)S(1)}, bf16[24]{0:T(256)(128)(2,1)}, u32[]{:S(2)}) copy-start(bf16[24]{0:T(256)(128)(2,1)} %param.29) | copy-start | bytes 148
  7.2 64.8 %copy-start.189 = (bf16[24]{0:T(256)(128)(2,1)S(1)}, bf16[24]{0:T(256)(128)(2,1)}, u32[]{:S(2)}) copy-start(bf16[24]{0:T(256)(128)(2,1)} %param.28) | copy-start | bytes 148
  7.3 65.1 %copy-start.190 = (bf16[24]{0:T(256)(128)(2,1)S(1)}, bf16[24]{0:T(256)(128)(2,1)}, u32[]{:S(2)}) copy-start(bf16[24]{0:T(256)(128)(2,1)} %param.33) | copy-start | bytes 148
  7.3 65.3 %copy-start.191 = (bf16[24]{0:T(256)(128)(2,1)S(1)}, bf16[24]{0:T(256)(128)(2,1)}, u32[]{:S(2)}) copy-start(bf16[24]{0:T(256)(128)(2,1)} %param.35) | copy-start | bytes 148
  7.3 65.5 %copy-start.192 = (bf16[24]{0:T(256)(128)(2,1)S(1)}, bf16[24]{0:T(256)(128)(2,1)}, u32[]{:S(2)}) copy-start(bf16[24]{0:T(256)(128)(2,1)} %param.34) | copy-start | bytes 148
  7.3 65.7 %copy-start.193 = (bf16[96]{0:T(256)(128)(2,1)S(1)}, bf16[96]{0:T(256)(128)(2,1)}, u32[]{:S(2)}) copy-start(bf16[96]{0:T(256)(128)(2,1)} %param.31) | copy-start | bytes 580
  7.3 60.5 %all-gather.27.cloned.1.call-start = ((), (), s32[]{:S(2)}) async-start(), calls=%async_computation.16 | async-start | bytes 1216512 | tf_op jit(solution)/shard_map/all_gather | solution.py:107
  8.0 115.7 %all-gather.23.cloned.1.call-start = ((), (), s32[]{:S(2)}) async-start(), calls=%async_computation.14 | async-start | bytes 1216512 | tf_op jit(solution)/shard_map/all_gather | solution.py:108
  8.8 170.9 %all-gather.25.cloned.1.call-start = ((), (), s32[]{:S(2)}) async-start(), calls=%async_computation.15 | async-start | bytes 1216512 | tf_op jit(solution)/shard_map/all_gather | solution.py:105
  9.5 214.8 %all-gather.49.cloned.1.call-start = ((), (), s32[]{:S(2)}) async-start(), calls=%async_computation.38 | async-start | bytes 3932160 | tf_op jit(solution)/shard_map/all_gather | solution.py:132
  71.1 201.0 %all-gather.47.cloned.1.call-start = ((), (), s32[]{:S(2)}) async-start(), calls=%async_computation.37 | async-start | bytes 3932160 | tf_op jit(solution)/shard_map/all_gather | solution.py:133
  126.7 200.8 %all-gather.29.cloned.1.call-start = ((), (), s32[]{:S(2)}) async-start(), calls=%async_computation.17 | async-start | bytes 1216512 | tf_op jit(solution)/shard_map/all_gather | solution.py:110
  127.3 245.0 %all-gather.45.cloned.1.call-start = ((), (), s32[]{:S(2)}) async-start(), calls=%async_computation.36 | async-start | bytes 3932160 | tf_op jit(solution)/shard_map/all_gather | solution.py:132
  130.3 290.0 %all-gather.43.cloned.1.call-start = ((), (), s32[]{:S(2)}) async-start(), calls=%async_computation.35 | async-start | bytes 3932160 | tf_op jit(solution)/shard_map/all_gather | solution.py:133
  133.3 330.7 %all-gather.41.cloned.1.call-start = ((), (), s32[]{:S(2)}) async-start(), calls=%async_computation.34 | async-start | bytes 3932160 | tf_op jit(solution)/shard_map/all_gather | solution.py:132
  136.3 375.4 %all-gather.39.cloned.1.call-start = ((), (), s32[]{:S(2)}) async-start(), calls=%async_computation.33 | async-start | bytes 3932160 | tf_op jit(solution)/shard_map/all_gather | solution.py:133
  139.4 416.1 %all-gather.37.cloned.1.call-start = ((), (), s32[]{:S(2)}) async-start(), calls=%async_computation.32 | async-start | bytes 3932160 | tf_op jit(solution)/shard_map/all_gather | solution.py:132
  142.5 460.8 %all-gather.35.cloned.1.call-start = ((), (), s32[]{:S(2)}) async-start(), calls=%async_computation.31 | async-start | bytes 3932160 | tf_op jit(solution)/shard_map/all_gather | solution.py:133
  145.5 522.2 %all-gather.31.cloned.1.call-start = ((), (), s32[]{:S(2)}) async-start(), calls=%async_computation.18 | async-start | bytes 4866048 | tf_op jit(solution)/shard_map/all_gather | solution.py:114
  146.2 599.3 %all-gather.33.cloned.1.call-start = ((), (), s32[]{:S(2)}) async-start(), calls=%async_computation.19 | async-start | bytes 4866048 | tf_op jit(solution)/shard_map/all_gather | solution.py:116
  146.8 1477.9 %reduce-scatter.29.cloned.1.call-start = ((), (), s32[]{:S(2)}) async-start(), calls=%async_computation.24 | async-start | bytes 3932160 | tf_op jit(solution)/shard_map/reduce_scatter | solution.py:231
  148.3 128.4 %copy-start.81 = (pred[2048]{0:T(1024)(128)(4,1)}, pred[2048]{0:T(1024)(128)(4,1)S(1)}, u32[]{:S(2)}) copy-start(pred[2048]{0:T(1024)(128)(4,1)S(1)} %iota_compare_fusion) | copy-start | bytes 6148
  149.0 276.1 %copy-start.87 = (pred[2048]{0:T(1024)(128)(4,1)}, pred[2048]{0:T(1024)(128)(4,1)S(1)}, u32[]{:S(2)}) copy-start(pred[2048]{0:T(1024)(128)(4,1)S(1)} %iota_compare_fusion.1) | copy-start | bytes 6148
  149.7 366.8 %copy-start.83 = (pred[2048]{0:T(1024)(128)(4,1)}, pred[2048]{0:T(1024)(128)(4,1)S(1)}, u32[]{:S(2)}) copy-start(pred[2048]{0:T(1024)(128)(4,1)S(1)} %iota_compare_fusion.2) | copy-start | bytes 6148
  329.9 47.0 %copy-start.101 = (f32[512]{0:T(512)}, f32[512]{0:T(512)S(1)}, u32[]{:S(2)}) copy-start(f32[512]{0:T(512)S(1)} %broadcast_multiply_fusion.1) | copy-start | bytes 6148
  331.4 45.6 %copy-start.116 = (f32[512]{0:T(512)}, f32[512]{0:T(512)S(1)}, u32[]{:S(2)}) copy-start(f32[512]{0:T(512)S(1)} %multiply_reduce_fusion.13) | copy-start | bytes 6148
  446.6 226.9 %copy-start.105 = (f32[512]{0:T(512)}, f32[512]{0:T(512)S(1)}, u32[]{:S(2)}) copy-start(f32[512]{0:T(512)S(1)} %broadcast_multiply_fusion.3) | copy-start | bytes 6148
  448.0 225.4 %copy-start.157 = (f32[512]{0:T(512)}, f32[512]{0:T(512)S(1)}, u32[]{:S(2)}) copy-start(f32[512]{0:T(512)S(1)} %fusion.245) | copy-start | bytes 6148
  538.0 138.3 %copy-start.108 = (f32[512]{0:T(512)}, f32[512]{0:T(512)S(1)}, u32[]{:S(2)}) copy-start(f32[512]{0:T(512)S(1)} %broadcast_multiply_fusion.5) | copy-start | bytes 6148
  539.5 136.8 %copy-start.160 = (f32[512]{0:T(512)}, f32[512]{0:T(512)S(1)}, u32[]{:S(2)}) copy-start(f32[512]{0:T(512)S(1)} %fusion.243) | copy-start | bytes 6148
  628.0 39.8 %copy-start.79 = (f32[768]{0:T(1024)S(1)}, f32[768]{0:T(1024)}, u32[]{:S(2)}) copy-start(f32[768]{0:T(1024)} %convert_element_type.686) | copy-start | bytes 9220
  628.0 39.8 %copy-start.102 = (f32[512]{0:T(512)S(1)}, f32[512]{0:T(512)}, u32[]{:S(2)}) copy-start(f32[512]{0:T(512)} %copy-done.101) | copy-start | bytes 6148
  628.0 39.7 %copy-start.147 = (f32[768]{0:T(1024)S(1)}, f32[768]{0:T(1024)}, u32[]{:S(2)}) copy-start(f32[768]{0:T(1024)} %convert_element_type.687) | copy-start | bytes 9220
  628.0 39.7 %copy-start.154 = (f32[512]{0:T(512)S(1)}, f32[512]{0:T(512)}, u32[]{:S(2)}) copy-start(f32[512]{0:T(512)} %fusion.247) | copy-start | bytes 6148
  629.0 221.8 %copy-start.111 = (f32[512]{0:T(512)}, f32[512]{0:T(512)S(1)}, u32[]{:S(2)}) copy-start(f32[512]{0:T(512)S(1)} %broadcast_multiply_fusion.7) | copy-start | bytes 6148
  630.2 43.3 %copy-start.120 = (f32[512]{0:T(512)}, f32[512]{0:T(512)S(1)}, u32[]{:S(2)}) copy-start(f32[512]{0:T(512)S(1)} %multiply_reduce_fusion.19) | copy-start | bytes 6148
  630.2 220.6 %copy-start.163 = (f32[512]{0:T(512)}, f32[512]{0:T(512)S(1)}, u32[]{:S(2)}) copy-start(f32[512]{0:T(512)S(1)} %fusion.241) | copy-start | bytes 6148
  630.2 43.3 %copy-start.24 = (f32[512,768]{1,0:T(8,128)S(1)}, f32[512,768]{1,0:T(8,128)}, u32[]{:S(2)}) copy-start(f32[512,768]{1,0:T(8,128)} %copy-done.23) | copy-start | bytes 4718596
  681.7 63.9 %copy-start.19 = (f32[512,768]{1,0:T(8,128)S(1)}, f32[512,768]{1,0:T(8,128)}, u32[]{:S(2)}) copy-start(f32[512,768]{1,0:T(8,128)} %copy-done.18) | copy-start | bytes 4718596
  681.7 63.9 %copy-start.103 = (f32[512]{0:T(512)S(1)}, f32[512]{0:T(512)}, u32[]{:S(2)}) copy-start(f32[512]{0:T(512)} %copy-done.101) | copy-start | bytes 6148
  681.7 63.9 %copy-start.155 = (f32[512]{0:T(512)S(1)}, f32[512]{0:T(512)}, u32[]{:S(2)}) copy-start(f32[512]{0:T(512)} %fusion.247) | copy-start | bytes 6148
  681.8 63.9 %copy-start.175 = (f32[768]{0:T(1024)S(1)}, f32[768]{0:T(1024)}, u32[]{:S(2)}) copy-start(f32[768]{0:T(1024)} %convert_element_type.691) | copy-start | bytes 9220
  947.4 680.7 %reduce-scatter.21.cloned.1.call-start = ((), (), s32[]{:S(2)}) async-start(), calls=%async_computation.20 | async-start | bytes 3932160 | tf_op jit(solution)/shard_map/reduce_scatter | solution.py:231
  1043.7 587.6 %reduce-scatter.25.cloned.1.call-start = ((), (), s32[]{:S(2)}) async-start(), calls=%async_computation.22 | async-start | bytes 3932160 | tf_op jit(solution)/shard_map/reduce_scatter | solution.py:231
  1052.4 21.5 copy-start.84
  1052.4 21.5 copy-start.96
  1140.2 494.5 %reduce-scatter.33.cloned.1.call-start = ((), (), s32[]{:S(2)}) async-start(), calls=%async_computation.26 | async-start | bytes 3932160 | tf_op jit(solution)/shard_map/reduce_scatter | solution.py:231
  1148.9 21.7 copy-start.82
  1148.9 21.7 copy-start.91
  1237.0 406.5 %reduce-scatter.31.cloned.1.call-start = ((), (), s32[]{:S(2)}) async-start(), calls=%async_computation.25 | async-start | bytes 3932160 | tf_op jit(solution)/shard_map/reduce_scatter | solution.py:237
  1260.3 386.5 %reduce-scatter.23.cloned.1.call-start = ((), (), s32[]{:S(2)}) async-start(), calls=%async_computation.21 | async-start | bytes 3932160 | tf_op jit(solution)/shard_map/reduce_scatter | solution.py:237
  1283.6 366.6 %reduce-scatter.27.cloned.1.call-start = ((), (), s32[]{:S(2)}) async-start(), calls=%async_computation.23 | async-start | bytes 3932160 | tf_op jit(solution)/shard_map/reduce_scatter | solution.py:237
  1307.0 346.6 %reduce-scatter.35.cloned.1.call-start = ((), (), s32[]{:S(2)}) async-start(), calls=%async_computation.27 | async-start | bytes 3932160 | tf_op jit(solution)/shard_map/reduce_scatter | solution.py:237
  1329.9 69.3 %copy-start.1 = (bf16[4,512,768]{2,1,0:T(8,128)(2,1)S(1)}, bf16[4,512,768]{2,1,0:T(8,128)(2,1)}, u32[]{:S(2)}) copy-start(bf16[4,512,768]{2,1,0:T(8,128)(2,1)} %param.18) | copy-start | bytes 9437188
  1329.9 465.9 %reduce-scatter.43.cloned.1.call-start = ((), (), s32[]{:S(2)}) async-start(), calls=%async_computation.39 | async-start | bytes 2433024
  1618.2 203.8 %reduce-scatter.37.cloned.1.call-start = ((), (), s32[]{:S(2)}) async-start(), calls=%async_computation.28 | async-start | bytes 2433024 | tf_op jit(solution)/shard_map/reduce_scatter | solution.py:262
  1624.4 301.5 %reduce-scatter.45.cloned.1.call-start = ((), (), s32[]{:S(2)}) async-start(), calls=%async_computation.40 | async-start | bytes 2433024
  1643.4 387.1 %reduce-scatter.47.cloned.1.call-start = ((), (), s32[]{:S(2)}) async-start(), calls=%async_computation.41 | async-start | bytes 2433024
  1662.4 509.1 %reduce-scatter.39.cloned.1.call-start = ((), (), s32[]{:S(2)}) async-start(), calls=%async_computation.29 | async-start | bytes 9732096 | tf_op jit(solution)/shard_map/reduce_scatter | solution.py:262
  1693.9 619.7 %reduce-scatter.41.cloned.1.call-start = ((), (), s32[]{:S(2)}) async-start(), calls=%async_computation.30 | async-start | bytes 9732096 | tf_op jit(solution)/shard_map/reduce_scatter | solution.py:262
  (172 other events, 717.4 us)
Sparse Core Ops, SparseCore 0:
  11.0 56.7 all-gather.26
  70.7 52.9 all-gather.22
  126.6 53.0 all-gather.24
  181.4 42.9 all-gather.48
  226.6 43.9 all-gather.46
  273.4 54.0 all-gather.28
  329.3 42.9 all-gather.44
  374.1 43.9 all-gather.42
  420.0 43.9 all-gather.40
  465.7 43.9 all-gather.38
  511.5 43.9 all-gather.36
  557.2 43.9 all-gather.34
  604.1 63.5 all-gather.30
  670.5 62.3 all-gather.32
  947.5 42.7 reduce-scatter.28
  1043.9 43.1 reduce-scatter.20
  1140.4 43.5 reduce-scatter.24
  1237.1 43.8 reduce-scatter.32
  1283.9 43.9 reduce-scatter.30
  1330.8 43.9 reduce-scatter.22
  1377.7 43.9 reduce-scatter.26
  1425.3 43.9 reduce-scatter.34
  1618.3 98.8 reduce-scatter.42
  1723.8 98.2 reduce-scatter.36
  1827.9 97.9 reduce-scatter.44
  1932.5 97.9 reduce-scatter.46
  2036.8 134.5 reduce-scatter.38
  2179.0 134.5 reduce-scatter.40
where the time goes:
time: 2330 us; the launch traced here: 2320 us
  matrix products  1220 us (52%)
  waiting for transfers between devices  776 us (33%)
  other arithmetic  126 us (5%)
  local copies, waits for them, and re-layouts  101 us (4%)
  blocking collectives  80.6 us (3%)
    reduce_scatter x3, waiting for transfers between devices, body(): lax.psum_scatter(tuple(totals), ('dp', 'seq'), scatter_dimension=0, tiled...  309 us
    dot_general x4, matrix products, body(): jnp.einsum('phqk,pkhd->pqhd', dscore_low, back_key_heads, preferred_eleme...  270 us
    dot_general x4, matrix products, body(): jnp.einsum('phqk,pqhd->pkhd', dscore_low, query_heads, preferred_element_...  265 us
    unnamed x31, waiting for transfers between devices  213 us
    dot_general x24, matrix products, matmul(): return jnp.dot(former, latter, preferred_element_type=jnp.float32)  130 us
    dot_general x24, matrix products, former_product(): lax.dot_general(former, latter, (((0,), (0,)), ((), ())), preferred_eleme...  110 us
    dot_general x24, matrix products, latter_product(): lax.dot_general(former, latter, (((1,), (1,)), ((), ())), preferred_eleme...  101 us
    all_gather x4, waiting for transfers between devices, body(): lax.all_gather(key_block, 'seq', axis=1, tiled=True)  95.9 us
  transfers between devices with their start and end apart: 28, of which 14 were waited for; matrix products, arithmetic and copies ran while one was open for 53% of the time, Pallas kernels for 0%

commit v1 on v0

--- a/solution.py
+++ b/solution.py
@@ -1,6 +1,10 @@
+import functools
+
 import jax
 import jax.numpy as jnp
 from jax import lax
+from jax.experimental import pallas as pl
+from jax.experimental.pallas import tpu as pltpu
 from jax.sharding import PartitionSpec as P
 
 H = 12
@@ -41,7 +45,7 @@
     return vector.astype(jnp.float32)
 
 
-def body(
+def general_body(
     tokens,
     lengths,
     cotangent,
@@ -283,6 +287,321 @@
     )
 
 
+LOG2E = 1.4426950408889634
+PAD = 16
+VMEM = 60 << 20
+CHUNK = 512
+
+
+def contract(former, latter, dim_former, dim_latter):
+    return lax.dot_general(
+        former,
+        latter,
+        (((dim_former,), (dim_latter,)), ((), ())),
+        preferred_element_type=jnp.float32,
+    )
+
+
+def mix_kernel(scale, qt, kt, vt, bias, mixed, total, probs, keys, vals):
+    size, slots = kt.shape[1], kt.shape[2]
+    key = kt[0]
+    keys[...] = jnp.concatenate([key, key, bias[...]], 0).T
+    vals[...] = jnp.concatenate([vt[0], jnp.ones((PAD, slots), jnp.bfloat16)], 0)
+    query = qt[0].astype(jnp.float32) * scale
+    high = query.astype(jnp.bfloat16)
+    low = (query - high.astype(jnp.float32)).astype(jnp.bfloat16)
+    row = lax.broadcasted_iota(jnp.int32, (PAD, slots), 0)
+    first = jnp.where(row == 0, 1.0, 0.0).astype(jnp.bfloat16)
+    columns = jnp.concatenate([high, low, first], 0)
+
+    def finish(sums):
+        weight = sums[size : size + 1]
+        mixed[0] = (sums[:size] / weight).astype(mixed.dtype)
+        total[0] = weight
+        return weight
+
+    sums, top = None, None
+    for at in range(0, slots, CHUNK):
+        scores = contract(keys[at : at + CHUNK], columns, 1, 0)
+        if top is None:
+            top = jnp.max(scores[:256], 0, keepdims=True)
+        part = jnp.exp2(scores - top).astype(jnp.bfloat16)
+        probs[0, at : at + CHUNK] = part
+        term = contract(vals[:, at : at + CHUNK], part, 1, 0)
+        sums = term if sums is None else sums + term
+    weight = finish(sums)
+
+    @pl.when(jnp.logical_not(jnp.max(weight) < 2.0**60))
+    def _():
+        top = jnp.full((1, slots), -jnp.inf, jnp.float32)
+        for at in range(0, slots, CHUNK):
+            scores = contract(keys[at : at + CHUNK], columns, 1, 0)
+            top = jnp.maximum(top, jnp.max(scores, 0, keepdims=True))
+        sums = None
+        for at in range(0, slots, CHUNK):
+            scores = contract(keys[at : at + CHUNK], columns, 1, 0)
+            part = jnp.exp2(scores - top).astype(jnp.bfloat16)
+            probs[0, at : at + CHUNK] = part
+            term = contract(vals[:, at : at + CHUNK], part, 1, 0)
+            sums = term if sums is None else sums + term
+        finish(sums)
+
+
+def mix(qt, kt, vt, bias, scale):
+    heads, size, slots = qt.shape
+    whole = pl.BlockSpec((1, size, slots), lambda i: (i, 0, 0))
+    return pl.pallas_call(
+        functools.partial(mix_kernel, scale),
+        grid=(heads,),
+        in_specs=[whole, whole, whole, pl.BlockSpec((PAD, slots), lambda i: (0, 0))],
+        out_specs=[
+            whole,
+            pl.BlockSpec((1, 1, slots), lambda i: (i, 0, 0)),
+            pl.BlockSpec((1, slots, slots), lambda i: (i, 0, 0)),
+        ],
+        out_shape=[
+            jax.ShapeDtypeStruct((heads, size, slots), jnp.bfloat16),
+            jax.ShapeDtypeStruct((heads, 1, slots), jnp.float32),
+            jax.ShapeDtypeStruct((heads, slots, slots), jnp.bfloat16),
+        ],
+        scratch_shapes=[
+            pltpu.VMEM((slots, 2 * size + PAD), jnp.bfloat16),
+            pltpu.VMEM((size + PAD, slots), jnp.bfloat16),
+        ],
+        compiler_params=pltpu.CompilerParams(vmem_limit_bytes=VMEM),
+        name="mix",
+    )(qt, kt, vt, bias)
+
+
+def unmix_kernel(scale, probs, qt, kt, vt, gt, mt, total, dq, dk, dv, grads, inner, sums):
+    step, last = pl.program_id(1), pl.num_programs(1) - 1
+
+    @pl.when(step == 0)
+    def _():
+        scaled = (gt[0].astype(jnp.float32) / total[0]).astype(jnp.bfloat16)
+        grads[...] = scaled
+        inner[...] = jnp.sum(
+            scaled.astype(jnp.float32) * mt[0].astype(jnp.float32), 0, keepdims=True
+        )
+
+    grad = grads[...]
+    prob = probs[0]
+    dprob = contract(vt[0], grad, 0, 0)
+    dscore = (prob.astype(jnp.float32) * (dprob - inner[...])).astype(jnp.bfloat16)
+    part = contract(kt[0], dscore, 1, 0)
+    dv[0] = contract(prob, grad, 1, 1).T.astype(jnp.bfloat16)
+    dk[0] = (contract(dscore, qt[0], 1, 1) * scale).T.astype(jnp.bfloat16)
+
+    @pl.when(step == 0)
+    def _():
+        sums[...] = part
+
+    @pl.when(step > 0)
+    def _():
+        sums[...] += part
+
+    @pl.when(step == last)
+    def _():
+        dq[0] = (sums[...] * scale).astype(jnp.bfloat16)
+
+
+def unmix(probs, qt, kt, vt, gt, mt, total, scale):
+    heads, size, slots = qt.shape
+    keys = slots // 2
+    whole = pl.BlockSpec((1, size, slots), lambda i, j: (i, 0, 0))
+    part = pl.BlockSpec((1, size, keys), lambda i, j: (i, 0, j))
+    return pl.pallas_call(
+        functools.partial(unmix_kernel, scale),
+        grid=(heads, slots // keys),
+        in_specs=[
+            pl.BlockSpec((1, keys, slots), lambda i, j: (i, j, 0)),
+            whole,
+            part,
+            part,
+            whole,
+            whole,
+            pl.BlockSpec((1, 1, slots), lambda i, j: (i, 0, 0)),
+        ],
+        out_specs=[whole, part, part],
+        out_shape=[jax.ShapeDtypeStruct((heads, size, slots), jnp.bfloat16)] * 3,
+        scratch_shapes=[
+            pltpu.VMEM((size, slots), jnp.bfloat16),
+            pltpu.VMEM((1, slots), jnp.float32),
+            pltpu.VMEM((size, slots), jnp.float32),
+        ],
+        compiler_params=pltpu.CompilerParams(vmem_limit_bytes=VMEM),
+        name="unmix",
+    )(probs, qt, kt, vt, gt, mt, total)
+
+
+def swap(piece, step):
+    size = lax.axis_size("seq")
+    return lax.ppermute(piece, "seq", [(i, i ^ step) for i in range(size)])
+
+
+def take(array, index):
+    return lax.dynamic_index_in_dim(array, index, 0, keepdims=False)
+
+
+def to_own(array):
+    me = lax.axis_index("seq")
+    pieces = [take(array, me)]
+    pieces += [swap(take(array, me ^ step), step) for step in range(1, lax.axis_size("seq"))]
+    return jnp.concatenate(pieces, 0)
+
+
+def to_split(rows, own, blank):
+    me = lax.axis_index("seq")
+    size = lax.axis_size("seq")
+    block = rows.shape[0] // size
+    result = lax.dynamic_update_index_in_dim(blank, own.astype(blank.dtype), me, 0)
+    for step in range(1, size):
+        came = swap(rows[step * block : (step + 1) * block], step)
+        result = lax.dynamic_update_index_in_dim(result, came.astype(blank.dtype), me ^ step, 0)
+    return result
+
+
+def whole_body(
+    tokens,
+    lengths,
+    cotangent,
+    w_query,
+    b_query,
+    w_key,
+    w_value,
+    b_value,
+    w_out,
+    b_out,
+    gain_one,
+    shift_one,
+    w_up,
+    b_up,
+    w_down,
+    b_down,
+    gain_two,
+    shift_two,
+):
+    count, block, width = tokens.shape
+    slots = count * block
+    wide = w_up.shape[1]
+    rows = w_query.shape[0]
+    axes = ("dp", "seq")
+    me = lax.axis_index("seq")
+    heads, size = H, HD
+    scale = size ** (-0.5)
+    times = wide // width
+
+    vectors = [b_query, b_value, b_out, gain_one, shift_one, b_down, gain_two, shift_two]
+    columns = [v.reshape(rows, 1) for v in vectors] + [b_up.reshape(rows, times)]
+    columns = jnp.concatenate(columns, 1)
+    columns = jnp.pad(columns, ((0, 0), (0, 128 - columns.shape[1])))
+    first = jnp.concatenate([w_query, w_key, w_value, w_out, columns], 1)
+    first = lax.all_gather(first, axes, axis=0, tiled=True)
+    second = jnp.concatenate([w_up, w_down.reshape(rows, wide)], 1)
+    second = lax.all_gather(second, axes, axis=0, tiled=True)
+
+    x = to_own(tokens)
+    cot = to_own(cotangent)
+    length = take(lengths, me)
+    order = me ^ jnp.arange(count, dtype=jnp.int32)
+    place = (order[:, None] * block + jnp.arange(block, dtype=jnp.int32)[None, :]).reshape(slots)
+    live = place < length
+    bias = jnp.where(live, 0.0, -1e30).astype(jnp.bfloat16)
+    bias = jnp.pad(bias[None, :], ((0, PAD - 1), (0, 0)))
+
+    wq, wk, wv, wo = (first[:, i * width : (i + 1) * width] for i in range(4))
+    vec = first[:, 4 * width :].astype(jnp.float32).T
+    bq, bv, bo, g1, s1, bd, g2, s2 = (vec[i] for i in range(8))
+    bu = vec[8 : 8 + times].T.reshape(wide)
+    wu = second[:, :wide]
+    wd = second[:, wide:].reshape(wide, width)
+
+    def columns_of(weight):
+        return contract(weight, x, 0, 1)
+
+    def by_head(array):
+        return array.astype(jnp.bfloat16).reshape(heads, size, slots)
+
+    qt = by_head(columns_of(wq) + bq[:, None])
+    kt = by_head(columns_of(wk))
+    vt = by_head(columns_of(wv) + bv[:, None])
+    mt, total, probs = mix(qt, kt, vt, bias, scale * LOG2E)
+    mixed = mt.reshape(width, slots)
+    resid_one = x.astype(jnp.float32) + contract(mixed, wo, 0, 0) + bo
+    normed = layer_norm(resid_one, g1, s1)
+    normed_low = normed.astype(jnp.bfloat16)
+    hidden = matmul(normed_low, wu) + bu
+    active_low = gelu_exact(hidden).astype(jnp.bfloat16)
+    resid_two = normed + matmul(active_low, wd) + bd
+    result = layer_norm(resid_two, g2, s2).astype(jnp.bfloat16)
+    output = to_split(result, result[:block], jnp.zeros((count, block, width), jnp.bfloat16))
+
+    incoming = cot.astype(jnp.float32) * live[:, None].astype(jnp.float32)
+    _, second_pull = jax.vjp(layer_norm, resid_two, g2, s2)
+    grad_two, d_g2, d_s2 = second_pull(incoming)
+    feed_low = grad_two.astype(jnp.bfloat16)
+    d_wd = former_product(active_low, feed_low)
+    d_bd = jnp.sum(feed_low.astype(jnp.float32), 0)
+    _, gelu_pull = jax.vjp(gelu_exact, hidden)
+    up_low = gelu_pull(latter_product(feed_low, wd))[0].astype(jnp.bfloat16)
+    d_wu = former_product(normed_low, up_low)
+    d_bu = jnp.sum(up_low.astype(jnp.float32), 0)
+    late = jnp.concatenate([d_wu, d_wd.reshape(width, wide)], 1).astype(jnp.bfloat16)
+    late = lax.psum_scatter(late, axes, scatter_dimension=0, tiled=True).astype(jnp.float32)
+    grad_normed = latter_product(up_low, wu) + grad_two
+    _, first_pull = jax.vjp(layer_norm, resid_one, g1, s1)
+    grad_one, d_g1, d_s1 = first_pull(grad_normed)
+    branch_low = grad_one.astype(jnp.bfloat16)
+    d_wo = matmul(mixed, branch_low)
+    d_bo = jnp.sum(branch_low.astype(jnp.float32), 0)
+    gt = by_head(latter_product(wo, branch_low))
+    dq, dk, dv = unmix(probs, qt, kt, vt, gt, mt, total, scale)
+    dq, dk, dv = (g.reshape(width, slots) for g in (dq, dk, dv))
+    d_wq, d_wk, d_wv = (contract(x, g, 0, 1) for g in (dq, dk, dv))
+    d_bq, d_bv = (jnp.sum(g.astype(jnp.float32), 1) for g in (dq, dv))
+    grad_x = contract(dq, wq, 0, 1) + contract(dk, wk, 0, 1) + contract(dv, wv, 0, 1) + grad_one
+    grad_tokens = to_split(
+        grad_x.astype(jnp.bfloat16), grad_x[:block], jnp.zeros((count, block, width), jnp.float32)
+    )
+
+    columns = jnp.stack([d_bq, d_bv, d_bo, d_g1, d_s1, d_bd, d_g2, d_s2], 1)
+    columns = jnp.concatenate([columns, d_bu.reshape(width, times)], 1)
+    columns = jnp.pad(columns, ((0, 0), (0, 128 - columns.shape[1])))
+    early = jnp.concatenate([d_wq, d_wk, d_wv, d_wo, columns], 1).astype(jnp.bfloat16)
+    early = lax.psum_scatter(early, axes, scatter_dimension=0, tiled=True).astype(jnp.float32)
+    o_wq, o_wk, o_wv, o_wo = (early[:, i * width : (i + 1) * width] for i in range(4))
+    vec = early[:, 4 * width :]
+    o_bq, o_bv, o_bo, o_g1, o_s1, o_bd, o_g2, o_s2 = (vec[:, i] for i in range(8))
+    o_bu = vec[:, 8 : 8 + times].reshape(rows * times)
+    o_wu = late[:, :wide]
+    o_wd = late[:, wide:].reshape(rows * times, width)
+    return (
+        output,
+        grad_tokens,
+        o_wq,
+        o_bq,
+        o_wk,
+        o_wv,
+        o_bv,
+        o_wo,
+        o_bo,
+        o_g1,
+        o_s1,
+        o_wu,
+        o_bu,
+        o_wd,
+        o_bd,
+        o_g2,
+        o_s2,
+    )
+
+
+def body(*arrays):
+    count = arrays[0].shape[0]
+    fits = count == lax.axis_size("seq") and count & (count - 1) == 0
+    return whole_body(*arrays) if fits else general_body(*arrays)
+
+
 def solution(mesh):
     in_specs = (
         P("dp", "seq", None),

time: 2330 us -> 939 us (0.40)
  matrix products: 1220 us -> 238 us
  waiting for transfers between devices: 776 us -> 351 us
  Pallas kernels: 0 us -> 167 us
  other arithmetic: 126 us -> 45.1 us
  blocking collectives: 80.6 us -> 0 us
    dot_general x24 -> x10, matrix products: 877 us -> 62.6 us  [contract(): lax.dot_general(former, latter, (((dim_former,), (dim_latter,)), ((), ())...]
    all_gather x14 -> x2, waiting for transfers between devices: 254 us -> 51.5 us  [the longest x1 49.3 us: whole_body(): first = lax.all_gather(first, axes, axis=0, tiled=True)]
    reduce_scatter x11 -> x1, waiting for transfers between devices: 309 us -> 134 us  [whole_body(): lax.psum_scatter(late, axes, scatter_dimension=0, tiled=True)]
    pallas_call x0 -> x2, Pallas kernels: none -> 167 us  [the longest x1 110 us: unmix(): pl.pallas_call(functools.partial(unmix_kernel, scale), grid=(heads, slots...]
    unnamed x31 -> x5, waiting for transfers between devices: 213 us -> 106 us
    reduce_sum x16 -> x4, other arithmetic: 93.1 us -> 6.19 us  [the longest x2 4.94 us: whole_body(): d_bq, d_bv = (jnp.sum(g.astype(jnp.float32), 1) for g in (dq, dv))]
    unnamed x2 -> x0, blocking collectives: 80.6 us -> none
    dot_general x24 -> x2, matrix products: 110 us -> 32.1 us  [former_product(): lax.dot_general(former, latter, (((0,), (0,)), ((), ())), preferred_eleme...]
  transfers between devices with their start and end apart: 28 -> 16, of which waited for: 14 -> 8; matrix products, arithmetic and copies ran while one was open for 53% -> 27% of each run, Pallas kernels for 0% -> 6%
where the time goes in v1:
time: 939 us; the launch traced here: 936 us
  waiting for transfers between devices  351 us (37%)
  matrix products  238 us (25%)
  Pallas kernels  167 us (18%)
  local copies, waits for them, and re-layouts  105 us (11%)
  other arithmetic  45.1 us (5%)
  starting transfers between devices  15.9 us (2%)
  between operations  14.9 us (2%)
    reduce_scatter x1, waiting for transfers between devices, whole_body(): lax.psum_scatter(late, axes, scatter_dimension=0, tiled=True)  134 us
    pallas_call x1, Pallas kernels, unmix(): pl.pallas_call(functools.partial(unmix_kernel, scale), grid=(heads, slots...  110 us
    unnamed x5, waiting for transfers between devices  106 us
    dot_general x3, matrix products, matmul(): return jnp.dot(former, latter, preferred_element_type=jnp.float32)  86.7 us
    dot_general x10, matrix products, contract(): lax.dot_general(former, latter, (((dim_former,), (dim_latter,)), ((), ())...  62.6 us
    ppermute x12, waiting for transfers between devices, swap(): return lax.ppermute(piece, 'seq', [(i, i ^ step) for i in range(size)])  59.5 us
    pallas_call x1, Pallas kernels, mix(): pl.pallas_call(functools.partial(mix_kernel, scale), grid=(heads,), in_sp...  56.6 us
    dot_general x3, matrix products, latter_product(): lax.dot_general(former, latter, (((1,), (1,)), ((), ())), preferred_eleme...  56.6 us
  transfers between devices with their start and end apart: 16, of which 8 were waited for; matrix products, arithmetic and copies ran while one was open for 27% of the time, Pallas kernels for 6%

profile of v1, /device:TPU:0, one launch (start us, length us, event | category | flops | bytes accessed | tf_op | source)
XLA Modules:
  0.0 936.1 jit_solution(10684194450765477730)
XLA Ops:
  18.9 1.6 pad_maximum_fusion.3
  20.7 4.7 constant_dynamic-slice_fusion.3
  25.3 2.3 copy.103
  27.7 2.9 collective-permute-start
  30.6 2.3 copy.104
  34.4 2.3 copy.105
  36.7 2.3 copy.119
  39.0 2.0 collective-permute-start.6
  42.2 1.5 collective-permute-start.7
  49.7 49.3 %all-gather.3.cloned.1.call-done = bf16[768,3200]{1,0:T(8,128)(2,1)} async-done(((bf16[24,3200]{1,0:T(8,128)(2,1)}), bf16[768,3200]{1,0:T(8,128)(2,1)}) %all-gather.3.cloned.1.call-update) | async-done | bytes 4915216 | tf_op jit(solution)/shard_map/all_gather | solution.py:499
  100.3 2.1 slice_reduce_fusion.1
  103.3 6.3 convolution_convert_fusion.3
  109.6 6.3 add_convert_fusion.2
  116.0 6.5 add_convert_fusion.3
  122.5 56.6 %mix.1 = (bf16[12,64,2048]{2,1,0:T(8,128)(2,1)}, f32[12,1,2048]{2,1,0:T(1,128)}, bf16[12,2048,2048]{2,1,0:T(8,128)(2,1)}) custom-call(bf16[12,64,2048]{2,1,0:T(8,128)(2,1)} %bitcast.99, bf16[12,64,2048]{2,1,0:T(8,128)(2,1)} %bitcast.95, bf16[12,64,2048]{2,1,0:T(8,128)(2,1)} %bitcast.97, bf16[16,2048]{1,0:T(8,128)(2,1)} %pad.14.bias), custom_call_target="tpu_custom_call" | custom-call | tf_op jit(solution)/shard_map/mix/pallas_call | solution.py:353
  179.1 6.2 fusion.46
  189.1 2.2 all-gather.5.cloned.1.call-done
  191.3 4.8 slice.178
  196.1 8.5 reshape.249
  204.5 65.0 %multiply_convert_fusion = (bf16[2048,3072]{1,0:T(8,128)(2,1)}, f32[2048,3072]{1,0:T(8,128)}, f32[2048,3072]{1,0:T(8,128)}) fusion(f32[3072]{0:T(1024)S(1)} %add.197, bf16[768,6144]{1,0:T(8,128)(2,1)} %all-gather.5.cloned.1.call-done, bf16[2048,768]{0,1:T(8,128)(2,1)S(1)} %fusion.36.clone.5), kind=kOutput, calls=%fused_computation.3 | convolution fusion | flops 10078912512 | bytes 70791168 | tf_op jit(solution)/shard_map/dot_general | solution.py:29
  269.6 18.0 %fusion.47 = (f32[2048]{0:T(1024)S(1)}, f32[2048,768]{0,1:T(8,128)}) fusion(f32[768]{0:T(1024)S(1)} %copy-done.35, bf16[2048,3072]{1,0:T(8,128)(2,1)} %get-tuple-element.102, bf16[3072,768]{1,0:T(8,128)(2,1)} %reshape.249, f32[768]{0:T(1024)S(1)} %copy-done.31, f32[768]{0:T(1024)S(1)} %copy-done.28, f32[2048]{0:T(1024)S(1)} %copy-done.26, ...), kind=kOutput, calls=%fused_computation.140 | convolution fusion | flops 9674684416 | bytes 29918208 | tf_op jit(solution)/shard_map/dot_general | solution.py:29
  287.6 3.6 multiply_reduce_fusion.4
  292.2 4.9 multiply_reduce_fusion
  297.1 5.9 fusion.40
  303.0 2.6 copy-done.3
  306.2 28.7 %fusion.49 = (bf16[3072]{0:T(1024)(128)(2,1)S(1)}, bf16[2048,3072]{1,0:T(8,128)(2,1)}) fusion(f32[2048,3072]{1,0:T(8,128)} %get-tuple-element.103, bf16[2048,768]{0,1:T(8,128)(2,1)S(1)} %get-tuple-element.95, bf16[3072,768]{1,0:T(8,128)(2,1)} %reshape.249, f32[2048,3072]{1,0:T(8,128)} %get-tuple-element.136, f32[3072]{0:T(1024)S(1)} %add.197), kind=kOutput, calls=%fused_computation.142 | convolution fusion | flops 9764336640 | bytes 70797312 | tf_op jit(solution)/shard_map/dot_general | solution.py:39
  334.9 16.4 %convolution_convert_fusion.1 = bf16[768,3072]{1,0:T(8,128)(2,1)} fusion(bf16[2048,3072]{1,0:T(8,128)(2,1)} %get-tuple-element.143, f32[2048,768]{0,1:T(8,128)} %copy-done.1, f32[768]{0:T(1024)S(1)} %copy-done.31, f32[768]{0:T(1024)S(1)} %copy-done.28, f32[2048]{0:T(1024)S(1)} %copy-done.26, f32[2048]{0:T(1024)S(1)} %copy-done.21), kind=kOutput, calls=%fused_computation.41 | convolution fusion | flops 9673900032 | bytes 23615488 | tf_op jit(solution)/shard_map/dot_general | solution.py:33
  351.3 21.7 %multiply_reduce_fusion.1 = (bf16[768]{0:T(1024)(128)(2,1)S(1)}, f32[2048]{0:T(1024)S(1)}, bf16[768]{0:T(1024)(128)(2,1)S(1)}, f32[2048,768]{0,1:T(8,128)}) fusion(f32[2048,768]{0,1:T(8,128)} %copy-done.1, f32[2048]{0:T(1024)S(1)} %copy-done.26, f32[2048]{0:T(1024)S(1)} %copy-done.21, f32[768]{0:T(1024)S(1)} %copy-done.28, f32[2048,768]{0,1:T(8,128)} %copy-done.3, ...), kind=kOutput, calls=%fused_computation.21 | convolution fusion | flops 9679400960 | bytes 36214784 | tf_op jit(solution)/shard_map/dot_general | solution.py:39
  373.1 3.9 fusion.39
  377.6 6.2 convolution_convert_fusion.2
  383.8 110.0 %unmix.1 = (bf16[12,64,2048]{2,1,0:T(8,128)(2,1)}, bf16[12,64,2048]{2,1,0:T(8,128)(2,1)}, bf16[12,64,2048]{2,1,0:T(8,128)(2,1)}) custom-call(bf16[12,2048,2048]{2,1,0:T(8,128)(2,1)} %get-tuple-element.24.probs, bf16[12,64,2048]{2,1,0:T(8,128)(2,1)} %bitcast.100, bf16[12,64,2048]{2,1,0:T(8,128)(2,1)} %bitcast.96, bf16[12,64,2048]{2,1,0:T(8,128)(2,1)} %bitcast.98, ...), custom_call_target="tpu_custom_call" | custom-call | tf_op jit(solution)/shard_map/unmix/pallas_call | solution.py:413
  493.9 2.5 reduce.2
  496.5 2.4 reduce.3
  499.7 5.7 fusion.18
  505.3 5.4 fusion.17
  510.8 5.5 fusion.16
  516.3 3.7 fusion.15
  520.8 15.7 %convolution_convert_fusion = bf16[3072,768]{1,0:T(8,128)(2,1)} fusion(bf16[2048,3072]{1,0:T(8,128)(2,1)} %get-tuple-element.102, bf16[2048,768]{0,1:T(8,128)(2,1)} %copy-done.13), kind=kOutput, calls=%fused_computation.40 | convolution fusion | flops 9666035712 | bytes 20447232 | tf_op jit(solution)/shard_map/dot_general | solution.py:33
  536.4 8.5 reshape.255
  544.9 9.1 pad_maximum_fusion
  554.0 7.7 fusion.26
  561.7 5.9 fusion.29
  567.6 7.1 fusion.48
  578.9 3.0 copy.126
  582.5 1.5 collective-permute-start.11
  584.0 1.7 fusion.43
  585.8 1.5 copy.114
  589.6 3.6 broadcast_in_dim.80
  594.4 2.5 collective-permute-done.9
  600.1 24.8 %collective-permute-done.10 = bf16[512,768]{0,1:T(8,128)(2,1)} collective-permute-done((bf16[512,768]{0,1:T(8,128)(2,1)}, bf16[512,768]{0,1:T(8,128)(2,1)}, u32[]{:S(2)}, u32[]{:S(2)}) %collective-permute-start.10) | collective-permute-done | bytes 786464 | tf_op jit(solution)/shard_map/ppermute | solution.py:439
  626.3 1.6 copy.128
  629.2 1.7 copy.129
  630.9 9.7 %collective-permute-done.3 = bf16[512,768]{0,1:T(8,128)(2,1)} collective-permute-done((bf16[512,768]{0,1:T(8,128)(2,1)}, bf16[512,768]{0,1:T(8,128)(2,1)}, u32[]{:S(2)}, u32[]{:S(2)}) %collective-permute-start.3) | collective-permute-done | bytes 786464 | tf_op jit(solution)/shard_map/ppermute | solution.py:439
  640.6 2.5 copy.115
  643.1 22.5 %collective-permute-done.4 = bf16[512,768]{0,1:T(8,128)(2,1)} collective-permute-done((bf16[512,768]{0,1:T(8,128)(2,1)}, bf16[512,768]{0,1:T(8,128)(2,1)}, u32[]{:S(2)}, u32[]{:S(2)}) %collective-permute-start.4) | collective-permute-done | bytes 786464 | tf_op jit(solution)/shard_map/ppermute | solution.py:439
  665.6 2.3 copy.116
  667.9 2.4 copy.117
  670.3 2.2 constant_dynamic-update-slice_fusion.11
  672.4 2.1 constant_dynamic-update-slice_fusion.10
  674.5 2.1 constant_dynamic-update-slice_fusion.9
  680.3 105.6 %all-reduce.6.cloned.1.call-done = bf16[768,3200]{0,1:T(8,128)(2,1)} async-done(((bf16[768,3200]{0,1:T(8,128)(2,1)}), bf16[768,3200]{0,1:T(8,128)(2,1)}) %all-reduce.6.cloned.1.call-update) | async-done | bytes 4915216
  786.0 1.7 dynamic-slice_convert_fusion
  792.1 134.4 %reduce-scatter.3.cloned.1.call-done = bf16[24,6144]{1,0:T(8,128)(2,1)} async-done(((bf16[768,6144]{1,0:T(8,128)(2,1)}), bf16[24,6144]{1,0:T(8,128)(2,1)}) %reduce-scatter.3.cloned.1.call-update) | async-done | bytes 294928 | tf_op jit(solution)/shard_map/reduce_scatter | solution.py:550
  926.6 1.7 fusion.45
  (185 shorter events, 53.4 us)
Async XLA Ops:
  7.2 91.8 %all-gather.3.cloned.1.call-start = ((), (), s32[]{:S(2)}) async-start(), calls=%async_computation.1 | async-start | bytes 5068800 | tf_op jit(solution)/shard_map/all_gather | solution.py:499
  17.2 0.7 copy-start.19
  17.9 173.4 %all-gather.5.cloned.1.call-start = ((), (), s32[]{:S(2)}) async-start(), calls=%async_computation.2 | async-start | bytes 9732096 | tf_op jit(solution)/shard_map/all_gather | solution.py:501
  20.6 765.3 %all-reduce.6.cloned.1.call-start = ((), (), s32[]{:S(2)}) async-start(), calls=%async_computation.4 | async-start | bytes 9830400
  25.3 18.6 %copy-start.37 = (s32[4]{0:T(128)S(1)}, s32[4]{0:T(128)}, u32[]{:S(2)}) copy-start(s32[4]{0:T(128)} %param.19) | copy-start | bytes 52
  27.7 74.8 %collective-permute-start = (bf16[512,768]{0,1:T(8,128)(2,1)}, bf16[512,768]{0,1:T(8,128)(2,1)}, u32[]{:S(2)}, u32[]{:S(2)}) collective-permute-start(bf16[512,768]{0,1:T(8,128)(2,1)} %bitcast.118), channel_id=1, source_target_pairs={{0,1},{1,0},{2,3},{3,2},{4,5},{5,4},{6,7},{7,6},{8,9},{9,8},{10,11... | collective-permute-start | bytes 2359304 | tf_op jit(solution)/shard_map/ppermute | solution.py:439
  32.9 70.4 %collective-permute-start.1 = (bf16[512,768]{0,1:T(8,128)(2,1)}, bf16[512,768]{0,1:T(8,128)(2,1)}, u32[]{:S(2)}, u32[]{:S(2)}) collective-permute-start(bf16[512,768]{0,1:T(8,128)(2,1)} %bitcast.117), channel_id=1, source_target_pairs={{0,2},{1,3},{2,0},{3,1},{4,6},{5,7},{6,4},{7,5},{8,10},{9,11},{10,... | collective-permute-start | bytes 2359304 | tf_op jit(solution)/shard_map/ppermute | solution.py:439
  36.7 66.6 %collective-permute-start.2 = (bf16[512,768]{0,1:T(8,128)(2,1)}, bf16[512,768]{0,1:T(8,128)(2,1)}, u32[]{:S(2)}, u32[]{:S(2)}) collective-permute-start(bf16[512,768]{0,1:T(8,128)(2,1)} %bitcast.119), channel_id=1, source_target_pairs={{0,3},{1,2},{2,1},{3,0},{4,7},{5,6},{6,5},{7,4},{8,11},{9,10},{10,... | collective-permute-start | bytes 2359304 | tf_op jit(solution)/shard_map/ppermute | solution.py:439
  39.0 252.2 %collective-permute-start.6 = (bf16[512,768]{0,1:T(8,128)(2,1)}, bf16[512,768]{0,1:T(8,128)(2,1)}, u32[]{:S(2)}, u32[]{:S(2)}) collective-permute-start(bf16[512,768]{0,1:T(8,128)(2,1)} %bitcast.115), channel_id=1, source_target_pairs={{0,1},{1,0},{2,3},{3,2},{4,5},{5,4},{6,7},{7,6},{8,9},{9,8},{10,11... | collective-permute-start | bytes 2359304 | tf_op jit(solution)/shard_map/ppermute | solution.py:439
  42.2 249.1 %collective-permute-start.7 = (bf16[512,768]{0,1:T(8,128)(2,1)}, bf16[512,768]{0,1:T(8,128)(2,1)}, u32[]{:S(2)}, u32[]{:S(2)}) collective-permute-start(bf16[512,768]{0,1:T(8,128)(2,1)} %bitcast.116), channel_id=1, source_target_pairs={{0,2},{1,3},{2,0},{3,1},{4,6},{5,7},{6,4},{7,5},{8,10},{9,11},{10,... | collective-permute-start | bytes 2359304 | tf_op jit(solution)/shard_map/ppermute | solution.py:439
  44.0 135.1 %copy-start.17 = (bf16[1,512,768]{1,2,0:T(8,128)(2,1)}, bf16[1,512,768]{1,2,0:T(8,128)(2,1)S(1)}, u32[]{:S(2)}) copy-start(bf16[1,512,768]{1,2,0:T(8,128)(2,1)S(1)} %copy.102) | copy-start | bytes 2359300
  102.4 84.8 %copy-start.27 = (f32[768]{0:T(1024)}, f32[768]{0:T(1024)S(1)}, u32[]{:S(2)}) copy-start(f32[768]{0:T(1024)S(1)} %get-tuple-element.90) | copy-start | bytes 9220
  102.4 84.8 %copy-start.30 = (f32[768]{0:T(1024)}, f32[768]{0:T(1024)S(1)}, u32[]{:S(2)}) copy-start(f32[768]{0:T(1024)S(1)} %get-tuple-element.89) | copy-start | bytes 9220
  102.5 188.8 %collective-permute-start.8 = (bf16[512,768]{0,1:T(8,128)(2,1)}, bf16[512,768]{0,1:T(8,128)(2,1)}, u32[]{:S(2)}, u32[]{:S(2)}) collective-permute-start(bf16[512,768]{0,1:T(8,128)(2,1)} %bitcast.26), channel_id=1, source_target_pairs={{0,3},{1,2},{2,1},{3,0},{4,7},{5,6},{6,5},{7,4},{8,11},{9,10},{10,... | collective-permute-start | bytes 2359304 | tf_op jit(solution)/shard_map/ppermute | solution.py:439
  185.4 2.7 copy-start.1
  185.4 2.7 copy-start.20
  186.1 1.1 copy-start.22
  186.1 2.0 copy-start.25
  204.5 65.0 %copy-start.21 = (f32[2048]{0:T(1024)S(1)}, f32[2048]{0:T(1024)}, u32[]{:S(2)}) copy-start(f32[2048]{0:T(1024)} %copy-done.20) | copy-start | bytes 24580
  204.5 65.0 %copy-start.26 = (f32[2048]{0:T(1024)S(1)}, f32[2048]{0:T(1024)}, u32[]{:S(2)}) copy-start(f32[2048]{0:T(1024)} %copy-done.25) | copy-start | bytes 24580
  204.5 65.0 %copy-start.28 = (f32[768]{0:T(1024)S(1)}, f32[768]{0:T(1024)}, u32[]{:S(2)}) copy-start(f32[768]{0:T(1024)} %copy-done.27) | copy-start | bytes 9220
  204.5 65.0 %copy-start.31 = (f32[768]{0:T(1024)S(1)}, f32[768]{0:T(1024)}, u32[]{:S(2)}) copy-start(f32[768]{0:T(1024)} %copy-done.30) | copy-start | bytes 9220
  204.5 65.0 %copy-start.35 = (f32[768]{0:T(1024)S(1)}, f32[768]{0:T(1024)}, u32[]{:S(2)}) copy-start(f32[768]{0:T(1024)} %get-tuple-element.88) | copy-start | bytes 9220
  269.6 21.7 %copy-start.6 = (bf16[1,512,768]{1,2,0:T(8,128)(2,1)S(1)}, bf16[1,512,768]{1,2,0:T(8,128)(2,1)}, u32[]{:S(2)}) copy-start(bf16[1,512,768]{1,2,0:T(8,128)(2,1)} %copy.118) | copy-start | bytes 2359300
  287.6 4.6 copy-start.2
  287.6 4.6 copy-start.24
  287.6 4.6 copy-start.29
  291.2 5.9 copy-start.32
  303.0 2.6 copy-start.3
  306.2 28.7 %copy-start.13 = (bf16[2048,768]{0,1:T(8,128)(2,1)}, bf16[2048,768]{0,1:T(8,128)(2,1)S(1)}, u32[]{:S(2)}) copy-start(bf16[2048,768]{0,1:T(8,128)(2,1)S(1)} %get-tuple-element.95) | copy-start | bytes 9437188
  334.9 38.2 %slice-start.2 = ((s8[6291456]{0:T(1024)(128)(4,1)}), s8[4194304]{0:T(1024)(128)(4,1)S(1)}, s32[]{:S(2)}) async-start(s8[6291456]{0:T(1024)(128)(4,1)} %bitcast.91), calls=%async_computation.7 | async-start | bytes 8388608
  351.3 21.7 %copy-start.23 = (f32[2048]{0:T(1024)S(1)}, f32[2048]{0:T(1024)}, u32[]{:S(2)}) copy-start(f32[2048]{0:T(1024)} %copy-done.22) | copy-start | bytes 24580
  351.3 21.8 %slice-start.3 = ((s8[6291456]{0:T(1024)(128)(4,1)}), s8[2097152]{0:T(1024)(128)(4,1)S(1)}, s32[]{:S(2)}) async-start(s8[6291456]{0:T(1024)(128)(4,1)} %bitcast.91), calls=%async_computation.8 | async-start | bytes 4194304
  377.0 6.8 copy-start
  377.6 6.2 copy-start.14
  493.8 5.8 copy-start.34
  493.8 5.8 copy-start.33
  493.9 5.8 copy-start.10
  499.6 5.7 copy-start.18
  499.6 5.7 copy-start.36
  505.3 5.4 copy-start.4
  510.8 5.5 copy-start.15
  510.8 5.5 copy-start.16
  520.7 405.9 %reduce-scatter.3.cloned.1.call-start = ((), (), s32[]{:S(2)}) async-start(), calls=%async_computation.3 | async-start | bytes 9732096 | tf_op jit(solution)/shard_map/reduce_scatter | solution.py:550
  554.0 7.7 copy-start.11
  554.0 13.6 %slice-start = ((s8[6291456]{0:T(1024)(128)(4,1)}), s8[4194304]{0:T(1024)(128)(4,1)S(1)}, s32[]{:S(2)}) async-start(s8[6291456]{0:T(1024)(128)(4,1)} %bitcast.89), calls=%async_computation.5 | async-start | bytes 8388608
  561.7 5.9 slice-start.1
  574.7 9.3 copy-start.5
  576.2 20.7 %collective-permute-start.9 = (bf16[512,768]{0,1:T(8,128)(2,1)}, bf16[512,768]{0,1:T(8,128)(2,1)}, u32[]{:S(2)}, u32[]{:S(2)}) collective-permute-start(bf16[512,768]{0,1:T(8,128)(2,1)} %get-tuple-element.107), channel_id=1, source_target_pairs={{0,1},{1,0},{2,3},{3,2},{4,5},{5,4},{6,7},{7,6},{8,9},{9,8},{10,11... | collective-permute-start | bytes 2359304 | tf_op jit(solution)/shard_map/ppermute | solution.py:439
  582.0 42.9 %collective-permute-start.10 = (bf16[512,768]{0,1:T(8,128)(2,1)}, bf16[512,768]{0,1:T(8,128)(2,1)}, u32[]{:S(2)}, u32[]{:S(2)}) collective-permute-start(bf16[512,768]{0,1:T(8,128)(2,1)} %get-tuple-element.106), channel_id=1, source_target_pairs={{0,2},{1,3},{2,0},{3,1},{4,6},{5,7},{6,4},{7,5},{8,10},{9,11},{10,... | collective-permute-start | bytes 2359304 | tf_op jit(solution)/shard_map/ppermute | solution.py:439
  582.5 45.4 %collective-permute-start.11 = (bf16[512,768]{0,1:T(8,128)(2,1)}, bf16[512,768]{0,1:T(8,128)(2,1)}, u32[]{:S(2)}, u32[]{:S(2)}) collective-permute-start(bf16[512,768]{0,1:T(8,128)(2,1)} %get-tuple-element.105), channel_id=1, source_target_pairs={{0,3},{1,2},{2,1},{3,0},{4,7},{5,6},{6,5},{7,4},{8,11},{9,10},{10,... | collective-permute-start | bytes 2359304 | tf_op jit(solution)/shard_map/ppermute | solution.py:439
  585.8 7.4 copy-start.9
  587.3 53.3 %collective-permute-start.3 = (bf16[512,768]{0,1:T(8,128)(2,1)}, bf16[512,768]{0,1:T(8,128)(2,1)}, u32[]{:S(2)}, u32[]{:S(2)}) collective-permute-start(bf16[512,768]{0,1:T(8,128)(2,1)} %get-tuple-element.114), channel_id=1, source_target_pairs={{0,1},{1,0},{2,3},{3,2},{4,5},{5,4},{6,7},{7,6},{8,9},{9,8},{10,11... | collective-permute-start | bytes 2359304 | tf_op jit(solution)/shard_map/ppermute | solution.py:439
  588.8 76.8 %collective-permute-start.4 = (bf16[512,768]{0,1:T(8,128)(2,1)}, bf16[512,768]{0,1:T(8,128)(2,1)}, u32[]{:S(2)}, u32[]{:S(2)}) collective-permute-start(bf16[512,768]{0,1:T(8,128)(2,1)} %get-tuple-element.113), channel_id=1, source_target_pairs={{0,2},{1,3},{2,0},{3,1},{4,6},{5,7},{6,4},{7,5},{8,10},{9,11},{10,... | collective-permute-start | bytes 2359304 | tf_op jit(solution)/shard_map/ppermute | solution.py:439
  589.6 8.7 copy-start.12
  596.9 71.0 %collective-permute-start.5 = (bf16[512,768]{0,1:T(8,128)(2,1)}, bf16[512,768]{0,1:T(8,128)(2,1)}, u32[]{:S(2)}, u32[]{:S(2)}) collective-permute-start(bf16[512,768]{0,1:T(8,128)(2,1)} %get-tuple-element.112), channel_id=1, source_target_pairs={{0,3},{1,2},{2,1},{3,0},{4,7},{5,6},{6,5},{7,4},{8,11},{9,10},{10,... | collective-permute-start | bytes 2359304 | tf_op jit(solution)/shard_map/ppermute | solution.py:439
  640.6 37.2 %copy-start.7 = (f32[1,512,768]{2,1,0:T(8,128)S(1)}, f32[1,512,768]{2,1,0:T(8,128)}, u32[]{:S(2)}) copy-start(f32[1,512,768]{2,1,0:T(8,128)} %copy.128) | copy-start | bytes 4718596
  670.3 8.8 copy-start.8
Sparse Core Ops, SparseCore 0:
  18.0 80.9 all-gather.2
  102.5 88.7 all-gather.4
  520.8 265.0 all-reduce.5
  791.7 134.8 reduce-scatter.2

commit v2 on v1

--- a/solution.py
+++ b/solution.py
@@ -290,7 +290,11 @@
 LOG2E = 1.4426950408889634
 PAD = 16
 VMEM = 60 << 20
-CHUNK = 512
+RATE = 1e9
+
+
+def cost(microseconds):
+    return pl.CostEstimate(flops=int(microseconds * RATE), bytes_accessed=0, transcendentals=0)
 
 
 def contract(former, latter, dim_former, dim_latter):
@@ -302,8 +306,11 @@
     )
 
 
-def mix_kernel(scale, qt, kt, vt, bias, mixed, total, probs, keys, vals):
+def mix_kernel(scale, chunk, me, qt, kt, vt, bias, mixed, total, probs, keys, vals):
     size, slots = kt.shape[1], kt.shape[2]
+    places = [
+        pl.ds(pl.multiple_of((me[0] ^ b) * chunk, chunk), chunk) for b in range(slots // chunk)
+    ]
     key = kt[0]
     keys[...] = jnp.concatenate([key, key, bias[...]], 0).T
     vals[...] = jnp.concatenate([vt[0], jnp.ones((PAD, slots), jnp.bfloat16)], 0)
@@ -321,39 +328,45 @@
         return weight
 
     sums, top = None, None
-    for at in range(0, slots, CHUNK):
-        scores = contract(keys[at : at + CHUNK], columns, 1, 0)
+    for at in places:
+        scores = contract(keys[at], columns, 1, 0)
         if top is None:
-            top = jnp.max(scores[:256], 0, keepdims=True)
+            top = jnp.max(scores[: chunk // 2], 0, keepdims=True)
         part = jnp.exp2(scores - top).astype(jnp.bfloat16)
-        probs[0, at : at + CHUNK] = part
-        term = contract(vals[:, at : at + CHUNK], part, 1, 0)
+        probs[0, at] = part
+        term = contract(vals[:, at], part, 1, 0)
         sums = term if sums is None else sums + term
     weight = finish(sums)
 
     @pl.when(jnp.logical_not(jnp.max(weight) < 2.0**60))
     def _():
         top = jnp.full((1, slots), -jnp.inf, jnp.float32)
-        for at in range(0, slots, CHUNK):
-            scores = contract(keys[at : at + CHUNK], columns, 1, 0)
+        for at in places:
+            scores = contract(keys[at], columns, 1, 0)
             top = jnp.maximum(top, jnp.max(scores, 0, keepdims=True))
         sums = None
-        for at in range(0, slots, CHUNK):
-            scores = contract(keys[at : at + CHUNK], columns, 1, 0)
+        for at in places:
+            scores = contract(keys[at], columns, 1, 0)
             part = jnp.exp2(scores - top).astype(jnp.bfloat16)
-            probs[0, at : at + CHUNK] = part
-            term = contract(vals[:, at : at + CHUNK], part, 1, 0)
+            probs[0, at] = part
+            term = contract(vals[:, at], part, 1, 0)
             sums = term if sums is None else sums + term
         finish(sums)
 
 
-def mix(qt, kt, vt, bias, scale):
+def mix(me, qt, kt, vt, bias, scale, chunk):
     heads, size, slots = qt.shape
     whole = pl.BlockSpec((1, size, slots), lambda i: (i, 0, 0))
     return pl.pallas_call(
-        functools.partial(mix_kernel, scale),
+        functools.partial(mix_kernel, scale, chunk),
         grid=(heads,),
-        in_specs=[whole, whole, whole, pl.BlockSpec((PAD, slots), lambda i: (0, 0))],
+        in_specs=[
+            pl.BlockSpec(memory_space=pltpu.SMEM),
+            whole,
+            whole,
+            whole,
+            pl.BlockSpec((PAD, slots), lambda i: (0, 0)),
+        ],
         out_specs=[
             whole,
             pl.BlockSpec((1, 1, slots), lambda i: (i, 0, 0)),
@@ -369,12 +382,15 @@
             pltpu.VMEM((size + PAD, slots), jnp.bfloat16),
         ],
         compiler_params=pltpu.CompilerParams(vmem_limit_bytes=VMEM),
+        cost_estimate=cost(57),
         name="mix",
-    )(qt, kt, vt, bias)
-
-
-def unmix_kernel(scale, probs, qt, kt, vt, gt, mt, total, dq, dk, dv, grads, inner, sums):
+    )(me, qt, kt, vt, bias)
+
+
+def unmix_kernel(scale, probs, qt, kt, vt, gt, mt, total, out, grads, inner, sums):
     step, last = pl.program_id(1), pl.num_programs(1) - 1
+    keys = kt.shape[2]
+    here = pl.ds(pl.multiple_of(step * keys, keys), keys)
 
     @pl.when(step == 0)
     def _():
@@ -389,8 +405,8 @@
     dprob = contract(vt[0], grad, 0, 0)
     dscore = (prob.astype(jnp.float32) * (dprob - inner[...])).astype(jnp.bfloat16)
     part = contract(kt[0], dscore, 1, 0)
-    dv[0] = contract(prob, grad, 1, 1).T.astype(jnp.bfloat16)
-    dk[0] = (contract(dscore, qt[0], 1, 1) * scale).T.astype(jnp.bfloat16)
+    out[2, 0, :, here] = contract(prob, grad, 1, 1).T.astype(jnp.bfloat16)
+    out[1, 0, :, here] = (contract(dscore, qt[0], 1, 1) * scale).T.astype(jnp.bfloat16)
 
     @pl.when(step == 0)
     def _():
@@ -402,7 +418,7 @@
 
     @pl.when(step == last)
     def _():
-        dq[0] = (sums[...] * scale).astype(jnp.bfloat16)
+        out[0, 0] = (sums[...] * scale).astype(jnp.bfloat16)
 
 
 def unmix(probs, qt, kt, vt, gt, mt, total, scale):
@@ -422,14 +438,15 @@
             whole,
             pl.BlockSpec((1, 1, slots), lambda i, j: (i, 0, 0)),
         ],
-        out_specs=[whole, part, part],
-        out_shape=[jax.ShapeDtypeStruct((heads, size, slots), jnp.bfloat16)] * 3,
+        out_specs=pl.BlockSpec((3, 1, size, slots), lambda i, j: (0, i, 0, 0)),
+        out_shape=jax.ShapeDtypeStruct((3, heads, size, slots), jnp.bfloat16),
         scratch_shapes=[
             pltpu.VMEM((size, slots), jnp.bfloat16),
             pltpu.VMEM((1, slots), jnp.float32),
             pltpu.VMEM((size, slots), jnp.float32),
         ],
         compiler_params=pltpu.CompilerParams(vmem_limit_bytes=VMEM),
+        cost_estimate=cost(110),
         name="unmix",
     )(probs, qt, kt, vt, gt, mt, total)
 
@@ -446,19 +463,289 @@
 def to_own(array):
     me = lax.axis_index("seq")
     pieces = [take(array, me)]
-    pieces += [swap(take(array, me ^ step), step) for step in range(1, lax.axis_size("seq"))]
-    return jnp.concatenate(pieces, 0)
-
-
-def to_split(rows, own, blank):
-    me = lax.axis_index("seq")
+    return pieces + [swap(take(array, me ^ step), step) for step in range(1, lax.axis_size("seq"))]
+
+
+def to_split(rows):
     size = lax.axis_size("seq")
     block = rows.shape[0] // size
-    result = lax.dynamic_update_index_in_dim(blank, own.astype(blank.dtype), me, 0)
-    for step in range(1, size):
-        came = swap(rows[step * block : (step + 1) * block], step)
-        result = lax.dynamic_update_index_in_dim(result, came.astype(blank.dtype), me ^ step, 0)
+    pieces = [rows[step * block : (step + 1) * block] for step in range(size)]
+    return pieces[:1] + [swap(pieces[step], step) for step in range(1, size)]
+
+
+def placed(pieces, dtype):
+    me = lax.axis_index("seq")
+    result = jnp.zeros((len(pieces),) + pieces[0].shape, dtype)
+    for step, piece in enumerate(pieces):
+        result = lax.dynamic_update_index_in_dim(result, piece.astype(dtype), me ^ step, 0)
     return result
+
+
+def row_sums(array):
+    return jnp.sum(array, 0, keepdims=True)
+
+
+def project_kernel(count, *refs):
+    pieces, (w, vec, x, qt, kt, vt) = refs[:count], refs[count:]
+    width = x.shape[1]
+    bias = vec[...]
+    for i, piece in enumerate(pieces):
+
+        @pl.when(pl.program_id(0) == i)
+        def _(piece=piece):
+            x[...] = piece[...]
+
+    outs = matmul(x[...], w[...])
+    for i, out in enumerate((qt, kt, vt)):
+        part = outs[:, i * width : (i + 1) * width]
+        if i != 1:
+            part = part + bias[i // 2 : i // 2 + 1]
+        out[...] = part.astype(jnp.bfloat16).T
+
+
+def project(pieces, first, vec):
+    rows, width = pieces[0].shape
+    count = len(pieces)
+    slots = count * rows
+    flat = pl.BlockSpec((width, rows), lambda i: (0, i))
+    one = pl.Buffered(1)
+    return pl.pallas_call(
+        functools.partial(project_kernel, count),
+        grid=(count,),
+        in_specs=[pl.BlockSpec((rows, width), lambda i: (0, 0), pipeline_mode=one)] * count
+        + [
+            pl.BlockSpec((width, 3 * width), lambda i: (0, 0), pipeline_mode=one),
+            pl.BlockSpec(vec.shape, lambda i: (0, 0)),
+        ],
+        out_specs=[pl.BlockSpec((rows, width), lambda i: (i, 0))] + [flat] * 3,
+        out_shape=[jax.ShapeDtypeStruct((slots, width), jnp.bfloat16)]
+        + [jax.ShapeDtypeStruct((width, slots), jnp.bfloat16)] * 3,
+        compiler_params=pltpu.CompilerParams(vmem_limit_bytes=VMEM),
+        cost_estimate=cost(11),
+        name="project",
+    )(*pieces, first, vec)
+
+
+def norm(rows):
+    centre = rows - jnp.mean(rows, -1, keepdims=True)
+    rstd = lax.rsqrt(jnp.mean(centre * centre, -1, keepdims=True) + epsilon)
+    return centre * rstd, rstd
+
+
+def norm_back(unit, rstd, grad):
+    mean = jnp.mean(grad, -1, keepdims=True)
+    inner = jnp.mean(grad * unit, -1, keepdims=True)
+    return rstd * (grad - mean - unit * inner)
+
+
+def feed_kernel(
+    x, mt, cot, live, vec, bu, wo, wu, wd,
+    output, grad_one, gt, left, right, sums, up_sums, slope,
+):
+    width = x.shape[1]
+    wide = wu.shape[1]
+    step = pl.program_id(0)
+    bo, g1, s1, bd, g2, s2 = (vec[i : i + 1] for i in range(2, 8))
+    mixed = mt[...].T
+    left[:, wide + width :] = mixed
+    resid = x[...].astype(jnp.float32) + matmul(mixed, wo[...]) + bo
+    unit_one, rstd_one = norm(resid)
+    normed = unit_one * g1 + s1
+    low = normed.astype(jnp.bfloat16)
+    left[:, :width] = low
+    resid = normed + bd
+    for at in range(0, wide, width):
+        cut = slice(at, at + width)
+        hidden = matmul(low, wu[:, cut]) + bu[:, cut]
+        share = 0.5 + 0.5 * lax.erf(hidden * 0.7071067811865476)
+        bell = jnp.exp2(hidden * hidden * -0.7213475204444817) * 0.3989422804014327
+        slope[:, cut] = (share + hidden * bell).astype(jnp.bfloat16)
+        active = (hidden * share).astype(jnp.bfloat16)
+        left[:, width + at : 2 * width + at] = active
+        resid = resid + matmul(active, wd[:, cut])
+    unit_two, rstd_two = norm(resid)
+    output[...] = (unit_two * g2 + s2).astype(jnp.bfloat16)
+    incoming = cot[...].astype(jnp.float32) * live[...]
+    grad_two = norm_back(unit_two, rstd_two, incoming * g2)
+    feed = grad_two.astype(jnp.bfloat16)
+    right[:, wide : wide + width] = feed
+    grad = grad_two
+    up_rows = []
+    for at in range(0, wide, width):
+        cut = slice(at, at + width)
+        part = contract(feed, wd[:, cut], 1, 1) * slope[:, cut].astype(jnp.float32)
+        part = part.astype(jnp.bfloat16)
+        right[:, cut] = part
+        up_rows.append(row_sums(part.astype(jnp.float32)))
+        grad = grad + contract(part, wu[:, cut], 1, 1)
+    first = norm_back(unit_one, rstd_one, grad * g1)
+    grad_one[...] = first
+    branch = first.astype(jnp.bfloat16)
+    right[:, wide + width :] = branch
+    gt[...] = contract(wo[...], branch, 1, 1).astype(jnp.bfloat16)
+    rows = [
+        row_sums(branch.astype(jnp.float32)),
+        row_sums(grad * unit_one),
+        row_sums(grad),
+        row_sums(feed.astype(jnp.float32)),
+        row_sums(incoming * unit_two),
+        row_sums(incoming),
+    ]
+    rows = jnp.concatenate(rows + [jnp.zeros((2, width), jnp.float32)], 0)
+    wide_rows = jnp.concatenate(up_rows, 1)
+
+    @pl.when(step == 0)
+    def _():
+        sums[...] = rows
+        up_sums[...] = wide_rows
+
+    @pl.when(step > 0)
+    def _():
+        sums[...] += rows
+        up_sums[...] += wide_rows
+
+
+def feed(x, mt, cot, live, vec, bu, second, rows):
+    slots, width = x.shape
+    wide = bu.shape[1]
+    one = pl.Buffered(1)
+    flat = pl.BlockSpec((rows, width), lambda i: (i, 0))
+    tall = pl.BlockSpec((width, rows), lambda i: (0, i))
+    stack = wide + 2 * width
+    broad = pl.BlockSpec((rows, stack), lambda i: (i, 0))
+    low = jnp.bfloat16
+    return pl.pallas_call(
+        feed_kernel,
+        grid=(slots // rows,),
+        in_specs=[
+            flat,
+            tall,
+            flat,
+            pl.BlockSpec((rows, 1), lambda i: (i, 0)),
+            pl.BlockSpec(vec.shape, lambda i: (0, 0)),
+            pl.BlockSpec((1, wide), lambda i: (0, 0)),
+            pl.BlockSpec((width, width), lambda i: (0, 2 * wide // width), pipeline_mode=one),
+            pl.BlockSpec((width, wide), lambda i: (0, 0), pipeline_mode=one),
+            pl.BlockSpec((width, wide), lambda i: (0, 1), pipeline_mode=one),
+        ],
+        out_specs=[
+            flat,
+            flat,
+            tall,
+            broad,
+            broad,
+            pl.BlockSpec((8, width), lambda i: (0, 0)),
+            pl.BlockSpec((1, wide), lambda i: (0, 0)),
+        ],
+        out_shape=[
+            jax.ShapeDtypeStruct((slots, width), low),
+            jax.ShapeDtypeStruct((slots, width), jnp.float32),
+            jax.ShapeDtypeStruct((width, slots), low),
+            jax.ShapeDtypeStruct((slots, stack), low),
+            jax.ShapeDtypeStruct((slots, stack), low),
+            jax.ShapeDtypeStruct((8, width), jnp.float32),
+            jax.ShapeDtypeStruct((1, wide), jnp.float32),
+        ],
+        scratch_shapes=[pltpu.VMEM((rows, wide), low)],
+        compiler_params=pltpu.CompilerParams(vmem_limit_bytes=VMEM),
+        cost_estimate=cost(70),
+        name="feed",
+    )(x, mt, cot, live, vec, bu, second, second, second)
+
+
+def feed_weights_kernel(left, right, d_w):
+    d_w[...] = contract(left[...], right[...], 0, 0).astype(d_w.dtype)
+
+
+def feed_weights(left, right, width):
+    slots, stack = left.shape
+    parts = stack // width - 2
+    return pl.pallas_call(
+        feed_weights_kernel,
+        grid=(2 * parts + 1,),
+        in_specs=[
+            pl.BlockSpec((slots, width), lambda i: (0, jnp.maximum(i - parts + 1, 0))),
+            pl.BlockSpec(
+                (slots, width), lambda i: (0, jnp.minimum(i, parts) + i // (2 * parts))
+            ),
+        ],
+        out_specs=pl.BlockSpec((width, width), lambda i: (0, i)),
+        out_shape=jax.ShapeDtypeStruct((width, (2 * parts + 1) * width), jnp.bfloat16),
+        compiler_params=pltpu.CompilerParams(vmem_limit_bytes=VMEM),
+        cost_estimate=cost(26),
+        name="feed_weights",
+    )(left, right)
+
+
+def inputs_kernel(grads, weights, grad_one, low):
+    low[...] = (contract(grads[...], weights[...], 0, 1) + grad_one[...]).astype(low.dtype)
+
+
+def inputs(grads, first, grad_one, rows):
+    depth, slots = grads.shape
+    width = first.shape[0]
+    flat = pl.BlockSpec((rows, width), lambda i: (i, 0))
+    return pl.pallas_call(
+        inputs_kernel,
+        grid=(slots // rows,),
+        in_specs=[
+            pl.BlockSpec((depth, rows), lambda i: (0, i)),
+            pl.BlockSpec((width, depth), lambda i: (0, 0), pipeline_mode=pl.Buffered(1)),
+            flat,
+        ],
+        out_specs=flat,
+        out_shape=jax.ShapeDtypeStruct((slots, width), jnp.bfloat16),
+        compiler_params=pltpu.CompilerParams(vmem_limit_bytes=VMEM),
+        cost_estimate=cost(12),
+        name="inputs",
+    )(grads, first, grad_one)
+
+
+def input_weights_kernel(x, grads, rows, d_w, edges):
+    step, last = pl.program_id(0), pl.num_programs(0) - 1
+    width = x.shape[1]
+    depth = 3 * width
+    size = grads.shape[0]
+    grad = grads[...]
+    product = contract(x[...], grad, 0, 1).astype(d_w.dtype)
+    edge = jnp.sum(grad.astype(jnp.float32), 1, keepdims=True)
+    for i in range(depth // size):
+
+        @pl.when(step == i)
+        def _(i=i):
+            d_w[:, i * size : (i + 1) * size] = product
+            column, top = i * size // width, i * size % width
+            edges[top : top + size, column : column + 1] = edge
+
+    @pl.when(step == last)
+    def _():
+        known = rows[...]
+        tall = jnp.concatenate([known, jnp.zeros((128 - known.shape[0], width), jnp.float32)], 0).T
+        column = lax.broadcasted_iota(jnp.int32, (width, 128), 1)
+        sums = edges[...]
+        columns = jnp.where(column == 0, sums[:, :1], jnp.where(column == 1, sums[:, 2:3], tall))
+        d_w[:, depth:] = columns.astype(d_w.dtype)
+
+
+def input_weights(x, grads, rows, size):
+    slots, width = x.shape
+    depth = grads.shape[0]
+    one = pl.Buffered(1)
+    return pl.pallas_call(
+        input_weights_kernel,
+        grid=(depth // size,),
+        in_specs=[
+            pl.BlockSpec((slots, width), lambda i: (0, 0), pipeline_mode=one),
+            pl.BlockSpec((size, slots), lambda i: (i, 0)),
+            pl.BlockSpec(rows.shape, lambda i: (0, 0)),
+        ],
+        out_specs=pl.BlockSpec((width, depth + 128), lambda i: (0, 0)),
+        out_shape=jax.ShapeDtypeStruct((width, depth + 128), jnp.bfloat16),
+        scratch_shapes=[pltpu.VMEM((width, 128), jnp.float32)],
+        compiler_params=pltpu.CompilerParams(vmem_limit_bytes=VMEM),
+        cost_estimate=cost(12),
+        name="input_weights",
+    )(x, grads, rows)
 
 
 def whole_body(
@@ -491,90 +778,77 @@
     scale = size ** (-0.5)
     times = wide // width
 
-    vectors = [b_query, b_value, b_out, gain_one, shift_one, b_down, gain_two, shift_two]
-    columns = [v.reshape(rows, 1) for v in vectors] + [b_up.reshape(rows, times)]
-    columns = jnp.concatenate(columns, 1)
-    columns = jnp.pad(columns, ((0, 0), (0, 128 - columns.shape[1])))
-    first = jnp.concatenate([w_query, w_key, w_value, w_out, columns], 1)
-    first = lax.all_gather(first, axes, axis=0, tiled=True)
-    second = jnp.concatenate([w_up, w_down.reshape(rows, wide)], 1)
+    vectors = [b_query, b_value, b_out, gain_one, shift_one, b_down, gain_two, shift_two, b_up]
+    vec = jnp.concatenate(vectors)
+    known = vec.shape[0]
+    vec = jnp.pad(vec, (0, 1024 - known)).reshape(8, 128)
+    first = jnp.concatenate([w_query, w_key, w_value], 1)
+    first = lax.all_gather(first, "seq", axis=0, tiled=True)
+    first = lax.all_gather(first, "dp", axis=0, tiled=True)
+    owners = width // rows
+    mixed_up = w_up.reshape(rows, owners, times, rows).transpose(0, 2, 1, 3).reshape(rows, wide)
+    downs = [w_down[i * rows : (i + 1) * rows] for i in range(times)]
+    second = jnp.concatenate([mixed_up] + downs + [w_out], 1)
+
+    pieces = to_own(tokens)
+    vec = lax.all_gather(vec, axes, axis=0, tiled=True)
+    vec, pieces = lax.optimization_barrier((vec, pieces))
+    second, first, pieces = lax.optimization_barrier((second, first, pieces))
     second = lax.all_gather(second, axes, axis=0, tiled=True)
-
-    x = to_own(tokens)
-    cot = to_own(cotangent)
     length = take(lengths, me)
     order = me ^ jnp.arange(count, dtype=jnp.int32)
     place = (order[:, None] * block + jnp.arange(block, dtype=jnp.int32)[None, :]).reshape(slots)
     live = place < length
     bias = jnp.where(live, 0.0, -1e30).astype(jnp.bfloat16)
     bias = jnp.pad(bias[None, :], ((0, PAD - 1), (0, 0)))
-
-    wq, wk, wv, wo = (first[:, i * width : (i + 1) * width] for i in range(4))
-    vec = first[:, 4 * width :].astype(jnp.float32).T
-    bq, bv, bo, g1, s1, bd, g2, s2 = (vec[i] for i in range(8))
-    bu = vec[8 : 8 + times].T.reshape(wide)
-    wu = second[:, :wide]
-    wd = second[:, wide:].reshape(wide, width)
-
-    def columns_of(weight):
-        return contract(weight, x, 0, 1)
+    live = live[:, None].astype(jnp.float32)
+
+    vec = vec.reshape(owners, 1024)[:, :known]
+    vec = vec.astype(jnp.float32).reshape(owners, 8 + times, rows).transpose(1, 0, 2)
+    vec = vec.reshape(8 + times, width)
+    bu = vec[8:].reshape(1, wide)
+    vec = vec[:8]
 
     def by_head(array):
-        return array.astype(jnp.bfloat16).reshape(heads, size, slots)
-
-    qt = by_head(columns_of(wq) + bq[:, None])
-    kt = by_head(columns_of(wk))
-    vt = by_head(columns_of(wv) + bv[:, None])
-    mt, total, probs = mix(qt, kt, vt, bias, scale * LOG2E)
-    mixed = mt.reshape(width, slots)
-    resid_one = x.astype(jnp.float32) + contract(mixed, wo, 0, 0) + bo
-    normed = layer_norm(resid_one, g1, s1)
-    normed_low = normed.astype(jnp.bfloat16)
-    hidden = matmul(normed_low, wu) + bu
-    active_low = gelu_exact(hidden).astype(jnp.bfloat16)
-    resid_two = normed + matmul(active_low, wd) + bd
-    result = layer_norm(resid_two, g2, s2).astype(jnp.bfloat16)
-    output = to_split(result, result[:block], jnp.zeros((count, block, width), jnp.bfloat16))
-
-    incoming = cot.astype(jnp.float32) * live[:, None].astype(jnp.float32)
-    _, second_pull = jax.vjp(layer_norm, resid_two, g2, s2)
-    grad_two, d_g2, d_s2 = second_pull(incoming)
-    feed_low = grad_two.astype(jnp.bfloat16)
-    d_wd = former_product(active_low, feed_low)
-    d_bd = jnp.sum(feed_low.astype(jnp.float32), 0)
-    _, gelu_pull = jax.vjp(gelu_exact, hidden)
-    up_low = gelu_pull(latter_product(feed_low, wd))[0].astype(jnp.bfloat16)
-    d_wu = former_product(normed_low, up_low)
-    d_bu = jnp.sum(up_low.astype(jnp.float32), 0)
-    late = jnp.concatenate([d_wu, d_wd.reshape(width, wide)], 1).astype(jnp.bfloat16)
-    late = lax.psum_scatter(late, axes, scatter_dimension=0, tiled=True).astype(jnp.float32)
-    grad_normed = latter_product(up_low, wu) + grad_two
-    _, first_pull = jax.vjp(layer_norm, resid_one, g1, s1)
-    grad_one, d_g1, d_s1 = first_pull(grad_normed)
-    branch_low = grad_one.astype(jnp.bfloat16)
-    d_wo = matmul(mixed, branch_low)
-    d_bo = jnp.sum(branch_low.astype(jnp.float32), 0)
-    gt = by_head(latter_product(wo, branch_low))
-    dq, dk, dv = unmix(probs, qt, kt, vt, gt, mt, total, scale)
-    dq, dk, dv = (g.reshape(width, slots) for g in (dq, dk, dv))
-    d_wq, d_wk, d_wv = (contract(x, g, 0, 1) for g in (dq, dk, dv))
-    d_bq, d_bv = (jnp.sum(g.astype(jnp.float32), 1) for g in (dq, dv))
-    grad_x = contract(dq, wq, 0, 1) + contract(dk, wk, 0, 1) + contract(dv, wv, 0, 1) + grad_one
-    grad_tokens = to_split(
-        grad_x.astype(jnp.bfloat16), grad_x[:block], jnp.zeros((count, block, width), jnp.float32)
-    )
-
-    columns = jnp.stack([d_bq, d_bv, d_bo, d_g1, d_s1, d_bd, d_g2, d_s2], 1)
-    columns = jnp.concatenate([columns, d_bu.reshape(width, times)], 1)
-    columns = jnp.pad(columns, ((0, 0), (0, 128 - columns.shape[1])))
-    early = jnp.concatenate([d_wq, d_wk, d_wv, d_wo, columns], 1).astype(jnp.bfloat16)
-    early = lax.psum_scatter(early, axes, scatter_dimension=0, tiled=True).astype(jnp.float32)
-    o_wq, o_wk, o_wv, o_wo = (early[:, i * width : (i + 1) * width] for i in range(4))
-    vec = early[:, 4 * width :]
+        return array.reshape(heads, size, slots)
+
+    x, qt, kt, vt = project(pieces, first, vec)
+    qt, cotangent = lax.optimization_barrier((qt, cotangent))
+    cot = jnp.concatenate(to_own(cotangent), 0)
+    qt, kt, vt = (by_head(a) for a in (qt, kt, vt))
+    mt, total, probs = mix(me.reshape(1), qt, kt, vt, bias, scale * LOG2E, block)
+    result, grad_one, gt, left, right, sums, up_sums = feed(
+        x, mt.reshape(width, slots), cot, live, vec, bu, second, block
+    )
+    late = feed_weights(left, right, width)
+    gt, late = lax.optimization_barrier((gt, late))
+    late = lax.psum_scatter(late, "dp", scatter_dimension=0, tiled=True)
+    output = to_split(result)
+    grads = unmix(probs, qt, kt, vt, by_head(gt), mt, total, scale)
+    grads, output, late = lax.optimization_barrier((grads, output, late))
+    late = lax.psum_scatter(late, "seq", scatter_dimension=0, tiled=True)
+    output = placed(output, jnp.bfloat16)
+    grads = grads.reshape(3 * width, slots)
+    edges = jnp.concatenate(
+        [jnp.zeros((2, width), jnp.float32), sums[:6], up_sums.reshape(times, width)], 0
+    )
+    early = input_weights(x, grads, edges, width // 2)
+    grads, early = lax.optimization_barrier((grads, early))
+    low = inputs(grads, first, grad_one, block)
+    grad_tokens = placed(to_split(low), jnp.float32)
+    early, late = lax.optimization_barrier((early, late))
+    early = lax.psum_scatter(early, "dp", scatter_dimension=0, tiled=True)
+    early = lax.psum_scatter(early, "seq", scatter_dimension=0, tiled=True).astype(jnp.float32)
+    late = late.astype(jnp.float32)
+    o_wq, o_wk, o_wv = (early[:, i * width : (i + 1) * width] for i in range(3))
+    vec = early[:, 3 * width :]
+    o_wu = late[:, :wide].reshape(rows, times, owners, rows).transpose(0, 2, 1, 3).reshape(rows, wide)
+    o_wd = jnp.concatenate(
+        [late[:, wide + i * width : wide + (i + 1) * width] for i in range(times)], 0
+    )
+    o_wo = late[:, 2 * wide :]
     o_bq, o_bv, o_bo, o_g1, o_s1, o_bd, o_g2, o_s2 = (vec[:, i] for i in range(8))
-    o_bu = vec[:, 8 : 8 + times].reshape(rows * times)
-    o_wu = late[:, :wide]
-    o_wd = late[:, wide:].reshape(rows * times, width)
+    o_bu = vec[:, 8 : 8 + times].T.reshape(rows * times)
     return (
         output,
         grad_tokens,

time: 939 us -> 545 us (0.58)
  waiting for transfers between devices: 351 us -> 47.2 us
  matrix products: 238 us -> 0 us
  Pallas kernels: 167 us -> 311 us
  blocking collectives: 0 us -> 98.6 us
  local copies, waits for them, and re-layouts: 105 us -> 38.7 us
  other arithmetic: 45.1 us -> 15.7 us
    dot_general x18 -> x0, matrix products: 238 us -> none  [the longest x3 86.7 us: matmul(): return jnp.dot(former, latter, preferred_element_type=jnp.float32)]
    pallas_call x1 -> x6, Pallas kernels: 56.6 us -> 202 us  [the longest x1 71.2 us: feed(): pl.pallas_call(feed_kernel, grid=(slots // rows,), in_specs=[flat, tall,...]
    reduce_scatter x1 -> x2, waiting for transfers between devices: 134 us -> 14 us  [the longest x1 14 us: whole_body(): early = lax.psum_scatter(early, 'dp', scatter_dimension=0, tiled=True)]
    all_gather x0 -> x2, blocking collectives: none -> 98.6 us  [the longest x1 86.6 us: whole_body(): vec = lax.all_gather(vec, axes, axis=0, tiled=True)]
    unnamed x5 -> x7, waiting for transfers between devices: 106 us -> 12.5 us
    ppermute x12, waiting for transfers between devices: 59.5 us -> 0.58 us  [swap(): return lax.ppermute(piece, 'seq', [(i, i ^ step) for i in range(size)])]
    all_gather x1, waiting for transfers between devices: 49.3 us -> 0.02 us  [whole_body(): first = lax.all_gather(first, 'dp', axis=0, tiled=True)]
    reduce_sum x9 -> x0, other arithmetic: 25.1 us -> none  [the longest x2 9.75 us: layer_norm(): centre = layer_input_rows - jnp.mean(layer_input_rows, -1, keepdims=True)]
  transfers between devices with their start and end apart: 16 -> 18, of which waited for: 8 -> 5; matrix products, arithmetic and copies ran while one was open for 27% -> 9% of each run, Pallas kernels for 6% -> 39%
where the time goes in v2:
time: 545 us; the launch traced here: 541 us
  Pallas kernels  311 us (57%)
  blocking collectives  98.6 us (18%)
  waiting for transfers between devices  47.2 us (9%)
  local copies, waits for them, and re-layouts  38.7 us (7%)
  other arithmetic  15.7 us (3%)
  between operations  14.8 us (3%)
  starting transfers between devices  14.3 us (3%)
    pallas_call x1, Pallas kernels, unmix(): pl.pallas_call(functools.partial(unmix_kernel, scale), grid=(heads, slots...  110 us
    all_gather x1, blocking collectives, whole_body(): vec = lax.all_gather(vec, axes, axis=0, tiled=True)  86.6 us
    pallas_call x1, Pallas kernels, feed(): pl.pallas_call(feed_kernel, grid=(slots // rows,), in_specs=[flat, tall,...  71.2 us
    pallas_call x1, Pallas kernels, mix(): pl.pallas_call(functools.partial(mix_kernel, scale, chunk), grid=(heads,)...  59.3 us
    pallas_call x1, Pallas kernels, feed_weights(): pl.pallas_call(feed_weights_kernel, grid=(2 * parts + 1,), in_specs=[pl.B...  29.3 us
    pallas_call x1, Pallas kernels, input_weights(): pl.pallas_call(input_weights_kernel, grid=(depth // size,), in_specs=[pl....  16 us
    ppermute x12, starting transfers between devices, swap(): return lax.ppermute(piece, 'seq', [(i, i ^ step) for i in range(size)])  14.1 us
    reduce_scatter x1, waiting for transfers between devices, whole_body(): early = lax.psum_scatter(early, 'dp', scatter_dimension=0, tiled=True)  14 us
  transfers between devices with their start and end apart: 18, of which 5 were waited for; matrix products, arithmetic and copies ran while one was open for 9% of the time, Pallas kernels for 39%

profile of v2, /device:TPU:0, one launch (start us, length us, event | category | flops | bytes accessed | tf_op | source)
XLA Modules:
  0.0 540.5 jit_solution(16143730039024645129)
XLA Ops:
  7.2 0.8 pad_maximum_fusion.2
  8.0 11.9 %all_gather.12 = bf16[96,2304]{1,0:T(8,128)(2,1)} all-gather(bf16[24,2304]{1,0:T(8,128)(2,1)S(1)} %pad_maximum_fusion.2), channel_id=1, replica_groups=mesh['dp'=8,'seq'=4] {'seq'}, dimensions={0}, use_global_device_ids=true | all-gather | bytes 552960 | tf_op jit(solution)/shard_map/all_gather | solution.py:786
  20.1 3.2 dynamic-slice_bitcast_fusion.4
  23.5 1.5 collective-permute-start
  24.9 0.6 collective-permute-start.1
  25.5 1.5 collective-permute-start.2
  27.0 1.2 reshape.162
  28.3 0.2 copy.51
  28.4 1.3 reshape.163
  29.9 86.6 %all_gather.14 = bf16[256,128]{1,0:T(8,128)(2,1)S(1)} all-gather(bf16[8,128]{1,0:T(8,128)(2,1)S(1)} %pad_bitcast_fusion), channel_id=1, replica_groups=mesh['dp'=8,'seq'=4] {'dp','seq'}, dimensions={0}, use_global_device_ids=true | all-gather | bytes 67584 | tf_op jit(solution)/shard_map/all_gather | solution.py:794
  116.7 0.7 copy-done.2
  117.4 0.6 dynamic_slice.33
  118.0 0.7 fusion
  118.7 0.7 convert_bitcast_fusion
  119.5 1.3 copy.60
  120.8 0.6 pad.9.bias
  121.7 0.7 slice.122.refs_5_.vec
  122.5 0.7 reshape.171.bu
  123.2 12.9 %project.1 = (bf16[2048,768]{1,0:T(8,128)(2,1)}, bf16[768,2048]{1,0:T(8,128)(2,1)}, bf16[768,2048]{1,0:T(8,128)(2,1)}, bf16[768,2048]{1,0:T(8,128)(2,1)}) custom-call(bf16[512,768]{1,0:T(8,128)(2,1)} %get-tuple-element.60.refs_0_, bf16[512,768]{1,0:T(8,128)(2,1)} %collective-permute-done.refs_1_, bf16[512,768]{1,0:T(8,128)(2,1)} %collective-permute-done.1.refs_2_, ...), custom_call_target="tpu_custom_call" | custom-call | flops 11000000512 | tf_op jit(solution)/shard_map/project/pallas_call | solution.py:512
  136.1 1.5 dynamic-slice_bitcast_fusion.3
  137.6 0.6 collective-permute-start.3
  138.2 2.9 collective-permute-start.5
  141.1 59.3 %mix.1 = (bf16[12,64,2048]{2,1,0:T(8,128)(2,1)}, f32[12,1,2048]{2,1,0:T(1,128)}, bf16[12,2048,2048]{2,1,0:T(8,128)(2,1)}) custom-call(s32[1]{0:T(128)} %bitcast.me, bf16[12,64,2048]{2,1,0:T(8,128)(2,1)} %bitcast.78, bf16[12,64,2048]{2,1,0:T(8,128)(2,1)} %bitcast.80, bf16[12,64,2048]{2,1,0:T(8,128)(2,1)} %bitcast.82, bf16[16,2048]{1,0:T(8,128)(2,1)} %pad.9.bias), custom_call_target="tpu_custom_call" | custom-call | flops 57000001536 | tf_op jit(solution)/shard_map/mix/pallas_call | solution.py:360
  200.4 1.9 pad_maximum_fusion.cot
  202.3 8.6 %all-gather.5.cloned.1.call-done.wo.wu.wd = bf16[768,6912]{1,0:T(8,128)(2,1)} async-done(((bf16[24,6912]{1,0:T(8,128)(2,1)}), bf16[768,6912]{1,0:T(8,128)(2,1)}) %all-gather.5.cloned.1.call-update) | async-done | bytes 10616848 | tf_op jit(solution)/shard_map/all_gather | solution.py:797
  210.9 71.2 %feed.1 = (bf16[2048,768]{1,0:T(8,128)(2,1)}, f32[2048,768]{1,0:T(8,128)}, bf16[768,2048]{1,0:T(8,128)(2,1)}, bf16[2048,4608]{1,0:T(8,128)(2,1)}, bf16[2048,4608...) custom-call(bf16[2048,768]{1,0:T(8,128)(2,1)} %get-tuple-element.71.x, bf16[768,2048]{1,0:T(8,128)(2,1)} %bitcast.84, ...), custom_call_target="tpu_custom_call" | custom-call | flops 70000001024 | tf_op jit(solution)/shard_map/feed/pallas_call | solution.py:617
  282.1 29.3 %feed_weights.1 = bf16[768,6912]{1,0:T(8,128)(2,1)} custom-call(bf16[2048,4608]{1,0:T(8,128)(2,1)} %get-tuple-element.76.left, bf16[2048,4608]{1,0:T(8,128)(2,1)} %get-tuple-element.77.right), custom_call_target="tpu_custom_call" | custom-call | flops 25999998976 | tf_op jit(solution)/shard_map/feed_weights/pallas_call | solution.py:663
  311.4 2.0 fusion.2
  313.5 1.5 collective-permute-start.6
  315.0 0.6 collective-permute-start.7
  315.6 1.4 collective-permute-start.8
  317.1 109.7 %unmix.1 = bf16[3,12,64,2048]{3,2,1,0:T(8,128)(2,1)} custom-call(bf16[12,2048,2048]{2,1,0:T(8,128)(2,1)} %get-tuple-element.70.probs, bf16[12,64,2048]{2,1,0:T(8,128)(2,1)} %bitcast.79, bf16[12,64,2048]{2,1,0:T(8,128)(2,1)} %bitcast.81, bf16[12,64,2048]{2,1,0:T(8,128)(2,1)} %bitcast.83, bf16[12,64,2048]{2,1,0:T(8,128)(2,1)} %bitcast.85, ...), custom_call_target="tpu_custom_call" | custom-call | flops 109999996928 | tf_op jit(solution)/shard_map/unmix/pallas_call | solution.py:429
  426.9 0.5 broadcast.69
  427.4 0.7 reduce.19
  428.1 0.7 pad_maximum_fusion.3.rows
  428.8 16.0 %input_weights.1 = bf16[768,2432]{1,0:T(8,128)(2,1)} custom-call(bf16[2048,768]{1,0:T(8,128)(2,1)} %get-tuple-element.71.x, bf16[2304,2048]{1,0:T(8,128)(2,1)} %bitcast.76, f32[12,768]{1,0:T(8,128)} %pad_maximum_fusion.3.rows), custom_call_target="tpu_custom_call" | custom-call | flops 12000000000 | tf_op jit(solution)/shard_map/input_weights/pallas_call | solution.py:734
  444.7 11.5 %reduce-scatter.13.cloned.1.call-done = bf16[24,6912]{1,0:T(8,128)(2,1)} async-done(((bf16[96,6912]{1,0:T(8,128)(2,1)}), bf16[24,6912]{1,0:T(8,128)(2,1)}) %reduce-scatter.13.cloned.1.call-update) | async-done | bytes 331792 | tf_op jit(solution)/shard_map/optimization_barrier | solution.py:839
  456.3 13.0 %inputs.1 = bf16[2048,768]{1,0:T(8,128)(2,1)} custom-call(bf16[2304,2048]{1,0:T(8,128)(2,1)} %bitcast.77, bf16[768,2304]{1,0:T(8,128)(2,1)} %all-gather.3.cloned.1.call-done.refs_4_.weights, f32[2048,768]{1,0:T(8,128)} %get-tuple-element.90.grad_one), custom_call_target="tpu_custom_call" | custom-call | flops 12000000000 | tf_op jit(solution)/shard_map/inputs/pallas_call | solution.py:688
  469.3 2.7 fusion.1
  472.0 1.5 collective-permute-start.9
  473.5 0.7 collective-permute-start.10
  474.2 1.2 collective-permute-start.11
  475.5 1.9 broadcast_in_dim.59
  477.3 0.9 bitcast_dynamic-update-slice_fusion.3
  478.3 3.2 broadcast_in_dim.66
  481.5 2.4 convert_dynamic-update-slice_fusion.3
  483.9 2.1 bitcast_dynamic-update-slice_fusion.2
  486.0 2.1 bitcast_dynamic-update-slice_fusion.1
  488.0 2.1 bitcast_dynamic-update-slice_fusion
  490.1 14.0 %reduce-scatter.11.cloned.1.call-done = bf16[96,2432]{1,0:T(8,128)(2,1)} async-done(((bf16[768,2432]{1,0:T(8,128)(2,1)}), bf16[96,2432]{1,0:T(8,128)(2,1)}) %reduce-scatter.11.cloned.1.call-update) | async-done | bytes 466960 | tf_op jit(solution)/shard_map/reduce_scatter | solution.py:840
  504.1 2.4 convert_dynamic-update-slice_fusion.2
  506.5 2.4 convert_dynamic-update-slice_fusion.1
  508.9 0.6 collective-permute-done.11
  509.5 1.3 convert_dynamic-update-slice_fusion
  510.8 1.1 reshape.175
  511.9 1.2 copy.56
  513.1 2.6 reshape.176
  515.7 0.7 fusion.3
  516.4 0.7 pad_maximum_fusion.1
  517.1 12.4 %reduce-scatter.15.cloned.1.call-done = bf16[24,2432]{1,0:T(8,128)(2,1)} async-done(((bf16[96,2432]{1,0:T(8,128)(2,1)}), bf16[24,2432]{1,0:T(8,128)(2,1)}) %reduce-scatter.15.cloned.1.call-update) | async-done | bytes 116752
  529.5 0.9 convert_element_type.37
  530.5 0.8 slice_reduce_fusion
  531.4 0.6 reshape.177
  532.0 1.5 fusion.4
  (85 shorter events, 1.2 us)
Async XLA Ops:
  7.2 109.5 %all-gather.3.cloned.1.call-start = ((), (), s32[]{:S(2)}) async-start(), calls=%async_computation.4 | async-start | bytes 3981312 | tf_op jit(solution)/shard_map/all_gather | solution.py:787
  20.0 190.9 %all-gather.5.cloned.1.call-start = ((), (), s32[]{:S(2)}) async-start(), calls=%async_computation.5 | async-start | bytes 10948608 | tf_op jit(solution)/shard_map/all_gather | solution.py:797
  20.1 6.9 %copy-start.3 = (bf16[24,3072]{1,0:T(8,128)(2,1)S(1)}, bf16[24,3072]{1,0:T(8,128)(2,1)}, u32[]{:S(2)}) copy-start(bf16[24,3072]{1,0:T(8,128)(2,1)} %param.30) | copy-start | bytes 442372
  23.3 6.3 %copy-start.8 = (bf16[24]{0:T(256)(128)(2,1)S(1)}, bf16[24]{0:T(256)(128)(2,1)}, u32[]{:S(2)}) copy-start(bf16[24]{0:T(256)(128)(2,1)} %param.22) | copy-start | bytes 148
  23.3 6.3 %copy-start.9 = (bf16[24]{0:T(256)(128)(2,1)S(1)}, bf16[24]{0:T(256)(128)(2,1)}, u32[]{:S(2)}) copy-start(bf16[24]{0:T(256)(128)(2,1)} %param.25) | copy-start | bytes 148
  23.3 6.4 %copy-start.10 = (bf16[24]{0:T(256)(128)(2,1)S(1)}, bf16[24]{0:T(256)(128)(2,1)}, u32[]{:S(2)}) copy-start(bf16[24]{0:T(256)(128)(2,1)} %param.27) | copy-start | bytes 148
  23.3 6.4 %copy-start.11 = (bf16[24]{0:T(256)(128)(2,1)S(1)}, bf16[24]{0:T(256)(128)(2,1)}, u32[]{:S(2)}) copy-start(bf16[24]{0:T(256)(128)(2,1)} %param.28) | copy-start | bytes 148
  23.4 6.4 %copy-start.12 = (bf16[24]{0:T(256)(128)(2,1)S(1)}, bf16[24]{0:T(256)(128)(2,1)}, u32[]{:S(2)}) copy-start(bf16[24]{0:T(256)(128)(2,1)} %param.29) | copy-start | bytes 148
  23.4 6.4 %copy-start.13 = (bf16[24]{0:T(256)(128)(2,1)S(1)}, bf16[24]{0:T(256)(128)(2,1)}, u32[]{:S(2)}) copy-start(bf16[24]{0:T(256)(128)(2,1)} %param.33) | copy-start | bytes 148
  23.4 6.4 %copy-start.14 = (bf16[24]{0:T(256)(128)(2,1)S(1)}, bf16[24]{0:T(256)(128)(2,1)}, u32[]{:S(2)}) copy-start(bf16[24]{0:T(256)(128)(2,1)} %param.34) | copy-start | bytes 148
  23.4 6.4 %copy-start.15 = (bf16[24]{0:T(256)(128)(2,1)S(1)}, bf16[24]{0:T(256)(128)(2,1)}, u32[]{:S(2)}) copy-start(bf16[24]{0:T(256)(128)(2,1)} %param.35) | copy-start | bytes 148
  23.4 6.3 %copy-start.16 = (bf16[96]{0:T(256)(128)(2,1)S(1)}, bf16[96]{0:T(256)(128)(2,1)}, u32[]{:S(2)}) copy-start(bf16[96]{0:T(256)(128)(2,1)} %param.31) | copy-start | bytes 580
  23.4 93.1 %copy-start.4 = (bf16[96,768]{1,0:T(8,128)(2,1)S(1)}, bf16[96,768]{1,0:T(8,128)(2,1)}, u32[]{:S(2)}) copy-start(bf16[96,768]{1,0:T(8,128)(2,1)} %param.32) | copy-start | bytes 442372
  23.4 93.1 %copy-start.5 = (bf16[24,768]{1,0:T(8,128)(2,1)S(1)}, bf16[24,768]{1,0:T(8,128)(2,1)}, u32[]{:S(2)}) copy-start(bf16[24,768]{1,0:T(8,128)(2,1)} %param.26) | copy-start | bytes 110596
  23.4 93.9 %copy-start.17 = (s32[4]{0:T(128)S(1)}, s32[4]{0:T(128)}, u32[]{:S(2)}) copy-start(s32[4]{0:T(128)} %param.19) | copy-start | bytes 52
  23.5 93.2 %collective-permute-start = (bf16[512,768]{1,0:T(8,128)(2,1)}, bf16[512,768]{1,0:T(8,128)(2,1)}, u32[]{:S(2)}, u32[]{:S(2)}) collective-permute-start(bf16[512,768]{1,0:T(8,128)(2,1)} %get-tuple-element.115), channel_id=1, source_target_pairs={{0,1},{1,0},{2,3},{3,2},{4,5},{5,4},{6,7},{7,6},{8,9},{9,8},{10,11... | collective-permute-start | bytes 2359304 | tf_op jit(solution)/shard_map/ppermute | solution.py:456
  24.9 91.7 %collective-permute-start.1 = (bf16[512,768]{1,0:T(8,128)(2,1)S(1)}, bf16[512,768]{1,0:T(8,128)(2,1)}, u32[]{:S(2)}, u32[]{:S(2)}) collective-permute-start(bf16[512,768]{1,0:T(8,128)(2,1)S(1)} %get-tuple-element.117), channel_id=1, source_target_pairs={{0,2},{1,3},{2,0},{3,1},{4,6},{5,7},{6,4},{7,5},{8,10},{9,11},{10,... | collective-permute-start | bytes 2359304 | tf_op jit(solution)/shard_map/ppermute | solution.py:456
  25.5 91.1 %collective-permute-start.2 = (bf16[512,768]{1,0:T(8,128)(2,1)S(1)}, bf16[512,768]{1,0:T(8,128)(2,1)}, u32[]{:S(2)}, u32[]{:S(2)}) collective-permute-start(bf16[512,768]{1,0:T(8,128)(2,1)S(1)} %get-tuple-element.114), channel_id=1, source_target_pairs={{0,3},{1,2},{2,1},{3,0},{4,7},{5,6},{6,5},{7,4},{8,11},{9,10},{10,... | collective-permute-start | bytes 2359304 | tf_op jit(solution)/shard_map/ppermute | solution.py:456
  116.6 0.7 copy-start.2
  117.3 309.4 %reduce-scatter.9.cloned.1.call-start = ((), (), s32[]{:S(2)}) async-start(), calls=%async_computation.6 | async-start | bytes 11943936 | tf_op jit(solution)/shard_map/reduce_scatter | solution.py:825
  123.2 12.9 %copy-start = (bf16[4,512,768]{2,1,0:T(8,128)(2,1)S(1)}, bf16[4,512,768]{2,1,0:T(8,128)(2,1)}, u32[]{:S(2)}) copy-start(bf16[4,512,768]{2,1,0:T(8,128)(2,1)} %param.20) | copy-start | bytes 9437188
  137.6 62.8 %collective-permute-start.3 = (bf16[512,768]{1,0:T(8,128)(2,1)}, bf16[512,768]{1,0:T(8,128)(2,1)S(1)}, u32[]{:S(2)}, u32[]{:S(2)}) collective-permute-start(bf16[512,768]{1,0:T(8,128)(2,1)} %get-tuple-element.113), channel_id=1, source_target_pairs={{0,1},{1,0},{2,3},{3,2},{4,5},{5,4},{6,7},{7,6},{8,9},{9,8},{10,11... | collective-permute-start | bytes 2359304 | tf_op jit(solution)/shard_map/ppermute | solution.py:456
  138.2 62.2 %collective-permute-start.4 = (bf16[512,768]{1,0:T(8,128)(2,1)}, bf16[512,768]{1,0:T(8,128)(2,1)S(1)}, u32[]{:S(2)}, u32[]{:S(2)}) collective-permute-start(bf16[512,768]{1,0:T(8,128)(2,1)} %get-tuple-element.112), channel_id=1, source_target_pairs={{0,2},{1,3},{2,0},{3,1},{4,6},{5,7},{6,4},{7,5},{8,10},{9,11},{10,... | collective-permute-start | bytes 2359304 | tf_op jit(solution)/shard_map/ppermute | solution.py:456
  138.2 62.2 %collective-permute-start.5 = (bf16[512,768]{1,0:T(8,128)(2,1)}, bf16[512,768]{1,0:T(8,128)(2,1)S(1)}, u32[]{:S(2)}, u32[]{:S(2)}) collective-permute-start(bf16[512,768]{1,0:T(8,128)(2,1)} %get-tuple-element.111), channel_id=1, source_target_pairs={{0,3},{1,2},{2,1},{3,0},{4,7},{5,6},{6,5},{7,4},{8,11},{9,10},{10,... | collective-permute-start | bytes 2359304 | tf_op jit(solution)/shard_map/ppermute | solution.py:456
  311.4 144.8 %reduce-scatter.13.cloned.1.call-start = ((), (), s32[]{:S(2)}) async-start(), calls=%async_computation.8 | async-start | bytes 1658880
  313.5 113.2 %collective-permute-start.6 = (bf16[512,768]{1,0:T(8,128)(2,1)S(1)}, bf16[512,768]{1,0:T(8,128)(2,1)}, u32[]{:S(2)}, u32[]{:S(2)}) collective-permute-start(bf16[512,768]{1,0:T(8,128)(2,1)S(1)} %get-tuple-element.108), channel_id=1, source_target_pairs={{0,1},{1,0},{2,3},{3,2},{4,5},{5,4},{6,7},{7,6},{8,9},{9,8},{10,11... | collective-permute-start | bytes 2359304 | tf_op jit(solution)/shard_map/ppermute | solution.py:456
  315.0 111.7 %collective-permute-start.7 = (bf16[512,768]{1,0:T(8,128)(2,1)S(1)}, bf16[512,768]{1,0:T(8,128)(2,1)}, u32[]{:S(2)}, u32[]{:S(2)}) collective-permute-start(bf16[512,768]{1,0:T(8,128)(2,1)S(1)} %get-tuple-element.107), channel_id=1, source_target_pairs={{0,2},{1,3},{2,0},{3,1},{4,6},{5,7},{6,4},{7,5},{8,10},{9,11},{10,... | collective-permute-start | bytes 2359304 | tf_op jit(solution)/shard_map/ppermute | solution.py:456
  315.6 111.1 %collective-permute-start.8 = (bf16[512,768]{1,0:T(8,128)(2,1)S(1)}, bf16[512,768]{1,0:T(8,128)(2,1)}, u32[]{:S(2)}, u32[]{:S(2)}) collective-permute-start(bf16[512,768]{1,0:T(8,128)(2,1)S(1)} %get-tuple-element.106), channel_id=1, source_target_pairs={{0,3},{1,2},{2,1},{3,0},{4,7},{5,6},{6,5},{7,4},{8,11},{9,10},{10,... | collective-permute-start | bytes 2359304 | tf_op jit(solution)/shard_map/ppermute | solution.py:456
  317.1 110.3 %copy-start.7 = (f32[1,3072]{1,0:T(1,128)S(1)}, f32[1,3072]{1,0:T(1,128)}, u32[]{:S(2)}) copy-start(f32[1,3072]{1,0:T(1,128)} %get-tuple-element.88) | copy-start | bytes 36868
  317.1 111.0 %copy-start.6 = (f32[8,768]{1,0:T(8,128)S(1)}, f32[8,768]{1,0:T(8,128)}, u32[]{:S(2)}) copy-start(f32[8,768]{1,0:T(8,128)} %get-tuple-element.87) | copy-start | bytes 73732
  426.8 77.3 %reduce-scatter.11.cloned.1.call-start = ((), (), s32[]{:S(2)}) async-start(), calls=%async_computation.7 | async-start | bytes 4202496 | tf_op jit(solution)/shard_map/reduce_scatter | solution.py:840
  456.2 73.3 %reduce-scatter.15.cloned.1.call-start = ((), (), s32[]{:S(2)}) async-start(), calls=%async_computation.9 | async-start | bytes 583680
  472.0 32.1 %collective-permute-start.9 = (bf16[512,768]{1,0:T(8,128)(2,1)}, bf16[512,768]{1,0:T(8,128)(2,1)}, u32[]{:S(2)}, u32[]{:S(2)}) collective-permute-start(bf16[512,768]{1,0:T(8,128)(2,1)} %get-tuple-element.105), channel_id=1, source_target_pairs={{0,1},{1,0},{2,3},{3,2},{4,5},{5,4},{6,7},{7,6},{8,9},{9,8},{10,11... | collective-permute-start | bytes 2359304 | tf_op jit(solution)/shard_map/ppermute | solution.py:456
  473.5 33.0 %collective-permute-start.10 = (bf16[512,768]{1,0:T(8,128)(2,1)S(1)}, bf16[512,768]{1,0:T(8,128)(2,1)}, u32[]{:S(2)}, u32[]{:S(2)}) collective-permute-start(bf16[512,768]{1,0:T(8,128)(2,1)S(1)} %get-tuple-element.104), channel_id=1, source_target_pairs={{0,2},{1,3},{2,0},{3,1},{4,6},{5,7},{6,4},{7,5},{8,10},{9,11},{10,... | collective-permute-start | bytes 2359304 | tf_op jit(solution)/shard_map/ppermute | solution.py:456
  474.2 35.3 %collective-permute-start.11 = (bf16[512,768]{1,0:T(8,128)(2,1)S(1)}, bf16[512,768]{1,0:T(8,128)(2,1)S(1)}, u32[]{:S(2)}, u32[]{:S(2)}) collective-permute-start(bf16[512,768]{1,0:T(8,128)(2,1)S(1)} %get-tuple-element.103), channel_id=1, source_target_pairs={{0,3},{1,2},{2,1},{3,0},{4,7},{5,6},{6,5},{7,4},{8,11},{9,10},{10,... | collective-permute-start | bytes 2359304 | tf_op jit(solution)/shard_map/ppermute | solution.py:456
  504.1 6.6 %copy-start.1 = (bf16[24,6912]{1,0:T(8,128)(2,1)S(1)}, bf16[24,6912]{1,0:T(8,128)(2,1)}, u32[]{:S(2)}) copy-start(bf16[24,6912]{1,0:T(8,128)(2,1)} %reduce-scatter.13.cloned.1.call-done) | copy-start | bytes 995332
Sparse Core Ops, SparseCore 0:
  20.1 41.7 all-gather.2
  117.5 93.4 all-gather.4
  311.5 109.4 reduce-scatter.8
  426.9 29.2 reduce-scatter.12
  458.4 45.6 reduce-scatter.10
  506.8 22.6 reduce-scatter.14

commit v3 on v2

--- a/solution.py
+++ b/solution.py
@@ -471,6 +471,16 @@
     block = rows.shape[0] // size
     pieces = [rows[step * block : (step + 1) * block] for step in range(size)]
     return pieces[:1] + [swap(pieces[step], step) for step in range(1, size)]
+
+
+def scattered(rows):
+    me = lax.axis_index("seq")
+    size = lax.axis_size("seq")
+    parts = rows.reshape(size, rows.shape[0] // size, rows.shape[1])
+    total = take(parts, me).astype(jnp.float32)
+    for step in range(1, size):
+        total = total + swap(take(parts, me ^ step), step).astype(jnp.float32)
+    return total
 
 
 def placed(pieces, dtype):
@@ -779,10 +789,9 @@
     times = wide // width
 
     vectors = [b_query, b_value, b_out, gain_one, shift_one, b_down, gain_two, shift_two, b_up]
-    vec = jnp.concatenate(vectors)
-    known = vec.shape[0]
-    vec = jnp.pad(vec, (0, 1024 - known)).reshape(8, 128)
-    first = jnp.concatenate([w_query, w_key, w_value], 1)
+    vec = jnp.concatenate(vectors).reshape(8 + times, rows)
+    vec = contract(vec, jnp.eye(8 + times, 128, dtype=jnp.bfloat16), 0, 0).astype(jnp.bfloat16)
+    first = jnp.concatenate([w_query, w_key, w_value, vec], 1)
     first = lax.all_gather(first, "seq", axis=0, tiled=True)
     first = lax.all_gather(first, "dp", axis=0, tiled=True)
     owners = width // rows
@@ -791,8 +800,6 @@
     second = jnp.concatenate([mixed_up] + downs + [w_out], 1)
 
     pieces = to_own(tokens)
-    vec = lax.all_gather(vec, axes, axis=0, tiled=True)
-    vec, pieces = lax.optimization_barrier((vec, pieces))
     second, first, pieces = lax.optimization_barrier((second, first, pieces))
     second = lax.all_gather(second, axes, axis=0, tiled=True)
     length = take(lengths, me)
@@ -803,9 +810,7 @@
     bias = jnp.pad(bias[None, :], ((0, PAD - 1), (0, 0)))
     live = live[:, None].astype(jnp.float32)
 
-    vec = vec.reshape(owners, 1024)[:, :known]
-    vec = vec.astype(jnp.float32).reshape(owners, 8 + times, rows).transpose(1, 0, 2)
-    vec = vec.reshape(8 + times, width)
+    vec = first[:, 3 * width :].T[: 8 + times].astype(jnp.float32)
     bu = vec[8:].reshape(1, wide)
     vec = vec[:8]
 
@@ -826,20 +831,20 @@
     output = to_split(result)
     grads = unmix(probs, qt, kt, vt, by_head(gt), mt, total, scale)
     grads, output, late = lax.optimization_barrier((grads, output, late))
-    late = lax.psum_scatter(late, "seq", scatter_dimension=0, tiled=True)
     output = placed(output, jnp.bfloat16)
     grads = grads.reshape(3 * width, slots)
     edges = jnp.concatenate(
         [jnp.zeros((2, width), jnp.float32), sums[:6], up_sums.reshape(times, width)], 0
     )
+    late = scattered(late)
     early = input_weights(x, grads, edges, width // 2)
-    grads, early = lax.optimization_barrier((grads, early))
+    early, late, grads = lax.optimization_barrier((early, late, grads))
+    early = lax.psum_scatter(early, "dp", scatter_dimension=0, tiled=True)
     low = inputs(grads, first, grad_one, block)
-    grad_tokens = placed(to_split(low), jnp.float32)
-    early, late = lax.optimization_barrier((early, late))
-    early = lax.psum_scatter(early, "dp", scatter_dimension=0, tiled=True)
-    early = lax.psum_scatter(early, "seq", scatter_dimension=0, tiled=True).astype(jnp.float32)
-    late = late.astype(jnp.float32)
+    grad_tokens = to_split(low)
+    early, grad_tokens = lax.optimization_barrier((early, grad_tokens))
+    early = scattered(early)
+    grad_tokens = placed(grad_tokens, jnp.float32)
     o_wq, o_wk, o_wv = (early[:, i * width : (i + 1) * width] for i in range(3))
     vec = early[:, 3 * width :]
     o_wu = late[:, :wide].reshape(rows, times, owners, rows).transpose(0, 2, 1, 3).reshape(rows, wide)

time: 545 us -> 500 us (0.917)
  blocking collectives: 98.6 us -> 12 us
  waiting for transfers between devices: 47.2 us -> 69.6 us
  local copies, waits for them, and re-layouts: 38.7 us -> 48.7 us
  starting transfers between devices: 14.3 us -> 21.4 us
    all_gather x1 -> x0, blocking collectives: 86.6 us -> none  [whole_body(): vec = lax.all_gather(vec, axes, axis=0, tiled=True)]
    ppermute x12 -> x18, waiting for transfers between devices: 0.58 us -> 51 us  [swap(): return lax.ppermute(piece, 'seq', [(i, i ^ step) for i in range(size)])]
    reduce_scatter x1, waiting for transfers between devices: 14 us -> 0.01 us  [whole_body(): early = lax.psum_scatter(early, 'dp', scatter_dimension=0, tiled=True)]
    unnamed x7 -> x4, waiting for transfers between devices: 12.5 us -> 0.07 us
    optimization_barrier x1 -> x0, waiting for transfers between devices: 11.5 us -> none  [whole_body(): early, late = lax.optimization_barrier((early, late))]
    ppermute x12 -> x18, starting transfers between devices: 14.1 us -> 21.2 us  [swap(): return lax.ppermute(piece, 'seq', [(i, i ^ step) for i in range(size)])]
    concatenate x1, local copies, waits for them, and re-layouts: 0.1 us -> 6.1 us  [whole_body(): vec = jnp.concatenate(vectors).reshape(8 + times, rows)]
  transfers between devices with their start and end apart: 18 -> 22, of which waited for: 5 -> 7; matrix products, arithmetic and copies ran while one was open for 9% -> 11% of each run, Pallas kernels for 39% -> 43%
where the time goes in v3:
time: 500 us; the launch traced here: 495 us
  Pallas kernels  311 us (62%)
  waiting for transfers between devices  69.6 us (14%)
  local copies, waits for them, and re-layouts  48.7 us (10%)
  starting transfers between devices  21.4 us (4%)
  other arithmetic  17.9 us (4%)
  between operations  14.3 us (3%)
  blocking collectives  12 us (2%)
    pallas_call x1, Pallas kernels, unmix(): pl.pallas_call(functools.partial(unmix_kernel, scale), grid=(heads, slots...  110 us
    pallas_call x1, Pallas kernels, feed(): pl.pallas_call(feed_kernel, grid=(slots // rows,), in_specs=[flat, tall,...  71.2 us
    pallas_call x1, Pallas kernels, mix(): pl.pallas_call(functools.partial(mix_kernel, scale, chunk), grid=(heads,)...  59.3 us
    ppermute x18, waiting for transfers between devices, swap(): return lax.ppermute(piece, 'seq', [(i, i ^ step) for i in range(size)])  51 us
    pallas_call x1, Pallas kernels, feed_weights(): pl.pallas_call(feed_weights_kernel, grid=(2 * parts + 1,), in_specs=[pl.B...  29.2 us
    ppermute x18, starting transfers between devices, swap(): return lax.ppermute(piece, 'seq', [(i, i ^ step) for i in range(size)])  21.2 us
    pallas_call x1, Pallas kernels, input_weights(): pl.pallas_call(input_weights_kernel, grid=(depth // size,), in_specs=[pl....  16 us
    all_gather x1, waiting for transfers between devices, whole_body(): second = lax.all_gather(second, axes, axis=0, tiled=True)  13.7 us
  transfers between devices with their start and end apart: 22, of which 7 were waited for; matrix products, arithmetic and copies ran while one was open for 11% of the time, Pallas kernels for 43%

profile of v3, /device:TPU:0, one launch (start us, length us, event | category | flops | bytes accessed | tf_op | source)
XLA Modules:
  0.0 495.3 jit_solution(16974184741937060940)
XLA Ops:
  7.2 6.1 %concatenate.19 = bf16[288]{0:T(512)(128)(2,1)S(1)} concatenate(bf16[24]{0:T(256)(128)(2,1)} %param.22, bf16[24]{0:T(256)(128)(2,1)} %param.25, bf16[24]{0:T(256)(128)(2,1)} %param.27, bf16[24]{0:T(256)(128)(2,1)} %param.28, bf16[24]{0:T(256)(128)(2,1)} %param.29, bf16[24]{0:T(256)(128)(2,1)} %param.33, bf16[24]{0:T(256)(128)(2,1)} %param.34, bf16[24]{0:T(256)(128)(2,1)} %param.35, ...), dimensions={0} | concatenate | bytes 1152 | tf_op jit(solution)/shard_map/concatenate | solution.py:792
  13.6 0.8 pad_maximum_fusion.2
  14.4 12.0 %all_gather.9 = bf16[96,2432]{1,0:T(8,128)(2,1)} all-gather(bf16[24,2432]{1,0:T(8,128)(2,1)S(1)} %pad_maximum_fusion.2), channel_id=1, replica_groups=mesh['dp'=8,'seq'=4] {'seq'}, dimensions={0}, use_global_device_ids=true | all-gather | bytes 583680 | tf_op jit(solution)/shard_map/all_gather | solution.py:795
  26.6 3.2 dynamic-slice_bitcast_fusion.4
  29.8 1.5 collective-permute-start
  31.9 1.5 collective-permute-start.2
  33.4 1.2 reshape.161
  34.8 1.3 reshape.162
  36.1 14.5 %collective-permute-done.refs_1_ = bf16[512,768]{1,0:T(8,128)(2,1)} collective-permute-done((bf16[512,768]{1,0:T(8,128)(2,1)}, bf16[512,768]{1,0:T(8,128)(2,1)}, u32[]{:S(2)}, u32[]{:S(2)}) %collective-permute-start) | collective-permute-done | bytes 786464 | tf_op jit(solution)/shard_map/ppermute | solution.py:456
  50.7 0.9 collective-permute-done.1.refs_2_
  51.6 13.6 %collective-permute-done.2.refs_3_ = bf16[512,768]{1,0:T(8,128)(2,1)} collective-permute-done((bf16[512,768]{1,0:T(8,128)(2,1)S(1)}, bf16[512,768]{1,0:T(8,128)(2,1)}, u32[]{:S(2)}, u32[]{:S(2)}) %collective-permute-start.2) | collective-permute-done | bytes 786464 | tf_op jit(solution)/shard_map/ppermute | solution.py:456
  65.2 4.8 all-gather.3.cloned.1.call-done.refs_4_.weights
  70.7 0.7 fusion.4
  71.4 0.7 convert_bitcast_fusion
  72.2 1.4 copy.49
  74.2 0.9 slice_bitcast_fusion
  75.1 0.7 copy.41.refs_5_.vec
  75.9 12.9 %project.1 = (bf16[2048,768]{1,0:T(8,128)(2,1)}, bf16[768,2048]{1,0:T(8,128)(2,1)}, bf16[768,2048]{1,0:T(8,128)(2,1)}, bf16[768,2048]{1,0:T(8,128)(2,1)}) custom-call(bf16[512,768]{1,0:T(8,128)(2,1)} %get-tuple-element.55.refs_0_, bf16[512,768]{1,0:T(8,128)(2,1)} %collective-permute-done.refs_1_, bf16[512,768]{1,0:T(8,128)(2,1)} %collective-permute-done.1.refs_2_, ...), custom_call_target="tpu_custom_call" | custom-call | flops 11000000512 | tf_op jit(solution)/shard_map/project/pallas_call | solution.py:522
  88.8 1.7 dynamic-slice_bitcast_fusion.3
  90.5 1.5 collective-permute-start.3
  92.0 1.5 collective-permute-start.4
  94.0 59.3 %mix.1 = (bf16[12,64,2048]{2,1,0:T(8,128)(2,1)}, f32[12,1,2048]{2,1,0:T(1,128)}, bf16[12,2048,2048]{2,1,0:T(8,128)(2,1)}) custom-call(s32[1]{0:T(128)} %bitcast.me, bf16[12,64,2048]{2,1,0:T(8,128)(2,1)} %bitcast.102, bf16[12,64,2048]{2,1,0:T(8,128)(2,1)} %bitcast.104, bf16[12,64,2048]{2,1,0:T(8,128)(2,1)} %bitcast.106, bf16[16,2048]{1,0:T(8,128)(2,1)} %pad.4.bias), custom_call_target="tpu_custom_call" | custom-call | flops 57000001536 | tf_op jit(solution)/shard_map/mix/pallas_call | solution.py:360
  154.3 2.9 pad_maximum_fusion.cot
  157.2 13.7 %all-gather.5.cloned.1.call-done.wo.wu.wd = bf16[768,6912]{1,0:T(8,128)(2,1)} async-done(((bf16[24,6912]{1,0:T(8,128)(2,1)}), bf16[768,6912]{1,0:T(8,128)(2,1)}) %all-gather.5.cloned.1.call-update) | async-done | bytes 10616848 | tf_op jit(solution)/shard_map/all_gather | solution.py:804
  170.9 71.2 %feed.1 = (bf16[2048,768]{1,0:T(8,128)(2,1)}, f32[2048,768]{1,0:T(8,128)}, bf16[768,2048]{1,0:T(8,128)(2,1)}, bf16[2048,4608]{1,0:T(8,128)(2,1)}, bf16[2048,4608...) custom-call(bf16[2048,768]{1,0:T(8,128)(2,1)} %get-tuple-element.65.x, bf16[768,2048]{1,0:T(8,128)(2,1)} %bitcast.108, ...), custom_call_target="tpu_custom_call" | custom-call | flops 70000001024 | tf_op jit(solution)/shard_map/feed/pallas_call | solution.py:627
  242.1 29.2 %feed_weights.1 = bf16[768,6912]{1,0:T(8,128)(2,1)} custom-call(bf16[2048,4608]{1,0:T(8,128)(2,1)} %get-tuple-element.70.left, bf16[2048,4608]{1,0:T(8,128)(2,1)} %get-tuple-element.71.right), custom_call_target="tpu_custom_call" | custom-call | flops 25999998976 | tf_op jit(solution)/shard_map/feed_weights/pallas_call | solution.py:673
  271.4 2.0 fusion.6
  273.4 1.5 collective-permute-start.6
  275.6 1.4 collective-permute-start.8
  277.0 109.6 %unmix.1 = bf16[3,12,64,2048]{3,2,1,0:T(8,128)(2,1)} custom-call(bf16[12,2048,2048]{2,1,0:T(8,128)(2,1)} %get-tuple-element.64.probs, bf16[12,64,2048]{2,1,0:T(8,128)(2,1)} %bitcast.103, bf16[12,64,2048]{2,1,0:T(8,128)(2,1)} %bitcast.105, bf16[12,64,2048]{2,1,0:T(8,128)(2,1)} %bitcast.107, bf16[12,64,2048]{2,1,0:T(8,128)(2,1)} %bitcast.109, ...), custom_call_target="tpu_custom_call" | custom-call | flops 109999996928 | tf_op jit(solution)/shard_map/unmix/pallas_call | solution.py:429
  387.8 0.7 pad_maximum_fusion.3.rows
  388.5 1.2 dynamic-slice_bitcast_fusion.10
  389.8 1.1 collective-permute-start.10
  390.9 1.9 collective-permute-start.11
  393.3 16.0 %input_weights.1 = bf16[768,2432]{1,0:T(8,128)(2,1)} custom-call(bf16[2048,768]{1,0:T(8,128)(2,1)} %get-tuple-element.65.x, bf16[2304,2048]{1,0:T(8,128)(2,1)} %bitcast.100, f32[12,768]{1,0:T(8,128)} %pad_maximum_fusion.3.rows), custom_call_target="tpu_custom_call" | custom-call | flops 12000000000 | tf_op jit(solution)/shard_map/input_weights/pallas_call | solution.py:744
  409.4 1.2 fusion.1
  410.6 1.9 broadcast_in_dim.59
  412.4 0.9 bitcast_dynamic-update-slice_fusion.3
  413.4 2.1 bitcast_dynamic-update-slice_fusion.2
  415.4 13.1 %inputs.1 = bf16[2048,768]{1,0:T(8,128)(2,1)} custom-call(bf16[2304,2048]{1,0:T(8,128)(2,1)} %bitcast.101, bf16[768,2432]{1,0:T(8,128)(2,1)} %all-gather.3.cloned.1.call-done.refs_4_.weights, f32[2048,768]{1,0:T(8,128)} %get-tuple-element.86.grad_one), custom_call_target="tpu_custom_call" | custom-call | flops 12000000000 | tf_op jit(solution)/shard_map/inputs/pallas_call | solution.py:698
  428.5 3.6 fusion.5
  432.1 1.7 collective-permute-start.12
  433.8 1.0 collective-permute-start.13
  434.8 0.8 collective-permute-start.14
  435.6 2.1 bitcast_dynamic-update-slice_fusion.1
  437.7 2.1 bitcast_dynamic-update-slice_fusion
  439.8 1.1 reshape.174
  440.9 1.2 copy.45
  442.2 2.6 reshape.175
  444.7 1.7 fusion.7
  446.4 0.7 pad_maximum_fusion.1
  447.1 5.8 %collective-permute-done.12 = bf16[512,768]{1,0:T(8,128)(2,1)} collective-permute-done((bf16[512,768]{1,0:T(8,128)(2,1)}, bf16[512,768]{1,0:T(8,128)(2,1)}, u32[]{:S(2)}, u32[]{:S(2)}) %collective-permute-start.12) | collective-permute-done | bytes 786464 | tf_op jit(solution)/shard_map/ppermute | solution.py:456
  452.9 16.1 %collective-permute-done.13 = bf16[512,768]{1,0:T(8,128)(2,1)} collective-permute-done((bf16[512,768]{1,0:T(8,128)(2,1)}, bf16[512,768]{1,0:T(8,128)(2,1)}, u32[]{:S(2)}, u32[]{:S(2)}) %collective-permute-start.13) | collective-permute-done | bytes 786464 | tf_op jit(solution)/shard_map/ppermute | solution.py:456
  469.0 1.0 dynamic-slice_bitcast_fusion.13
  470.1 0.9 collective-permute-start.15
  471.0 0.9 collective-permute-start.16
  471.9 1.8 collective-permute-start.17
  473.6 3.2 broadcast_in_dim.66
  476.9 1.3 convert_dynamic-update-slice_fusion.3
  478.1 2.4 convert_dynamic-update-slice_fusion.2
  480.5 2.4 convert_dynamic-update-slice_fusion.1
  482.9 2.4 convert_dynamic-update-slice_fusion
  485.3 1.0 fusion.3
  487.0 0.8 slice_reduce_fusion
  (77 shorter events, 8.0 us)
Async XLA Ops:
  7.2 62.8 %all-gather.3.cloned.1.call-start = ((), (), s32[]{:S(2)}) async-start(), calls=%async_computation.2 | async-start | bytes 4202496 | tf_op jit(solution)/shard_map/all_gather | solution.py:796
  26.5 144.4 %all-gather.5.cloned.1.call-start = ((), (), s32[]{:S(2)}) async-start(), calls=%async_computation.3 | async-start | bytes 10948608 | tf_op jit(solution)/shard_map/all_gather | solution.py:804
  26.5 6.8 %copy-start.5 = (bf16[24,3072]{1,0:T(8,128)(2,1)S(1)}, bf16[24,3072]{1,0:T(8,128)(2,1)}, u32[]{:S(2)}) copy-start(bf16[24,3072]{1,0:T(8,128)(2,1)} %param.30) | copy-start | bytes 442372
  29.8 6.2 %copy-start.6 = (bf16[96,768]{1,0:T(8,128)(2,1)S(1)}, bf16[96,768]{1,0:T(8,128)(2,1)}, u32[]{:S(2)}) copy-start(bf16[96,768]{1,0:T(8,128)(2,1)} %param.32) | copy-start | bytes 442372
  29.8 6.3 %copy-start.7 = (bf16[24,768]{1,0:T(8,128)(2,1)S(1)}, bf16[24,768]{1,0:T(8,128)(2,1)}, u32[]{:S(2)}) copy-start(bf16[24,768]{1,0:T(8,128)(2,1)} %param.26) | copy-start | bytes 110596
  29.8 40.3 %copy-start.10 = (s32[4]{0:T(128)S(1)}, s32[4]{0:T(128)}, u32[]{:S(2)}) copy-start(s32[4]{0:T(128)} %param.19) | copy-start | bytes 52
  29.8 20.9 %collective-permute-start = (bf16[512,768]{1,0:T(8,128)(2,1)}, bf16[512,768]{1,0:T(8,128)(2,1)}, u32[]{:S(2)}, u32[]{:S(2)}) collective-permute-start(bf16[512,768]{1,0:T(8,128)(2,1)} %get-tuple-element.114), channel_id=1, source_target_pairs={{0,1},{1,0},{2,3},{3,2},{4,5},{5,4},{6,7},{7,6},{8,9},{9,8},{10,11... | collective-permute-start | bytes 2359304 | tf_op jit(solution)/shard_map/ppermute | solution.py:456
  31.3 20.3 %collective-permute-start.1 = (bf16[512,768]{1,0:T(8,128)(2,1)S(1)}, bf16[512,768]{1,0:T(8,128)(2,1)}, u32[]{:S(2)}, u32[]{:S(2)}) collective-permute-start(bf16[512,768]{1,0:T(8,128)(2,1)S(1)} %get-tuple-element.116), channel_id=1, source_target_pairs={{0,2},{1,3},{2,0},{3,1},{4,6},{5,7},{6,4},{7,5},{8,10},{9,11},{10,... | collective-permute-start | bytes 2359304 | tf_op jit(solution)/shard_map/ppermute | solution.py:456
  31.9 33.3 %collective-permute-start.2 = (bf16[512,768]{1,0:T(8,128)(2,1)S(1)}, bf16[512,768]{1,0:T(8,128)(2,1)}, u32[]{:S(2)}, u32[]{:S(2)}) collective-permute-start(bf16[512,768]{1,0:T(8,128)(2,1)S(1)} %get-tuple-element.113), channel_id=1, source_target_pairs={{0,3},{1,2},{2,1},{3,0},{4,7},{5,6},{6,5},{7,4},{8,11},{9,10},{10,... | collective-permute-start | bytes 2359304 | tf_op jit(solution)/shard_map/ppermute | solution.py:456
  36.1 33.9 %copy-start.4 = (bf16[24,6912]{1,0:T(8,128)(2,1)}, bf16[24,6912]{1,0:T(8,128)(2,1)S(1)}, u32[]{:S(2)}) copy-start(bf16[24,6912]{1,0:T(8,128)(2,1)S(1)} %constant_dynamic-update-slice_fusion) | copy-start | bytes 995332
  70.0 318.5 %reduce-scatter.3.cloned.1.call-start = ((), (), s32[]{:S(2)}) async-start(), calls=%async_computation.4 | async-start | bytes 11943936 | tf_op jit(solution)/shard_map/reduce_scatter | solution.py:830
  75.9 12.9 %copy-start.1 = (bf16[4,512,768]{2,1,0:T(8,128)(2,1)S(1)}, bf16[4,512,768]{2,1,0:T(8,128)(2,1)}, u32[]{:S(2)}) copy-start(bf16[4,512,768]{2,1,0:T(8,128)(2,1)} %param.20) | copy-start | bytes 9437188
  90.5 63.8 %collective-permute-start.3 = (bf16[512,768]{1,0:T(8,128)(2,1)}, bf16[512,768]{1,0:T(8,128)(2,1)S(1)}, u32[]{:S(2)}, u32[]{:S(2)}) collective-permute-start(bf16[512,768]{1,0:T(8,128)(2,1)} %get-tuple-element.112), channel_id=1, source_target_pairs={{0,1},{1,0},{2,3},{3,2},{4,5},{5,4},{6,7},{7,6},{8,9},{9,8},{10,11... | collective-permute-start | bytes 2359304 | tf_op jit(solution)/shard_map/ppermute | solution.py:456
  92.0 62.3 %collective-permute-start.4 = (bf16[512,768]{1,0:T(8,128)(2,1)}, bf16[512,768]{1,0:T(8,128)(2,1)S(1)}, u32[]{:S(2)}, u32[]{:S(2)}) collective-permute-start(bf16[512,768]{1,0:T(8,128)(2,1)} %get-tuple-element.111), channel_id=1, source_target_pairs={{0,2},{1,3},{2,0},{3,1},{4,6},{5,7},{6,4},{7,5},{8,10},{9,11},{10,... | collective-permute-start | bytes 2359304 | tf_op jit(solution)/shard_map/ppermute | solution.py:456
  93.4 60.8 %collective-permute-start.5 = (bf16[512,768]{1,0:T(8,128)(2,1)}, bf16[512,768]{1,0:T(8,128)(2,1)}, u32[]{:S(2)}, u32[]{:S(2)}) collective-permute-start(bf16[512,768]{1,0:T(8,128)(2,1)} %get-tuple-element.110), channel_id=1, source_target_pairs={{0,3},{1,2},{2,1},{3,0},{4,7},{5,6},{6,5},{7,4},{8,11},{9,10},{10,... | collective-permute-start | bytes 2359304 | tf_op jit(solution)/shard_map/ppermute | solution.py:456
  94.0 60.3 %copy-start.2 = (bf16[512,768]{1,0:T(8,128)(2,1)S(1)}, bf16[512,768]{1,0:T(8,128)(2,1)}, u32[]{:S(2)}) copy-start(bf16[512,768]{1,0:T(8,128)(2,1)} %get-tuple-element.109) | copy-start | bytes 2359300
  271.3 197.7 %reduce-scatter.5.cloned.1.call-start = ((), (), s32[]{:S(2)}) async-start(), calls=%async_computation.5 | async-start | bytes 4202496 | tf_op jit(solution)/shard_map/reduce_scatter | solution.py:842
  273.4 115.1 %collective-permute-start.6 = (bf16[512,768]{1,0:T(8,128)(2,1)S(1)}, bf16[512,768]{1,0:T(8,128)(2,1)}, u32[]{:S(2)}, u32[]{:S(2)}) collective-permute-start(bf16[512,768]{1,0:T(8,128)(2,1)S(1)} %get-tuple-element.107), channel_id=1, source_target_pairs={{0,1},{1,0},{2,3},{3,2},{4,5},{5,4},{6,7},{7,6},{8,9},{9,8},{10,11... | collective-permute-start | bytes 2359304 | tf_op jit(solution)/shard_map/ppermute | solution.py:456
  275.0 113.5 %collective-permute-start.7 = (bf16[512,768]{1,0:T(8,128)(2,1)S(1)}, bf16[512,768]{1,0:T(8,128)(2,1)}, u32[]{:S(2)}, u32[]{:S(2)}) collective-permute-start(bf16[512,768]{1,0:T(8,128)(2,1)S(1)} %get-tuple-element.106), channel_id=1, source_target_pairs={{0,2},{1,3},{2,0},{3,1},{4,6},{5,7},{6,4},{7,5},{8,10},{9,11},{10,... | collective-permute-start | bytes 2359304 | tf_op jit(solution)/shard_map/ppermute | solution.py:456
  275.6 112.9 %collective-permute-start.8 = (bf16[512,768]{1,0:T(8,128)(2,1)S(1)}, bf16[512,768]{1,0:T(8,128)(2,1)}, u32[]{:S(2)}, u32[]{:S(2)}) collective-permute-start(bf16[512,768]{1,0:T(8,128)(2,1)S(1)} %get-tuple-element.105), channel_id=1, source_target_pairs={{0,3},{1,2},{2,1},{3,0},{4,7},{5,6},{6,5},{7,4},{8,11},{9,10},{10,... | collective-permute-start | bytes 2359304 | tf_op jit(solution)/shard_map/ppermute | solution.py:456
  277.0 110.1 %copy-start.9 = (f32[1,3072]{1,0:T(1,128)S(1)}, f32[1,3072]{1,0:T(1,128)}, u32[]{:S(2)}) copy-start(f32[1,3072]{1,0:T(1,128)} %get-tuple-element.82) | copy-start | bytes 36868
  277.0 110.8 %copy-start.8 = (f32[8,768]{1,0:T(8,128)S(1)}, f32[8,768]{1,0:T(8,128)}, u32[]{:S(2)}) copy-start(f32[8,768]{1,0:T(8,128)} %get-tuple-element.81) | copy-start | bytes 73732
  389.8 19.6 %collective-permute-start.10 = (bf16[24,6912]{1,0:T(8,128)(2,1)S(1)}, bf16[24,6912]{1,0:T(8,128)(2,1)S(1)}, u32[]{:S(2)}, u32[]{:S(2)}) collective-permute-start(bf16[24,6912]{1,0:T(8,128)(2,1)S(1)} %get-tuple-element.119), channel_id=1, source_target_pairs={{0,2},{1,3},{2,0},{3,1},{4,6},{5,7},{6,4},{7,5},{8,10},{9,11},{10,... | collective-permute-start | bytes 995336 | tf_op jit(solution)/shard_map/ppermute | solution.py:456
  390.9 18.5 %collective-permute-start.11 = (bf16[24,6912]{1,0:T(8,128)(2,1)S(1)}, bf16[24,6912]{1,0:T(8,128)(2,1)S(1)}, u32[]{:S(2)}, u32[]{:S(2)}) collective-permute-start(bf16[24,6912]{1,0:T(8,128)(2,1)S(1)} %get-tuple-element.118), channel_id=1, source_target_pairs={{0,3},{1,2},{2,1},{3,0},{4,7},{5,6},{6,5},{7,4},{8,11},{9,10},{10,... | collective-permute-start | bytes 995336 | tf_op jit(solution)/shard_map/ppermute | solution.py:456
  392.8 16.5 %collective-permute-start.9 = (bf16[24,6912]{1,0:T(8,128)(2,1)S(1)}, bf16[24,6912]{1,0:T(8,128)(2,1)S(1)}, u32[]{:S(2)}, u32[]{:S(2)}) collective-permute-start(bf16[24,6912]{1,0:T(8,128)(2,1)S(1)} %get-tuple-element.117), channel_id=1, source_target_pairs={{0,1},{1,0},{2,3},{3,2},{4,5},{5,4},{6,7},{7,6},{8,9},{9,8},{10,11... | collective-permute-start | bytes 995336 | tf_op jit(solution)/shard_map/ppermute | solution.py:456
  410.5 29.2 %copy-start.3 = (f32[24,6912]{1,0:T(8,128)}, f32[24,6912]{1,0:T(8,128)S(1)}, u32[]{:S(2)}) copy-start(f32[24,6912]{1,0:T(8,128)S(1)} %fusion.1) | copy-start | bytes 1990660
  432.1 20.8 %collective-permute-start.12 = (bf16[512,768]{1,0:T(8,128)(2,1)}, bf16[512,768]{1,0:T(8,128)(2,1)}, u32[]{:S(2)}, u32[]{:S(2)}) collective-permute-start(bf16[512,768]{1,0:T(8,128)(2,1)} %get-tuple-element.103), channel_id=1, source_target_pairs={{0,1},{1,0},{2,3},{3,2},{4,5},{5,4},{6,7},{7,6},{8,9},{9,8},{10,11... | collective-permute-start | bytes 2359304 | tf_op jit(solution)/shard_map/ppermute | solution.py:456
  433.8 35.3 %collective-permute-start.13 = (bf16[512,768]{1,0:T(8,128)(2,1)}, bf16[512,768]{1,0:T(8,128)(2,1)}, u32[]{:S(2)}, u32[]{:S(2)}) collective-permute-start(bf16[512,768]{1,0:T(8,128)(2,1)} %get-tuple-element.102), channel_id=1, source_target_pairs={{0,2},{1,3},{2,0},{3,1},{4,6},{5,7},{6,4},{7,5},{8,10},{9,11},{10,... | collective-permute-start | bytes 2359304 | tf_op jit(solution)/shard_map/ppermute | solution.py:456
  434.8 34.3 %collective-permute-start.14 = (bf16[512,768]{1,0:T(8,128)(2,1)}, bf16[512,768]{1,0:T(8,128)(2,1)}, u32[]{:S(2)}, u32[]{:S(2)}) collective-permute-start(bf16[512,768]{1,0:T(8,128)(2,1)} %get-tuple-element.101), channel_id=1, source_target_pairs={{0,3},{1,2},{2,1},{3,0},{4,7},{5,6},{6,5},{7,4},{8,11},{9,10},{10,... | collective-permute-start | bytes 2359304 | tf_op jit(solution)/shard_map/ppermute | solution.py:456
  470.1 15.2 %collective-permute-start.15 = (bf16[24,2432]{1,0:T(8,128)(2,1)S(1)}, bf16[24,2432]{1,0:T(8,128)(2,1)S(1)}, u32[]{:S(2)}, u32[]{:S(2)}) collective-permute-start(bf16[24,2432]{1,0:T(8,128)(2,1)S(1)} %get-tuple-element.125), channel_id=1, source_target_pairs={{0,1},{1,0},{2,3},{3,2},{4,5},{5,4},{6,7},{7,6},{8,9},{9,8},{10,11... | collective-permute-start | bytes 350216 | tf_op jit(solution)/shard_map/ppermute | solution.py:456
  471.0 14.3 %collective-permute-start.16 = (bf16[24,2432]{1,0:T(8,128)(2,1)S(1)}, bf16[24,2432]{1,0:T(8,128)(2,1)S(1)}, u32[]{:S(2)}, u32[]{:S(2)}) collective-permute-start(bf16[24,2432]{1,0:T(8,128)(2,1)S(1)} %get-tuple-element.127), channel_id=1, source_target_pairs={{0,2},{1,3},{2,0},{3,1},{4,6},{5,7},{6,4},{7,5},{8,10},{9,11},{10,... | collective-permute-start | bytes 350216 | tf_op jit(solution)/shard_map/ppermute | solution.py:456
  471.9 5.0 %copy-start = (bf16[512,768]{1,0:T(8,128)(2,1)S(1)}, bf16[512,768]{1,0:T(8,128)(2,1)}, u32[]{:S(2)}) copy-start(bf16[512,768]{1,0:T(8,128)(2,1)} %get-tuple-element.87) | copy-start | bytes 2359300
  471.9 13.4 %collective-permute-start.17 = (bf16[24,2432]{1,0:T(8,128)(2,1)S(1)}, bf16[24,2432]{1,0:T(8,128)(2,1)S(1)}, u32[]{:S(2)}, u32[]{:S(2)}) collective-permute-start(bf16[24,2432]{1,0:T(8,128)(2,1)S(1)} %get-tuple-element.126), channel_id=1, source_target_pairs={{0,3},{1,2},{2,1},{3,0},{4,7},{5,6},{6,5},{7,4},{8,11},{9,10},{10,... | collective-permute-start | bytes 350216 | tf_op jit(solution)/shard_map/ppermute | solution.py:456
Sparse Core Ops, SparseCore 0:
  26.6 43.3 all-gather.2
  72.9 97.9 all-gather.4
  271.4 108.9 reduce-scatter.2
  410.7 44.9 reduce-scatter.4

commit v4 on v3

--- a/solution.py
+++ b/solution.py
@@ -306,11 +306,9 @@
     )
 
 
-def mix_kernel(scale, chunk, me, qt, kt, vt, bias, mixed, total, probs, keys, vals):
+def mix_kernel(scale, chunk, qt, kt, vt, bias, mixed, total, probs, keys, vals):
     size, slots = kt.shape[1], kt.shape[2]
-    places = [
-        pl.ds(pl.multiple_of((me[0] ^ b) * chunk, chunk), chunk) for b in range(slots // chunk)
-    ]
+    places = [slice(at, at + chunk) for at in range(0, slots, chunk)]
     key = kt[0]
     keys[...] = jnp.concatenate([key, key, bias[...]], 0).T
     vals[...] = jnp.concatenate([vt[0], jnp.ones((PAD, slots), jnp.bfloat16)], 0)
@@ -354,14 +352,13 @@
         finish(sums)
 
 
-def mix(me, qt, kt, vt, bias, scale, chunk):
+def mix(qt, kt, vt, bias, scale, chunk):
     heads, size, slots = qt.shape
     whole = pl.BlockSpec((1, size, slots), lambda i: (i, 0, 0))
     return pl.pallas_call(
         functools.partial(mix_kernel, scale, chunk),
         grid=(heads,),
         in_specs=[
-            pl.BlockSpec(memory_space=pltpu.SMEM),
             whole,
             whole,
             whole,
@@ -384,7 +381,7 @@
         compiler_params=pltpu.CompilerParams(vmem_limit_bytes=VMEM),
         cost_estimate=cost(57),
         name="mix",
-    )(me, qt, kt, vt, bias)
+    )(qt, kt, vt, bias)
 
 
 def unmix_kernel(scale, probs, qt, kt, vt, gt, mt, total, out, grads, inner, sums):
@@ -451,60 +448,34 @@
     )(probs, qt, kt, vt, gt, mt, total)
 
 
-def swap(piece, step):
-    size = lax.axis_size("seq")
-    return lax.ppermute(piece, "seq", [(i, i ^ step) for i in range(size)])
+def exchange(blocks):
+    return lax.all_to_all(blocks, "seq", 0, 0, tiled=True)
 
 
 def take(array, index):
     return lax.dynamic_index_in_dim(array, index, 0, keepdims=False)
 
 
-def to_own(array):
-    me = lax.axis_index("seq")
-    pieces = [take(array, me)]
-    return pieces + [swap(take(array, me ^ step), step) for step in range(1, lax.axis_size("seq"))]
-
-
-def to_split(rows):
+def columns(*vectors):
+    rows = vectors[0].shape[0]
+    stack = jnp.concatenate(vectors).reshape(-1, rows)
+    unit = jnp.eye(stack.shape[0], 128, dtype=stack.dtype)
+    return contract(stack, unit, 0, 0).astype(stack.dtype)
+
+
+def scattered(rows):
     size = lax.axis_size("seq")
-    block = rows.shape[0] // size
-    pieces = [rows[step * block : (step + 1) * block] for step in range(size)]
-    return pieces[:1] + [swap(pieces[step], step) for step in range(1, size)]
-
-
-def scattered(rows):
-    me = lax.axis_index("seq")
-    size = lax.axis_size("seq")
-    parts = rows.reshape(size, rows.shape[0] // size, rows.shape[1])
-    total = take(parts, me).astype(jnp.float32)
-    for step in range(1, size):
-        total = total + swap(take(parts, me ^ step), step).astype(jnp.float32)
-    return total
-
-
-def placed(pieces, dtype):
-    me = lax.axis_index("seq")
-    result = jnp.zeros((len(pieces),) + pieces[0].shape, dtype)
-    for step, piece in enumerate(pieces):
-        result = lax.dynamic_update_index_in_dim(result, piece.astype(dtype), me ^ step, 0)
-    return result
+    parts = exchange(rows.reshape(size, rows.shape[0] // size, rows.shape[1]))
+    return jnp.sum(parts.astype(jnp.float32), 0)
 
 
 def row_sums(array):
     return jnp.sum(array, 0, keepdims=True)
 
 
-def project_kernel(count, *refs):
-    pieces, (w, vec, x, qt, kt, vt) = refs[:count], refs[count:]
+def project_kernel(x, w, vec, qt, kt, vt):
     width = x.shape[1]
     bias = vec[...]
-    for i, piece in enumerate(pieces):
-
-        @pl.when(pl.program_id(0) == i)
-        def _(piece=piece):
-            x[...] = piece[...]
-
     outs = matmul(x[...], w[...])
     for i, out in enumerate((qt, kt, vt)):
         part = outs[:, i * width : (i + 1) * width]
@@ -513,27 +484,24 @@
         out[...] = part.astype(jnp.bfloat16).T
 
 
-def project(pieces, first, vec):
-    rows, width = pieces[0].shape
-    count = len(pieces)
-    slots = count * rows
+def project(x, first, vec, rows):
+    slots, width = x.shape
     flat = pl.BlockSpec((width, rows), lambda i: (0, i))
     one = pl.Buffered(1)
     return pl.pallas_call(
-        functools.partial(project_kernel, count),
-        grid=(count,),
-        in_specs=[pl.BlockSpec((rows, width), lambda i: (0, 0), pipeline_mode=one)] * count
-        + [
+        project_kernel,
+        grid=(slots // rows,),
+        in_specs=[
+            pl.BlockSpec((rows, width), lambda i: (i, 0)),
             pl.BlockSpec((width, 3 * width), lambda i: (0, 0), pipeline_mode=one),
             pl.BlockSpec(vec.shape, lambda i: (0, 0)),
         ],
-        out_specs=[pl.BlockSpec((rows, width), lambda i: (i, 0))] + [flat] * 3,
-        out_shape=[jax.ShapeDtypeStruct((slots, width), jnp.bfloat16)]
-        + [jax.ShapeDtypeStruct((width, slots), jnp.bfloat16)] * 3,
+        out_specs=[flat] * 3,
+        out_shape=[jax.ShapeDtypeStruct((width, slots), jnp.bfloat16)] * 3,
         compiler_params=pltpu.CompilerParams(vmem_limit_bytes=VMEM),
         cost_estimate=cost(11),
         name="project",
-    )(*pieces, first, vec)
+    )(x, first, vec)
 
 
 def norm(rows):
@@ -555,7 +523,7 @@
     width = x.shape[1]
     wide = wu.shape[1]
     step = pl.program_id(0)
-    bo, g1, s1, bd, g2, s2 = (vec[i : i + 1] for i in range(2, 8))
+    bo, g1, s1, bd, g2, s2 = (vec[i : i + 1] for i in range(6))
     mixed = mt[...].T
     left[:, wide + width :] = mixed
     resid = x[...].astype(jnp.float32) + matmul(mixed, wo[...]) + bo
@@ -788,63 +756,55 @@
     scale = size ** (-0.5)
     times = wide // width
 
-    vectors = [b_query, b_value, b_out, gain_one, shift_one, b_down, gain_two, shift_two, b_up]
-    vec = jnp.concatenate(vectors).reshape(8 + times, rows)
-    vec = contract(vec, jnp.eye(8 + times, 128, dtype=jnp.bfloat16), 0, 0).astype(jnp.bfloat16)
-    first = jnp.concatenate([w_query, w_key, w_value, vec], 1)
+    x = exchange(tokens).reshape(slots, width)
+
+    first = jnp.concatenate([w_query, w_key, w_value, columns(b_query, b_value)], 1)
     first = lax.all_gather(first, "seq", axis=0, tiled=True)
     first = lax.all_gather(first, "dp", axis=0, tiled=True)
     owners = width // rows
     mixed_up = w_up.reshape(rows, owners, times, rows).transpose(0, 2, 1, 3).reshape(rows, wide)
     downs = [w_down[i * rows : (i + 1) * rows] for i in range(times)]
-    second = jnp.concatenate([mixed_up] + downs + [w_out], 1)
-
-    pieces = to_own(tokens)
-    second, first, pieces = lax.optimization_barrier((second, first, pieces))
+    vectors = columns(b_out, gain_one, shift_one, b_down, gain_two, shift_two, b_up)
+    second = jnp.concatenate([mixed_up] + downs + [w_out, vectors], 1)
+
+    second, first, x = lax.optimization_barrier((second, first, x))
     second = lax.all_gather(second, axes, axis=0, tiled=True)
     length = take(lengths, me)
-    order = me ^ jnp.arange(count, dtype=jnp.int32)
-    place = (order[:, None] * block + jnp.arange(block, dtype=jnp.int32)[None, :]).reshape(slots)
-    live = place < length
+    live = jnp.arange(slots, dtype=jnp.int32) < length
     bias = jnp.where(live, 0.0, -1e30).astype(jnp.bfloat16)
     bias = jnp.pad(bias[None, :], ((0, PAD - 1), (0, 0)))
     live = live[:, None].astype(jnp.float32)
 
-    vec = first[:, 3 * width :].T[: 8 + times].astype(jnp.float32)
-    bu = vec[8:].reshape(1, wide)
-    vec = vec[:8]
-
     def by_head(array):
         return array.reshape(heads, size, slots)
 
-    x, qt, kt, vt = project(pieces, first, vec)
+    qt, kt, vt = project(x, first, first[:, 3 * width :].T[:8].astype(jnp.float32), block)
     qt, cotangent = lax.optimization_barrier((qt, cotangent))
-    cot = jnp.concatenate(to_own(cotangent), 0)
+    cot = exchange(cotangent).reshape(slots, width)
     qt, kt, vt = (by_head(a) for a in (qt, kt, vt))
-    mt, total, probs = mix(me.reshape(1), qt, kt, vt, bias, scale * LOG2E, block)
+    mt, total, probs = mix(qt, kt, vt, bias, scale * LOG2E, block)
+    vec = second[:, 2 * wide + width :].T[: 6 + times].astype(jnp.float32)
+    bu = vec[6:].reshape(1, wide)
     result, grad_one, gt, left, right, sums, up_sums = feed(
-        x, mt.reshape(width, slots), cot, live, vec, bu, second, block
+        x, mt.reshape(width, slots), cot, live, vec[:6], bu, second, block
     )
     late = feed_weights(left, right, width)
     gt, late = lax.optimization_barrier((gt, late))
     late = lax.psum_scatter(late, "dp", scatter_dimension=0, tiled=True)
-    output = to_split(result)
+    output = exchange(result.reshape(count, block, width))
     grads = unmix(probs, qt, kt, vt, by_head(gt), mt, total, scale)
     grads, output, late = lax.optimization_barrier((grads, output, late))
-    output = placed(output, jnp.bfloat16)
     grads = grads.reshape(3 * width, slots)
     edges = jnp.concatenate(
         [jnp.zeros((2, width), jnp.float32), sums[:6], up_sums.reshape(times, width)], 0
     )
     late = scattered(late)
-    early = input_weights(x, grads, edges, width // 2)
+    early = input_weights(x, grads, edges, width)
     early, late, grads = lax.optimization_barrier((early, late, grads))
     early = lax.psum_scatter(early, "dp", scatter_dimension=0, tiled=True)
     low = inputs(grads, first, grad_one, block)
-    grad_tokens = to_split(low)
-    early, grad_tokens = lax.optimization_barrier((early, grad_tokens))
+    grad_tokens = exchange(low.reshape(count, block, width)).astype(jnp.float32)
     early = scattered(early)
-    grad_tokens = placed(grad_tokens, jnp.float32)
     o_wq, o_wk, o_wv = (early[:, i * width : (i + 1) * width] for i in range(3))
     vec = early[:, 3 * width :]
     o_wu = late[:, :wide].reshape(rows, times, owners, rows).transpose(0, 2, 1, 3).reshape(rows, wide)

time: 500 us -> 495 us (0.990)
  local copies, waits for them, and re-layouts: 48.7 us -> 36.1 us
  waiting for transfers between devices: 69.6 us -> 81.8 us
  Pallas kernels: 311 us -> 305 us
    all_to_all x0 -> x6, waiting for transfers between devices: none -> 52.8 us  [exchange(): return lax.all_to_all(blocks, 'seq', 0, 0, tiled=True)]
    ppermute x18 -> x0, waiting for transfers between devices: 51 us -> none  [swap(): return lax.ppermute(piece, 'seq', [(i, i ^ step) for i in range(size)])]
    all_to_all x0 -> x6, starting transfers between devices: none -> 24.7 us  [exchange(): return lax.all_to_all(blocks, 'seq', 0, 0, tiled=True)]
    ppermute x18 -> x0, starting transfers between devices: 21.2 us -> none  [swap(): return lax.ppermute(piece, 'seq', [(i, i ^ step) for i in range(size)])]
    all_gather x1, waiting for transfers between devices: 13.7 us -> 23.9 us  [whole_body(): second = lax.all_gather(second, axes, axis=0, tiled=True)]
    dynamic_update_slice x4 -> x0, other arithmetic: 8.4 us -> none  [placed(): lax.dynamic_update_index_in_dim(result, piece.astype(dtype), me ^ step, 0)]
    convert_element_type x1 -> x5, other arithmetic: 0.03 us -> 8.19 us  [the longest x1 5.13 us: whole_body(): grad_tokens = exchange(low.reshape(count, block, width)).astype(jnp.float32)]
    squeeze x4 -> x0, local copies, waits for them, and re-layouts: 7.24 us -> none  [take(): return lax.dynamic_index_in_dim(array, index, 0, keepdims=False)]
  transfers between devices with their start and end apart: 22 -> 10, of which waited for: 7 -> 5; matrix products, arithmetic and copies ran while one was open for 11% -> 8% of each run, Pallas kernels for 43% -> 42%
where the time goes in v4:
time: 495 us; the launch traced here: 490 us
  Pallas kernels  305 us (62%)
  waiting for transfers between devices  81.8 us (17%)
  local copies, waits for them, and re-layouts  36.1 us (7%)
  starting transfers between devices  25 us (5%)
  other arithmetic  15.4 us (3%)
  between operations  14.3 us (3%)
  blocking collectives  12 us (2%)
    pallas_call x1, Pallas kernels, unmix(): pl.pallas_call(functools.partial(unmix_kernel, scale), grid=(heads, slots...  110 us
    pallas_call x1, Pallas kernels, feed(): pl.pallas_call(feed_kernel, grid=(slots // rows,), in_specs=[flat, tall,...  71.2 us
    pallas_call x1, Pallas kernels, mix(): pl.pallas_call(functools.partial(mix_kernel, scale, chunk), grid=(heads,)...  56.3 us
    all_to_all x6, waiting for transfers between devices, exchange(): return lax.all_to_all(blocks, 'seq', 0, 0, tiled=True)  52.8 us
    pallas_call x1, Pallas kernels, feed_weights(): pl.pallas_call(feed_weights_kernel, grid=(2 * parts + 1,), in_specs=[pl.B...  29.3 us
    all_to_all x6, starting transfers between devices, exchange(): return lax.all_to_all(blocks, 'seq', 0, 0, tiled=True)  24.7 us
    all_gather x1, waiting for transfers between devices, whole_body(): second = lax.all_gather(second, axes, axis=0, tiled=True)  23.9 us
    pallas_call x1, Pallas kernels, input_weights(): pl.pallas_call(input_weights_kernel, grid=(depth // size,), in_specs=[pl....  13.4 us
  transfers between devices with their start and end apart: 10, of which 5 were waited for; matrix products, arithmetic and copies ran while one was open for 8% of the time, Pallas kernels for 42%

profile of v4, /device:TPU:0, one launch (start us, length us, event | category | flops | bytes accessed | tf_op | source)
XLA Modules:
  0.0 490.0 jit_solution(11879467512604439320)
XLA Ops:
  7.2 0.7 pad_maximum_fusion.3
  8.0 0.1 reshape.124
  8.1 0.2 convolution_convert_fusion.1
  8.3 0.8 pad_maximum_fusion.1
  9.1 12.0 %all_gather.9 = bf16[96,2432]{1,0:T(8,128)(2,1)} all-gather(bf16[24,2432]{1,0:T(8,128)(2,1)S(1)} %pad_maximum_fusion.1), channel_id=1, replica_groups=mesh['dp'=8,'seq'=4] {'seq'}, dimensions={0}, use_global_device_ids=true | all-gather | bytes 583680 | tf_op jit(solution)/shard_map/all_gather | solution.py:762
  21.1 3.8 all-to-all-start
  25.2 2.1 reshape.121
  27.3 2.2 copy.40
  29.5 2.9 reshape.122
  32.4 0.1 concatenate.18
  32.5 0.1 reshape.123
  32.6 0.9 constant_dynamic-update-slice_fusion.1
  33.6 0.8 slice_dynamic-update-slice_fusion.3
  34.3 0.8 slice_dynamic-update-slice_fusion.2
  35.1 0.8 slice_dynamic-update-slice_fusion.1
  35.9 0.8 slice_dynamic-update-slice_fusion
  36.7 0.2 fusion
  36.8 22.7 %all-to-all-done = bf16[4,512,768]{2,1,0:T(8,128)(2,1)S(1)} async-done(((bf16[4,512,768]{2,1,0:T(8,128)(2,1)}), bf16[4,512,768]{2,1,0:T(8,128)(2,1)S(1)}, u32[]{:S(2)}, u32[]{:S(2)}) %all-to-all-start) | async-done | bytes 3145760 | tf_op jit(solution)/shard_map/all_to_all | solution.py:452
  59.6 5.1 %all-gather.3.cloned.1.call-done.w.weights = bf16[768,2432]{1,0:T(8,128)(2,1)} async-done(((bf16[96,2432]{1,0:T(8,128)(2,1)}), bf16[768,2432]{1,0:T(8,128)(2,1)}) %all-gather.3.cloned.1.call-update) | async-done | bytes 3735568 | tf_op jit(solution)/shard_map/all_gather | solution.py:763
  64.7 0.6 dynamic_slice.4
  65.3 0.7 fusion.2
  66.0 0.6 pad.4.bias
  66.6 1.7 fusion.1.live
  68.3 0.9 slice_bitcast_fusion.1
  69.3 0.1 copy.41
  69.4 0.6 convert_element_type.40.vec
  70.0 11.9 %project.1 = (bf16[768,2048]{1,0:T(8,128)(2,1)}, bf16[768,2048]{1,0:T(8,128)(2,1)}, bf16[768,2048]{1,0:T(8,128)(2,1)}) custom-call(bf16[2048,768]{1,0:T(8,128)(2,1)} %bitcast.33, bf16[768,2432]{1,0:T(8,128)(2,1)} %all-gather.3.cloned.1.call-done.w.weights, f32[8,768]{1,0:T(8,128)} %convert_element_type.40.vec), custom_call_target="tpu_custom_call" | custom-call | flops 11000000512 | tf_op jit(solution)/shard_map/project/pallas_call | solution.py:491
  81.9 3.7 all-to-all-start.1
  85.6 0.2 reduce-scatter.3.cloned.1.call-start
  85.8 56.3 %mix.1 = (bf16[12,64,2048]{2,1,0:T(8,128)(2,1)}, f32[12,1,2048]{2,1,0:T(1,128)}, bf16[12,2048,2048]{2,1,0:T(8,128)(2,1)}) custom-call(bf16[12,64,2048]{2,1,0:T(8,128)(2,1)} %bitcast.48, bf16[12,64,2048]{2,1,0:T(8,128)(2,1)} %bitcast.50, bf16[12,64,2048]{2,1,0:T(8,128)(2,1)} %bitcast.52, bf16[16,2048]{1,0:T(8,128)(2,1)} %pad.4.bias), custom_call_target="tpu_custom_call" | custom-call | flops 57000001536 | tf_op jit(solution)/shard_map/mix/pallas_call | solution.py:358
  142.1 23.9 %all-gather.5.cloned.1.call-done.wo.wu.wd = bf16[768,7040]{1,0:T(8,128)(2,1)} async-done(((bf16[24,7040]{1,0:T(8,128)(2,1)}), bf16[768,7040]{1,0:T(8,128)(2,1)}) %all-gather.5.cloned.1.call-update) | async-done | bytes 10813456 | tf_op jit(solution)/shard_map/all_gather | solution.py:771
  166.0 0.9 slice_bitcast_fusion
  167.0 0.9 slice.130
  167.9 1.1 copy.43
  169.0 0.6 copy.47
  169.6 0.8 copy.46.vec
  170.4 1.6 copy-done.1
  172.0 71.2 %feed.1 = (bf16[2048,768]{1,0:T(8,128)(2,1)}, f32[2048,768]{1,0:T(8,128)}, bf16[768,2048]{1,0:T(8,128)(2,1)}, bf16[2048,4608]{1,0:T(8,128)(2,1)}, bf16[2048,4608...) custom-call(bf16[2048,768]{1,0:T(8,128)(2,1)} %bitcast.34, bf16[768,2048]{1,0:T(8,128)(2,1)} %bitcast.54, ...), custom_call_target="tpu_custom_call" | custom-call | flops 70000001024 | tf_op jit(solution)/shard_map/feed/pallas_call | solution.py:595
  243.2 29.3 %feed_weights.1 = bf16[768,6912]{1,0:T(8,128)(2,1)} custom-call(bf16[2048,4608]{1,0:T(8,128)(2,1)} %get-tuple-element.54.left, bf16[2048,4608]{1,0:T(8,128)(2,1)} %get-tuple-element.55.right), custom_call_target="tpu_custom_call" | custom-call | flops 25999998976 | tf_op jit(solution)/shard_map/feed_weights/pallas_call | solution.py:641
  272.6 3.7 all-to-all-start.2
  276.4 110.1 %unmix.1 = bf16[3,12,64,2048]{3,2,1,0:T(8,128)(2,1)} custom-call(bf16[12,2048,2048]{2,1,0:T(8,128)(2,1)} %get-tuple-element.49.probs, bf16[12,64,2048]{2,1,0:T(8,128)(2,1)} %bitcast.49, bf16[12,64,2048]{2,1,0:T(8,128)(2,1)} %bitcast.51, bf16[12,64,2048]{2,1,0:T(8,128)(2,1)} %bitcast.53, bf16[12,64,2048]{2,1,0:T(8,128)(2,1)} %bitcast.55, ...), custom_call_target="tpu_custom_call" | custom-call | flops 109999996928 | tf_op jit(solution)/shard_map/unmix/pallas_call | solution.py:426
  386.4 0.5 broadcast.43
  386.9 0.7 reduce.19
  387.7 0.7 pad_maximum_fusion.2.rows
  388.4 4.3 all-to-all-start.3
  392.7 13.4 %input_weights.1 = bf16[768,2432]{1,0:T(8,128)(2,1)} custom-call(bf16[2048,768]{1,0:T(8,128)(2,1)} %bitcast.35, bf16[2304,2048]{1,0:T(8,128)(2,1)} %bitcast.46, f32[12,768]{1,0:T(8,128)} %pad_maximum_fusion.2.rows), custom_call_target="tpu_custom_call" | custom-call | flops 12000000000 | tf_op jit(solution)/shard_map/input_weights/pallas_call | solution.py:712
  406.2 4.0 all-to-all-done.3
  410.1 2.4 convert_reduce_fusion
  412.6 12.8 %inputs.1 = bf16[2048,768]{1,0:T(8,128)(2,1)} custom-call(bf16[2304,2048]{1,0:T(8,128)(2,1)} %bitcast.47, bf16[768,2432]{1,0:T(8,128)(2,1)} %all-gather.3.cloned.1.call-done.w.weights, f32[2048,768]{1,0:T(8,128)} %get-tuple-element.66.grad_one), custom_call_target="tpu_custom_call" | custom-call | flops 12000000000 | tf_op jit(solution)/shard_map/inputs/pallas_call | solution.py:666
  425.3 5.0 %all-to-all-start.4 = ((bf16[4,512,768]{2,1,0:T(8,128)(2,1)}), bf16[4,512,768]{2,1,0:T(8,128)(2,1)}, u32[]{:S(2)}, u32[]{:S(2)}) async-start(bf16[4,512,768]{2,1,0:T(8,128)(2,1)} %bitcast.38), calls=%async_computation.5 | async-start | bytes 6291456 | tf_op jit(solution)/shard_map/all_to_all | solution.py:452
  430.3 2.3 reshape.139
  432.6 3.8 copy.44
  436.4 4.0 reshape.140
  440.4 26.1 %all-to-all-done.4 = bf16[4,512,768]{2,1,0:T(8,128)(2,1)} async-done(((bf16[4,512,768]{2,1,0:T(8,128)(2,1)}), bf16[4,512,768]{2,1,0:T(8,128)(2,1)}, u32[]{:S(2)}, u32[]{:S(2)}) %all-to-all-start.4) | async-done | bytes 3145760 | tf_op jit(solution)/shard_map/all_to_all | solution.py:452
  466.5 4.1 all-to-all-start.5
  470.6 1.7 fusion.6
  472.3 0.7 pad_maximum_fusion
  473.1 5.1 %convert_element_type.45 = f32[4,512,768]{2,1,0:T(8,128)} convert(bf16[4,512,768]{2,1,0:T(8,128)(2,1)} %all-to-all-done.4) | non-fusion elementwise | flops 1572864 | bytes 9437184 | tf_op jit(solution)/shard_map/convert_element_type | solution.py:806
  478.2 1.1 convert_reduce_fusion.1
  479.3 0.7 fusion.7
  480.1 0.8 slice_reduce_fusion
  480.9 0.1 copy.45
  481.0 0.6 reshape.141
  481.6 1.7 copy.55
  (49 shorter events, 0.4 us)
Async XLA Ops:
  7.2 57.5 %all-gather.3.cloned.1.call-start = ((), (), s32[]{:S(2)}) async-start(), calls=%async_computation.8 | async-start | bytes 4202496 | tf_op jit(solution)/shard_map/all_gather | solution.py:763
  21.1 4.0 copy-start.3
  21.1 38.5 %all-to-all-start = ((bf16[4,512,768]{2,1,0:T(8,128)(2,1)}), bf16[4,512,768]{2,1,0:T(8,128)(2,1)S(1)}, u32[]{:S(2)}, u32[]{:S(2)}) async-start(bf16[4,512,768]{2,1,0:T(8,128)(2,1)} %param.18), calls=%async_computation | async-start | bytes 6291456 | tf_op jit(solution)/shard_map/all_to_all | solution.py:452
  25.0 7.4 %copy-start.7 = (bf16[24]{0:T(256)(128)(2,1)S(1)}, bf16[24]{0:T(256)(128)(2,1)}, u32[]{:S(2)}) copy-start(bf16[24]{0:T(256)(128)(2,1)} %param.27) | copy-start | bytes 148
  25.0 7.4 %copy-start.8 = (bf16[24]{0:T(256)(128)(2,1)S(1)}, bf16[24]{0:T(256)(128)(2,1)}, u32[]{:S(2)}) copy-start(bf16[24]{0:T(256)(128)(2,1)} %param.28) | copy-start | bytes 148
  25.0 7.4 %copy-start.9 = (bf16[24]{0:T(256)(128)(2,1)S(1)}, bf16[24]{0:T(256)(128)(2,1)}, u32[]{:S(2)}) copy-start(bf16[24]{0:T(256)(128)(2,1)} %param.29) | copy-start | bytes 148
  25.0 7.4 %copy-start.10 = (bf16[24]{0:T(256)(128)(2,1)S(1)}, bf16[24]{0:T(256)(128)(2,1)}, u32[]{:S(2)}) copy-start(bf16[24]{0:T(256)(128)(2,1)} %param.33) | copy-start | bytes 148
  25.0 7.4 %copy-start.11 = (bf16[24]{0:T(256)(128)(2,1)S(1)}, bf16[24]{0:T(256)(128)(2,1)}, u32[]{:S(2)}) copy-start(bf16[24]{0:T(256)(128)(2,1)} %param.34) | copy-start | bytes 148
  25.0 7.4 %copy-start.12 = (bf16[24]{0:T(256)(128)(2,1)S(1)}, bf16[24]{0:T(256)(128)(2,1)}, u32[]{:S(2)}) copy-start(bf16[24]{0:T(256)(128)(2,1)} %param.35) | copy-start | bytes 148
  25.1 7.4 %copy-start.13 = (bf16[96]{0:T(256)(128)(2,1)S(1)}, bf16[96]{0:T(256)(128)(2,1)}, u32[]{:S(2)}) copy-start(bf16[96]{0:T(256)(128)(2,1)} %param.31) | copy-start | bytes 580
  25.1 11.6 %copy-start.4 = (bf16[24,768]{1,0:T(8,128)(2,1)S(1)}, bf16[24,768]{1,0:T(8,128)(2,1)}, u32[]{:S(2)}) copy-start(bf16[24,768]{1,0:T(8,128)(2,1)} %param.26) | copy-start | bytes 110596
  25.1 39.6 %copy-start.14 = (s32[4]{0:T(128)S(1)}, s32[4]{0:T(128)}, u32[]{:S(2)}) copy-start(s32[4]{0:T(128)} %param.19) | copy-start | bytes 52
  25.1 140.9 %all-gather.5.cloned.1.call-start = ((), (), s32[]{:S(2)}) async-start(), calls=%async_computation.9 | async-start | bytes 11151360 | tf_op jit(solution)/shard_map/all_gather | solution.py:771
  36.8 27.8 %copy-start.2 = (bf16[24,7040]{1,0:T(8,128)(2,1)}, bf16[24,7040]{1,0:T(8,128)(2,1)S(1)}, u32[]{:S(2)}) copy-start(bf16[24,7040]{1,0:T(8,128)(2,1)S(1)} %fusion) | copy-start | bytes 1013764
  59.6 10.4 %copy-start = (bf16[4,512,768]{2,1,0:T(8,128)(2,1)}, bf16[4,512,768]{2,1,0:T(8,128)(2,1)S(1)}, u32[]{:S(2)}) copy-start(bf16[4,512,768]{2,1,0:T(8,128)(2,1)S(1)} %all-to-all-done) | copy-start | bytes 9437188
  81.9 88.5 %all-to-all-start.1 = ((bf16[4,512,768]{2,1,0:T(8,128)(2,1)}), bf16[4,512,768]{2,1,0:T(8,128)(2,1)S(1)}, u32[]{:S(2)}, u32[]{:S(2)}) async-start(bf16[4,512,768]{2,1,0:T(8,128)(2,1)} %param.20), calls=%async_computation.1 | async-start | bytes 6291456 | tf_op jit(solution)/shard_map/all_to_all | solution.py:452
  85.6 302.8 %reduce-scatter.3.cloned.1.call-start = ((), (), s32[]{:S(2)}) async-start(), calls=%async_computation.10 | async-start | bytes 11943936 | tf_op jit(solution)/shard_map/reduce_scatter | solution.py:793
  170.4 1.6 copy-start.1
  272.6 115.7 %all-to-all-start.2 = ((bf16[4,512,768]{2,1,0:T(8,128)(2,1)}), bf16[4,512,768]{2,1,0:T(8,128)(2,1)S(1)}, u32[]{:S(2)}, u32[]{:S(2)}) async-start(bf16[4,512,768]{2,1,0:T(8,128)(2,1)} %bitcast.36), calls=%async_computation.2 | async-start | bytes 6291456 | tf_op jit(solution)/shard_map/all_to_all | solution.py:452
  276.3 110.6 %copy-start.6 = (f32[1,3072]{1,0:T(1,128)S(1)}, f32[1,3072]{1,0:T(1,128)}, u32[]{:S(2)}) copy-start(f32[1,3072]{1,0:T(1,128)} %get-tuple-element.63) | copy-start | bytes 36868
  276.3 111.3 %copy-start.5 = (f32[8,768]{1,0:T(8,128)S(1)}, f32[8,768]{1,0:T(8,128)}, u32[]{:S(2)}) copy-start(f32[8,768]{1,0:T(8,128)} %get-tuple-element.62) | copy-start | bytes 73732
  388.4 21.8 %all-to-all-start.3 = ((bf16[4,24,6912]{2,1,0:T(8,128)(2,1)}), bf16[4,24,6912]{2,1,0:T(8,128)(2,1)}, u32[]{:S(2)}, u32[]{:S(2)}) async-start(bf16[4,24,6912]{2,1,0:T(8,128)(2,1)} %bitcast.40), calls=%async_computation.4 | async-start | bytes 2654208 | tf_op jit(solution)/shard_map/all_to_all | solution.py:452
  392.7 73.8 %reduce-scatter.5.cloned.1.call-start = ((), (), s32[]{:S(2)}) async-start(), calls=%async_computation.11 | async-start | bytes 4202496 | tf_op jit(solution)/shard_map/reduce_scatter | solution.py:804
  425.3 5.0 %slice-start = ((f32[24,6912]{1,0:T(8,128)}), f32[24,3072]{1,0:T(8,128)S(1)}, s32[]{:S(2)}) async-start(f32[24,6912]{1,0:T(8,128)} %convert_reduce_fusion), calls=%async_computation.12 | async-start | bytes 589824 | tf_op jit(solution)/shard_map/slice | solution.py:810
  425.3 41.1 %all-to-all-start.4 = ((bf16[4,512,768]{2,1,0:T(8,128)(2,1)}), bf16[4,512,768]{2,1,0:T(8,128)(2,1)}, u32[]{:S(2)}, u32[]{:S(2)}) async-start(bf16[4,512,768]{2,1,0:T(8,128)(2,1)} %bitcast.38), calls=%async_computation.5 | async-start | bytes 6291456 | tf_op jit(solution)/shard_map/all_to_all | solution.py:452
  466.5 11.7 %all-to-all-start.5 = ((bf16[4,24,2432]{2,1,0:T(8,128)(2,1)}), bf16[4,24,2432]{2,1,0:T(8,128)(2,1)}, u32[]{:S(2)}, u32[]{:S(2)}) async-start(bf16[4,24,2432]{2,1,0:T(8,128)(2,1)} %bitcast.42), calls=%async_computation.7 | async-start | bytes 933888 | tf_op jit(solution)/shard_map/all_to_all | solution.py:452
Sparse Core Ops, SparseCore 0:
  21.2 43.3 all-gather.2
  68.2 97.7 all-gather.4
  272.7 108.7 reduce-scatter.2
  412.7 43.3 reduce-scatter.4

commit v5 on v4

--- a/solution.py
+++ b/solution.py
@@ -306,64 +306,44 @@
     )
 
 
-def mix_kernel(scale, chunk, qt, kt, vt, bias, mixed, total, probs, keys, vals):
+def mix_kernel(scale, chunk, qt, kt, vt, bias, mixed, total, probs, queries, vals):
     size, slots = kt.shape[1], kt.shape[2]
-    places = [slice(at, at + chunk) for at in range(0, slots, chunk)]
-    key = kt[0]
-    keys[...] = jnp.concatenate([key, key, bias[...]], 0).T
-    vals[...] = jnp.concatenate([vt[0], jnp.ones((PAD, slots), jnp.bfloat16)], 0)
     query = qt[0].astype(jnp.float32) * scale
     high = query.astype(jnp.bfloat16)
     low = (query - high.astype(jnp.float32)).astype(jnp.bfloat16)
     row = lax.broadcasted_iota(jnp.int32, (PAD, slots), 0)
     first = jnp.where(row == 0, 1.0, 0.0).astype(jnp.bfloat16)
-    columns = jnp.concatenate([high, low, first], 0)
-
-    def finish(sums):
+    queries[...] = jnp.concatenate([high, low, first], 0).T
+    keys = jnp.concatenate([kt[0], kt[0], bias[...]], 0)
+    vals[...] = jnp.concatenate([vt[0], jnp.ones((PAD, slots), jnp.bfloat16)], 0).T
+
+    def block(at, seen):
+        cut = slice(at, at + chunk)
+        scores = matmul(queries[cut], keys)
+        top = jnp.max(scores[:, :seen], 1, keepdims=True)
+        part = jnp.exp2(scores - top).astype(jnp.bfloat16)
+        probs[0, cut] = part
+        sums = matmul(part, vals[...]).T
         weight = sums[size : size + 1]
-        mixed[0] = (sums[:size] / weight).astype(mixed.dtype)
-        total[0] = weight
-        return weight
-
-    sums, top = None, None
-    for at in places:
-        scores = contract(keys[at], columns, 1, 0)
-        if top is None:
-            top = jnp.max(scores[: chunk // 2], 0, keepdims=True)
-        part = jnp.exp2(scores - top).astype(jnp.bfloat16)
-        probs[0, at] = part
-        term = contract(vals[:, at], part, 1, 0)
-        sums = term if sums is None else sums + term
-    weight = finish(sums)
-
-    @pl.when(jnp.logical_not(jnp.max(weight) < 2.0**60))
+        mixed[0, :, cut] = (sums[:size] / weight).astype(mixed.dtype)
+        total[0, :, cut] = weight
+        return jnp.max(weight)
+
+    largest = [block(at, 256) for at in range(0, slots, chunk)]
+
+    @pl.when(jnp.logical_not(functools.reduce(jnp.maximum, largest) < 2.0**60))
     def _():
-        top = jnp.full((1, slots), -jnp.inf, jnp.float32)
-        for at in places:
-            scores = contract(keys[at], columns, 1, 0)
-            top = jnp.maximum(top, jnp.max(scores, 0, keepdims=True))
-        sums = None
-        for at in places:
-            scores = contract(keys[at], columns, 1, 0)
-            part = jnp.exp2(scores - top).astype(jnp.bfloat16)
-            probs[0, at] = part
-            term = contract(vals[:, at], part, 1, 0)
-            sums = term if sums is None else sums + term
-        finish(sums)
-
-
-def mix(qt, kt, vt, bias, scale, chunk):
+        for at in range(0, slots, chunk):
+            block(at, slots)
+
+
+def mix(qt, kt, vt, bias, scale):
     heads, size, slots = qt.shape
     whole = pl.BlockSpec((1, size, slots), lambda i: (i, 0, 0))
     return pl.pallas_call(
-        functools.partial(mix_kernel, scale, chunk),
+        functools.partial(mix_kernel, scale, 512),
         grid=(heads,),
-        in_specs=[
-            whole,
-            whole,
-            whole,
-            pl.BlockSpec((PAD, slots), lambda i: (0, 0)),
-        ],
+        in_specs=[whole, whole, whole, pl.BlockSpec((PAD, slots), lambda i: (0, 0))],
         out_specs=[
             whole,
             pl.BlockSpec((1, 1, slots), lambda i: (i, 0, 0)),
@@ -376,74 +356,50 @@
         ],
         scratch_shapes=[
             pltpu.VMEM((slots, 2 * size + PAD), jnp.bfloat16),
-            pltpu.VMEM((size + PAD, slots), jnp.bfloat16),
+            pltpu.VMEM((slots, size + PAD), jnp.bfloat16),
         ],
         compiler_params=pltpu.CompilerParams(vmem_limit_bytes=VMEM),
-        cost_estimate=cost(57),
+        cost_estimate=cost(65),
         name="mix",
     )(qt, kt, vt, bias)
 
 
-def unmix_kernel(scale, probs, qt, kt, vt, gt, mt, total, out, grads, inner, sums):
-    step, last = pl.program_id(1), pl.num_programs(1) - 1
-    keys = kt.shape[2]
-    here = pl.ds(pl.multiple_of(step * keys, keys), keys)
-
-    @pl.when(step == 0)
-    def _():
-        scaled = (gt[0].astype(jnp.float32) / total[0]).astype(jnp.bfloat16)
-        grads[...] = scaled
-        inner[...] = jnp.sum(
-            scaled.astype(jnp.float32) * mt[0].astype(jnp.float32), 0, keepdims=True
-        )
-
-    grad = grads[...]
-    prob = probs[0]
-    dprob = contract(vt[0], grad, 0, 0)
-    dscore = (prob.astype(jnp.float32) * (dprob - inner[...])).astype(jnp.bfloat16)
-    part = contract(kt[0], dscore, 1, 0)
-    out[2, 0, :, here] = contract(prob, grad, 1, 1).T.astype(jnp.bfloat16)
-    out[1, 0, :, here] = (contract(dscore, qt[0], 1, 1) * scale).T.astype(jnp.bfloat16)
-
-    @pl.when(step == 0)
-    def _():
-        sums[...] = part
-
-    @pl.when(step > 0)
-    def _():
-        sums[...] += part
-
-    @pl.when(step == last)
-    def _():
-        out[0, 0] = (sums[...] * scale).astype(jnp.bfloat16)
+def unmix_kernel(scale, chunk, probs, qt, kt, vt, gt, mt, total, out, keys):
+    slots = kt.shape[2]
+    grad = (gt[0].astype(jnp.float32) / total[0]).astype(jnp.bfloat16)
+    inner = jnp.sum(grad.astype(jnp.float32) * mt[0].astype(jnp.float32), 0, keepdims=True)
+    inner = jnp.broadcast_to(inner, (8, slots)).T[:, :1]
+    turned = grad.T
+    keys[...] = kt[0].T
+    dk = dv = None
+    for at in range(0, slots, chunk):
+        cut = slice(at, at + chunk)
+        prob = probs[0, cut]
+        dprob = matmul(turned[cut], vt[0])
+        dscore = (prob.astype(jnp.float32) * (dprob - inner[cut])).astype(jnp.bfloat16)
+        out[0, 0, :, cut] = (matmul(dscore, keys[...]) * scale).T.astype(jnp.bfloat16)
+        value_term = matmul(grad[:, cut], prob)
+        key_term = matmul(qt[0, :, cut], dscore)
+        dv = value_term if dv is None else dv + value_term
+        dk = key_term if dk is None else dk + key_term
+    out[1, 0] = (dk * scale).astype(jnp.bfloat16)
+    out[2, 0] = dv.astype(jnp.bfloat16)
 
 
 def unmix(probs, qt, kt, vt, gt, mt, total, scale):
     heads, size, slots = qt.shape
-    keys = slots // 2
-    whole = pl.BlockSpec((1, size, slots), lambda i, j: (i, 0, 0))
-    part = pl.BlockSpec((1, size, keys), lambda i, j: (i, 0, j))
+    whole = pl.BlockSpec((1, size, slots), lambda i: (i, 0, 0))
     return pl.pallas_call(
-        functools.partial(unmix_kernel, scale),
-        grid=(heads, slots // keys),
-        in_specs=[
-            pl.BlockSpec((1, keys, slots), lambda i, j: (i, j, 0)),
-            whole,
-            part,
-            part,
-            whole,
-            whole,
-            pl.BlockSpec((1, 1, slots), lambda i, j: (i, 0, 0)),
-        ],
-        out_specs=pl.BlockSpec((3, 1, size, slots), lambda i, j: (0, i, 0, 0)),
+        functools.partial(unmix_kernel, scale, 256),
+        grid=(heads,),
+        in_specs=[pl.BlockSpec((1, slots, slots), lambda i: (i, 0, 0))]
+        + [whole] * 5
+        + [pl.BlockSpec((1, 1, slots), lambda i: (i, 0, 0))],
+        out_specs=pl.BlockSpec((3, 1, size, slots), lambda i: (0, i, 0, 0)),
         out_shape=jax.ShapeDtypeStruct((3, heads, size, slots), jnp.bfloat16),
-        scratch_shapes=[
-            pltpu.VMEM((size, slots), jnp.bfloat16),
-            pltpu.VMEM((1, slots), jnp.float32),
-            pltpu.VMEM((size, slots), jnp.float32),
-        ],
+        scratch_shapes=[pltpu.VMEM((slots, size), jnp.bfloat16)],
         compiler_params=pltpu.CompilerParams(vmem_limit_bytes=VMEM),
-        cost_estimate=cost(110),
+        cost_estimate=cost(95),
         name="unmix",
     )(probs, qt, kt, vt, gt, mt, total)
 
@@ -475,7 +431,7 @@
 
 def project_kernel(x, w, vec, qt, kt, vt):
     width = x.shape[1]
-    bias = vec[...]
+    bias = vec[...].T[:8].astype(jnp.float32)
     outs = matmul(x[...], w[...])
     for i, out in enumerate((qt, kt, vt)):
         part = outs[:, i * width : (i + 1) * width]
@@ -484,7 +440,7 @@
         out[...] = part.astype(jnp.bfloat16).T
 
 
-def project(x, first, vec, rows):
+def project(x, first, rows):
     slots, width = x.shape
     flat = pl.BlockSpec((width, rows), lambda i: (0, i))
     one = pl.Buffered(1)
@@ -494,14 +450,14 @@
         in_specs=[
             pl.BlockSpec((rows, width), lambda i: (i, 0)),
             pl.BlockSpec((width, 3 * width), lambda i: (0, 0), pipeline_mode=one),
-            pl.BlockSpec(vec.shape, lambda i: (0, 0)),
+            pl.BlockSpec((width, 128), lambda i: (0, 3 * width // 128)),
         ],
         out_specs=[flat] * 3,
         out_shape=[jax.ShapeDtypeStruct((width, slots), jnp.bfloat16)] * 3,
         compiler_params=pltpu.CompilerParams(vmem_limit_bytes=VMEM),
         cost_estimate=cost(11),
         name="project",
-    )(x, first, vec)
+    )(x, first, first)
 
 
 def norm(rows):
@@ -517,13 +473,13 @@
 
 
 def feed_kernel(
-    x, mt, cot, live, vec, bu, wo, wu, wd,
-    output, grad_one, gt, left, right, sums, up_sums, slope,
+    x, mt, cot, live, vec, wo, wu, wd, output, grad_one, gt, left, right, sums, slope,
 ):
     width = x.shape[1]
     wide = wu.shape[1]
     step = pl.program_id(0)
-    bo, g1, s1, bd, g2, s2 = (vec[i : i + 1] for i in range(6))
+    known = vec[...].T[:16].astype(jnp.float32)
+    bo, g1, s1, bd, g2, s2 = (known[i : i + 1] for i in range(6))
     mixed = mt[...].T
     left[:, wide + width :] = mixed
     resid = x[...].astype(jnp.float32) + matmul(mixed, wo[...]) + bo
@@ -534,7 +490,7 @@
     resid = normed + bd
     for at in range(0, wide, width):
         cut = slice(at, at + width)
-        hidden = matmul(low, wu[:, cut]) + bu[:, cut]
+        hidden = matmul(low, wu[:, cut]) + known[6 + at // width : 7 + at // width]
         share = 0.5 + 0.5 * lax.erf(hidden * 0.7071067811865476)
         bell = jnp.exp2(hidden * hidden * -0.7213475204444817) * 0.3989422804014327
         slope[:, cut] = (share + hidden * bell).astype(jnp.bfloat16)
@@ -569,23 +525,20 @@
         row_sums(incoming * unit_two),
         row_sums(incoming),
     ]
-    rows = jnp.concatenate(rows + [jnp.zeros((2, width), jnp.float32)], 0)
-    wide_rows = jnp.concatenate(up_rows, 1)
+    blank = [jnp.zeros((2, width), jnp.float32)]
+    rows = jnp.concatenate(blank + rows + up_rows, 0)
 
     @pl.when(step == 0)
     def _():
         sums[...] = rows
-        up_sums[...] = wide_rows
 
     @pl.when(step > 0)
     def _():
         sums[...] += rows
-        up_sums[...] += wide_rows
-
-
-def feed(x, mt, cot, live, vec, bu, second, rows):
+
+
+def feed(x, mt, cot, live, second, wide, rows):
     slots, width = x.shape
-    wide = bu.shape[1]
     one = pl.Buffered(1)
     flat = pl.BlockSpec((rows, width), lambda i: (i, 0))
     tall = pl.BlockSpec((width, rows), lambda i: (0, i))
@@ -600,8 +553,7 @@
             tall,
             flat,
             pl.BlockSpec((rows, 1), lambda i: (i, 0)),
-            pl.BlockSpec(vec.shape, lambda i: (0, 0)),
-            pl.BlockSpec((1, wide), lambda i: (0, 0)),
+            pl.BlockSpec((width, 128), lambda i: (0, (2 * wide + width) // 128)),
             pl.BlockSpec((width, width), lambda i: (0, 2 * wide // width), pipeline_mode=one),
             pl.BlockSpec((width, wide), lambda i: (0, 0), pipeline_mode=one),
             pl.BlockSpec((width, wide), lambda i: (0, 1), pipeline_mode=one),
@@ -612,8 +564,7 @@
             tall,
             broad,
             broad,
-            pl.BlockSpec((8, width), lambda i: (0, 0)),
-            pl.BlockSpec((1, wide), lambda i: (0, 0)),
+            pl.BlockSpec((8 + wide // width, width), lambda i: (0, 0)),
         ],
         out_shape=[
             jax.ShapeDtypeStruct((slots, width), low),
@@ -621,14 +572,13 @@
             jax.ShapeDtypeStruct((width, slots), low),
             jax.ShapeDtypeStruct((slots, stack), low),
             jax.ShapeDtypeStruct((slots, stack), low),
-            jax.ShapeDtypeStruct((8, width), jnp.float32),
-            jax.ShapeDtypeStruct((1, wide), jnp.float32),
+            jax.ShapeDtypeStruct((8 + wide // width, width), jnp.float32),
         ],
         scratch_shapes=[pltpu.VMEM((rows, wide), low)],
         compiler_params=pltpu.CompilerParams(vmem_limit_bytes=VMEM),
         cost_estimate=cost(70),
         name="feed",
-    )(x, mt, cot, live, vec, bu, second, second, second)
+    )(x, mt, cot, live, second, second, second, second)
 
 
 def feed_weights_kernel(left, right, d_w):
@@ -767,44 +717,43 @@
     vectors = columns(b_out, gain_one, shift_one, b_down, gain_two, shift_two, b_up)
     second = jnp.concatenate([mixed_up] + downs + [w_out, vectors], 1)
 
-    second, first, x = lax.optimization_barrier((second, first, x))
-    second = lax.all_gather(second, axes, axis=0, tiled=True)
     length = take(lengths, me)
     live = jnp.arange(slots, dtype=jnp.int32) < length
     bias = jnp.where(live, 0.0, -1e30).astype(jnp.bfloat16)
     bias = jnp.pad(bias[None, :], ((0, PAD - 1), (0, 0)))
     live = live[:, None].astype(jnp.float32)
+    x, live, bias = lax.optimization_barrier((x, live, bias))
+    second, first, x = lax.optimization_barrier((second, first, x))
+    second = lax.all_gather(second, axes, axis=0, tiled=True)
 
     def by_head(array):
         return array.reshape(heads, size, slots)
 
-    qt, kt, vt = project(x, first, first[:, 3 * width :].T[:8].astype(jnp.float32), block)
+    qt, kt, vt = project(x, first, block)
     qt, cotangent = lax.optimization_barrier((qt, cotangent))
     cot = exchange(cotangent).reshape(slots, width)
     qt, kt, vt = (by_head(a) for a in (qt, kt, vt))
-    mt, total, probs = mix(qt, kt, vt, bias, scale * LOG2E, block)
-    vec = second[:, 2 * wide + width :].T[: 6 + times].astype(jnp.float32)
-    bu = vec[6:].reshape(1, wide)
-    result, grad_one, gt, left, right, sums, up_sums = feed(
-        x, mt.reshape(width, slots), cot, live, vec[:6], bu, second, block
+    mt, total, probs = mix(qt, kt, vt, bias, scale * LOG2E)
+    result, grad_one, gt, left, right, sums = feed(
+        x, mt.reshape(width, slots), cot, live, second, wide, block
     )
     late = feed_weights(left, right, width)
     gt, late = lax.optimization_barrier((gt, late))
     late = lax.psum_scatter(late, "dp", scatter_dimension=0, tiled=True)
     output = exchange(result.reshape(count, block, width))
     grads = unmix(probs, qt, kt, vt, by_head(gt), mt, total, scale)
-    grads, output, late = lax.optimization_barrier((grads, output, late))
+    grads, output = lax.optimization_barrier((grads, output))
     grads = grads.reshape(3 * width, slots)
-    edges = jnp.concatenate(
-        [jnp.zeros((2, width), jnp.float32), sums[:6], up_sums.reshape(times, width)], 0
-    )
-    late = scattered(late)
-    early = input_weights(x, grads, edges, width)
+    early = input_weights(x, grads, sums, width)
     early, late, grads = lax.optimization_barrier((early, late, grads))
     early = lax.psum_scatter(early, "dp", scatter_dimension=0, tiled=True)
+    late = scattered(late)
     low = inputs(grads, first, grad_one, block)
-    grad_tokens = exchange(low.reshape(count, block, width)).astype(jnp.float32)
+    low, late = lax.optimization_barrier((low, late))
+    grad_tokens = exchange(low.reshape(count, block, width))
+    early, grad_tokens = lax.optimization_barrier((early, grad_tokens))
     early = scattered(early)
+    grad_tokens = grad_tokens.astype(jnp.float32)
     o_wq, o_wk, o_wv = (early[:, i * width : (i + 1) * width] for i in range(3))
     vec = early[:, 3 * width :]
     o_wu = late[:, :wide].reshape(rows, times, owners, rows).transpose(0, 2, 1, 3).reshape(rows, wide)

time: 495 us -> 472 us (0.954)
  waiting for transfers between devices: 81.8 us -> 73.3 us
  local copies, waits for them, and re-layouts: 36.1 us -> 28.5 us
  Pallas kernels: 305 us -> 299 us
    pallas_call x2, Pallas kernels: 166 us -> 161 us  [the longest x1 95.1 us: unmix(): pl.pallas_call(functools.partial(unmix_kernel, scale, 256), grid=(heads,)...]
    all_gather x1, waiting for transfers between devices: 23.9 us -> 18.8 us  [whole_body(): second = lax.all_gather(second, axes, axis=0, tiled=True)]
  transfers between devices with their start and end apart: 10 -> 10, of which waited for: 5 -> 5; matrix products, arithmetic and copies ran while one was open for 8% -> 8% of each run, Pallas kernels for 42% -> 43%
where the time goes in v5:
time: 472 us; the launch traced here: 466 us
  Pallas kernels  299 us (63%)
  waiting for transfers between devices  73.3 us (16%)
  local copies, waits for them, and re-layouts  28.5 us (6%)
  starting transfers between devices  25.1 us (5%)
  between operations  14.3 us (3%)
  other arithmetic  13.4 us (3%)
  blocking collectives  12 us (3%)
    pallas_call x1, Pallas kernels, unmix(): pl.pallas_call(functools.partial(unmix_kernel, scale, 256), grid=(heads,)...  95.1 us
    pallas_call x1, Pallas kernels, feed(): pl.pallas_call(feed_kernel, grid=(slots // rows,), in_specs=[flat, tall,...  70.8 us
    pallas_call x1, Pallas kernels, mix(): pl.pallas_call(functools.partial(mix_kernel, scale, 512), grid=(heads,),...  65.8 us
    all_to_all x6, waiting for transfers between devices, exchange(): return lax.all_to_all(blocks, 'seq', 0, 0, tiled=True)  49.5 us
    pallas_call x1, Pallas kernels, feed_weights(): pl.pallas_call(feed_weights_kernel, grid=(2 * parts + 1,), in_specs=[pl.B...  29.2 us
    all_to_all x6, starting transfers between devices, exchange(): return lax.all_to_all(blocks, 'seq', 0, 0, tiled=True)  24.7 us
    all_gather x1, waiting for transfers between devices, whole_body(): second = lax.all_gather(second, axes, axis=0, tiled=True)  18.8 us
    pallas_call x1, Pallas kernels, input_weights(): pl.pallas_call(input_weights_kernel, grid=(depth // size,), in_specs=[pl....  13.4 us
  transfers between devices with their start and end apart: 10, of which 5 were waited for; matrix products, arithmetic and copies ran while one was open for 8% of the time, Pallas kernels for 43%

profile of v5, /device:TPU:0, one launch (start us, length us, event | category | flops | bytes accessed | tf_op | source)
XLA Modules:
  0.0 466.4 jit_solution(17670171464797248519)
XLA Ops:
  7.2 0.0 all-gather.3.cloned.1.call-start
  7.2 0.7 pad_maximum_fusion.2
  8.0 0.1 reshape.118
  8.1 0.2 convolution_convert_fusion.1
  8.3 0.8 pad_maximum_fusion.1
  9.1 12.0 %all_gather.9 = bf16[96,2432]{1,0:T(8,128)(2,1)} all-gather(bf16[24,2432]{1,0:T(8,128)(2,1)S(1)} %pad_maximum_fusion.1), channel_id=1, replica_groups=mesh['dp'=8,'seq'=4] {'seq'}, dimensions={0}, use_global_device_ids=true | all-gather | bytes 583680 | tf_op jit(solution)/shard_map/all_gather | solution.py:712
  21.1 0.0 all-gather.3.cloned.1.call-update
  21.1 0.0 copy-start.5
  21.2 0.0 copy-start.8
  21.2 0.0 copy-start.9
  21.2 0.0 copy-start.11
  21.2 3.8 all-to-all-start
  25.1 0.0 all-gather.5.cloned.1.call-start
  25.2 0.1 concatenate.15
  25.3 0.1 reshape.117
  25.4 2.1 reshape.115
  27.6 2.2 copy.38
  29.8 2.8 reshape.116
  32.6 0.6 dynamic_slice.4
  33.2 0.7 fusion.2
  33.9 0.6 pad.4.bias
  34.5 0.9 constant_dynamic-update-slice_fusion.1
  35.5 0.8 slice_dynamic-update-slice_fusion.3
  36.2 0.8 slice_dynamic-update-slice_fusion.2
  37.0 0.8 slice_dynamic-update-slice_fusion.1
  37.8 0.8 slice_dynamic-update-slice_fusion
  38.6 0.2 fusion
  38.7 1.7 fusion.1.live
  40.5 19.2 %all-to-all-done = bf16[4,512,768]{2,1,0:T(8,128)(2,1)S(1)} async-done(((bf16[4,512,768]{2,1,0:T(8,128)(2,1)}), bf16[4,512,768]{2,1,0:T(8,128)(2,1)S(1)}, u32[]{:S(2)}, u32[]{:S(2)}) %all-to-all-start) | async-done | bytes 3145760 | tf_op jit(solution)/shard_map/all_to_all | solution.py:408
  59.7 5.0 %all-gather.3.cloned.1.call-done.w.vec.weights = bf16[768,2432]{1,0:T(8,128)(2,1)} async-done(((bf16[96,2432]{1,0:T(8,128)(2,1)}), bf16[768,2432]{1,0:T(8,128)(2,1)}) %all-gather.3.cloned.1.call-update) | async-done | bytes 3735568 | tf_op jit(solution)/shard_map/all_gather | solution.py:713
  64.7 0.0 all-gather.5.cloned.1.call-update
  64.7 11.9 %project.1 = (bf16[768,2048]{1,0:T(8,128)(2,1)}, bf16[768,2048]{1,0:T(8,128)(2,1)}, bf16[768,2048]{1,0:T(8,128)(2,1)}) custom-call(bf16[2048,768]{1,0:T(8,128)(2,1)} %bitcast.22, bf16[768,2432]{1,0:T(8,128)(2,1)} %all-gather.3.cloned.1.call-done.w.vec.weights, bf16[768,2432]{1,0:T(8,128)(2,1)} %all-gather.3.cloned.1.call-done.w.vec.weights), custom_call_target="tpu_custom_call" | custom-call | flops 11000000512 | tf_op jit(solution)/shard_map/project/pallas_call | solution.py:447
  76.6 3.7 all-to-all-start.1
  80.3 0.3 reduce-scatter.3.cloned.1.call-start
  80.6 65.8 %mix.1 = (bf16[12,64,2048]{2,1,0:T(8,128)(2,1)}, f32[12,1,2048]{2,1,0:T(1,128)}, bf16[12,2048,2048]{2,1,0:T(8,128)(2,1)}) custom-call(bf16[12,64,2048]{2,1,0:T(8,128)(2,1)} %bitcast.33, bf16[12,64,2048]{2,1,0:T(8,128)(2,1)} %bitcast.35, bf16[12,64,2048]{2,1,0:T(8,128)(2,1)} %bitcast.37, bf16[16,2048]{1,0:T(8,128)(2,1)} %pad.4.bias), custom_call_target="tpu_custom_call" | custom-call | flops 65000001536 | tf_op jit(solution)/shard_map/mix/pallas_call | solution.py:343
  146.3 18.8 %all-gather.5.cloned.1.call-done.vec.wo.wu.wd = bf16[768,7040]{1,0:T(8,128)(2,1)} async-done(((bf16[24,7040]{1,0:T(8,128)(2,1)}), bf16[768,7040]{1,0:T(8,128)(2,1)}) %all-gather.5.cloned.1.call-update) | async-done | bytes 10813456 | tf_op jit(solution)/shard_map/all_gather | solution.py:727
  165.1 70.8 %feed.1 = (bf16[2048,768]{1,0:T(8,128)(2,1)}, f32[2048,768]{1,0:T(8,128)}, bf16[768,2048]{1,0:T(8,128)(2,1)}, bf16[2048,4608]{1,0:T(8,128)(2,1)}, bf16[2048,4608]{1,0:T(8,128)(2,1)}, /*index=5*/f32[12,768]{1,0:T(8,128)}) custom-call(bf16[2048,768]{1,0:T(8,128)(2,1)} %bitcast.23, bf16[768,2048]{1,0:T(8,128)(2,1)} %bitcast.39, bf16[2048,768]{1,0:T(8,128)(2,1)} %bitcast.26, ...), custom_call_target="tpu_custom_call" | custom-call | flops 70000001024 | tf_op jit(solution)/shard_map/feed/pallas_call | solution.py:548
  235.9 29.2 %feed_weights.1 = bf16[768,6912]{1,0:T(8,128)(2,1)} custom-call(bf16[2048,4608]{1,0:T(8,128)(2,1)} %get-tuple-element.62.left, bf16[2048,4608]{1,0:T(8,128)(2,1)} %get-tuple-element.63.right), custom_call_target="tpu_custom_call" | custom-call | flops 25999998976 | tf_op jit(solution)/shard_map/feed_weights/pallas_call | solution.py:591
  265.1 0.0 reduce-scatter.3.cloned.1.call-update
  265.1 3.7 all-to-all-start.2
  268.9 0.0 reduce-scatter.5.cloned.1.call-start
  268.9 95.1 %unmix.1 = bf16[3,12,64,2048]{3,2,1,0:T(8,128)(2,1)} custom-call(bf16[12,2048,2048]{2,1,0:T(8,128)(2,1)} %get-tuple-element.56.probs, bf16[12,64,2048]{2,1,0:T(8,128)(2,1)} %bitcast.34, bf16[12,64,2048]{2,1,0:T(8,128)(2,1)} %bitcast.36, bf16[12,64,2048]{2,1,0:T(8,128)(2,1)} %bitcast.38, bf16[12,64,2048]{2,1,0:T(8,128)(2,1)} %bitcast.40, ...), custom_call_target="tpu_custom_call" | custom-call | flops 95000002560 | tf_op jit(solution)/shard_map/unmix/pallas_call | solution.py:392
  364.0 13.4 %input_weights.1 = bf16[768,2432]{1,0:T(8,128)(2,1)} custom-call(bf16[2048,768]{1,0:T(8,128)(2,1)} %bitcast.24, bf16[2304,2048]{1,0:T(8,128)(2,1)} %bitcast.31, f32[12,768]{1,0:T(8,128)} %get-tuple-element.69.rows), custom_call_target="tpu_custom_call" | custom-call | flops 12000000000 | tf_op jit(solution)/shard_map/input_weights/pallas_call | solution.py:662
  377.5 0.0 reduce-scatter.5.cloned.1.call-update
  377.5 4.5 all-to-all-start.3
  382.0 13.2 %inputs.1 = bf16[2048,768]{1,0:T(8,128)(2,1)} custom-call(bf16[2304,2048]{1,0:T(8,128)(2,1)} %bitcast.32, bf16[768,2432]{1,0:T(8,128)(2,1)} %all-gather.3.cloned.1.call-done.w.vec.weights, f32[2048,768]{1,0:T(8,128)} %get-tuple-element.73.grad_one), custom_call_target="tpu_custom_call" | custom-call | flops 12000000000 | tf_op jit(solution)/shard_map/inputs/pallas_call | solution.py:616
  395.2 4.3 all-to-all-done.3
  399.5 2.4 convert_reduce_fusion
  401.9 4.8 %all-to-all-start.4 = ((bf16[4,512,768]{2,1,0:T(8,128)(2,1)}), bf16[4,512,768]{2,1,0:T(8,128)(2,1)}, u32[]{:S(2)}, u32[]{:S(2)}) async-start(bf16[4,512,768]{2,1,0:T(8,128)(2,1)} %bitcast.27), calls=%async_computation.6 | async-start | bytes 6291456 | tf_op jit(solution)/shard_map/all_to_all | solution.py:408
  406.7 2.3 reshape.131
  409.0 3.8 copy.39
  412.8 4.0 reshape.132
  416.8 26.0 %all-to-all-done.4 = bf16[4,512,768]{2,1,0:T(8,128)(2,1)} async-done(((bf16[4,512,768]{2,1,0:T(8,128)(2,1)}), bf16[4,512,768]{2,1,0:T(8,128)(2,1)}, u32[]{:S(2)}, u32[]{:S(2)}) %all-to-all-start.4) | async-done | bytes 3145760 | tf_op jit(solution)/shard_map/all_to_all | solution.py:408
  442.9 4.1 all-to-all-start.5
  447.0 1.7 fusion.6
  448.7 0.7 pad_maximum_fusion
  449.4 5.1 %convert_element_type.45 = f32[4,512,768]{2,1,0:T(8,128)} convert(bf16[4,512,768]{2,1,0:T(8,128)(2,1)} %all-to-all-done.4) | non-fusion elementwise | flops 1572864 | bytes 9437184 | tf_op jit(solution)/shard_map/convert_element_type | solution.py:756
  454.6 1.1 convert_reduce_fusion.1
  455.7 0.8 slice_reduce_fusion
  456.5 0.1 slice_bitcast_fusion
  456.6 0.7 fusion.7
  457.3 0.1 copy.40
  457.3 0.6 reshape.133
  457.9 1.7 copy.48
  (30 shorter events, 0.1 us)
Async XLA Ops:
  7.2 57.5 %all-gather.3.cloned.1.call-start = ((), (), s32[]{:S(2)}) async-start(), calls=%async_computation.8 | async-start | bytes 4202496 | tf_op jit(solution)/shard_map/all_gather | solution.py:713
  21.1 4.0 copy-start.5
  21.1 4.0 copy-start.6
  21.2 4.0 copy-start.7
  21.2 4.0 copy-start.8
  21.2 4.0 copy-start.9
  21.2 4.0 copy-start.10
  21.2 4.0 copy-start.11
  21.2 4.2 copy-start.3
  21.2 38.5 %all-to-all-start = ((bf16[4,512,768]{2,1,0:T(8,128)(2,1)}), bf16[4,512,768]{2,1,0:T(8,128)(2,1)S(1)}, u32[]{:S(2)}, u32[]{:S(2)}) async-start(bf16[4,512,768]{2,1,0:T(8,128)(2,1)} %param.18), calls=%async_computation | async-start | bytes 6291456 | tf_op jit(solution)/shard_map/all_to_all | solution.py:408
  25.1 7.6 %copy-start.12 = (s32[4]{0:T(128)S(1)}, s32[4]{0:T(128)}, u32[]{:S(2)}) copy-start(s32[4]{0:T(128)} %param.19) | copy-start | bytes 52
  25.1 13.5 %copy-start.4 = (bf16[24,768]{1,0:T(8,128)(2,1)S(1)}, bf16[24,768]{1,0:T(8,128)(2,1)}, u32[]{:S(2)}) copy-start(bf16[24,768]{1,0:T(8,128)(2,1)} %param.26) | copy-start | bytes 110596
  25.1 140.0 %all-gather.5.cloned.1.call-start = ((), (), s32[]{:S(2)}) async-start(), calls=%async_computation.9 | async-start | bytes 11151360 | tf_op jit(solution)/shard_map/all_gather | solution.py:727
  38.7 25.9 %copy-start.2 = (bf16[24,7040]{1,0:T(8,128)(2,1)}, bf16[24,7040]{1,0:T(8,128)(2,1)S(1)}, u32[]{:S(2)}) copy-start(bf16[24,7040]{1,0:T(8,128)(2,1)S(1)} %fusion) | copy-start | bytes 1013764
  59.7 5.0 %copy-start = (bf16[4,512,768]{2,1,0:T(8,128)(2,1)}, bf16[4,512,768]{2,1,0:T(8,128)(2,1)S(1)}, u32[]{:S(2)}) copy-start(bf16[4,512,768]{2,1,0:T(8,128)(2,1)S(1)} %all-to-all-done) | copy-start | bytes 9437188
  76.6 69.7 %all-to-all-start.1 = ((bf16[4,512,768]{2,1,0:T(8,128)(2,1)}), bf16[4,512,768]{2,1,0:T(8,128)(2,1)S(1)}, u32[]{:S(2)}, u32[]{:S(2)}) async-start(bf16[4,512,768]{2,1,0:T(8,128)(2,1)} %param.20), calls=%async_computation.1 | async-start | bytes 6291456 | tf_op jit(solution)/shard_map/all_to_all | solution.py:408
  80.3 297.2 %reduce-scatter.3.cloned.1.call-start = ((), (), s32[]{:S(2)}) async-start(), calls=%async_computation.10 | async-start | bytes 11943936 | tf_op jit(solution)/shard_map/reduce_scatter | solution.py:742
  146.3 18.8 %copy-start.1 = (bf16[4,512,768]{2,1,0:T(8,128)(2,1)}, bf16[4,512,768]{2,1,0:T(8,128)(2,1)S(1)}, u32[]{:S(2)}) copy-start(bf16[4,512,768]{2,1,0:T(8,128)(2,1)S(1)} %all-to-all-done.1) | copy-start | bytes 9437188
  265.1 98.9 %all-to-all-start.2 = ((bf16[4,512,768]{2,1,0:T(8,128)(2,1)}), bf16[4,512,768]{2,1,0:T(8,128)(2,1)S(1)}, u32[]{:S(2)}, u32[]{:S(2)}) async-start(bf16[4,512,768]{2,1,0:T(8,128)(2,1)} %bitcast.25), calls=%async_computation.2 | async-start | bytes 6291456 | tf_op jit(solution)/shard_map/all_to_all | solution.py:408
  268.9 174.0 %reduce-scatter.5.cloned.1.call-start = ((), (), s32[]{:S(2)}) async-start(), calls=%async_computation.11 | async-start | bytes 4202496 | tf_op jit(solution)/shard_map/reduce_scatter | solution.py:749
  377.5 22.0 %all-to-all-start.3 = ((bf16[4,24,6912]{2,1,0:T(8,128)(2,1)}), bf16[4,24,6912]{2,1,0:T(8,128)(2,1)}, u32[]{:S(2)}, u32[]{:S(2)}) async-start(bf16[4,24,6912]{2,1,0:T(8,128)(2,1)} %bitcast.29), calls=%async_computation.5 | async-start | bytes 2654208 | tf_op jit(solution)/shard_map/all_to_all | solution.py:408
  401.9 4.8 %slice-start = ((f32[24,6912]{1,0:T(8,128)}), f32[24,3072]{1,0:T(8,128)S(1)}, s32[]{:S(2)}) async-start(f32[24,6912]{1,0:T(8,128)} %convert_reduce_fusion), calls=%async_computation.12 | async-start | bytes 589824 | tf_op jit(solution)/shard_map/slice | solution.py:759
  401.9 41.0 %all-to-all-start.4 = ((bf16[4,512,768]{2,1,0:T(8,128)(2,1)}), bf16[4,512,768]{2,1,0:T(8,128)(2,1)}, u32[]{:S(2)}, u32[]{:S(2)}) async-start(bf16[4,512,768]{2,1,0:T(8,128)(2,1)} %bitcast.27), calls=%async_computation.6 | async-start | bytes 6291456 | tf_op jit(solution)/shard_map/all_to_all | solution.py:408
  442.9 11.7 %all-to-all-start.5 = ((bf16[4,24,2432]{2,1,0:T(8,128)(2,1)}), bf16[4,24,2432]{2,1,0:T(8,128)(2,1)}, u32[]{:S(2)}, u32[]{:S(2)}) async-start(bf16[4,24,2432]{2,1,0:T(8,128)(2,1)} %bitcast.30), calls=%async_computation.7 | async-start | bytes 933888 | tf_op jit(solution)/shard_map/all_to_all | solution.py:408
Sparse Core Ops, SparseCore 0:
  21.3 43.3 all-gather.2
  68.2 96.8 all-gather.4
  265.3 109.1 reduce-scatter.2
  377.6 45.6 reduce-scatter.4

commit v6 on v5

--- a/solution.py
+++ b/solution.py
@@ -420,9 +420,15 @@
 
 
 def scattered(rows):
+    me = lax.axis_index("seq")
     size = lax.axis_size("seq")
-    parts = exchange(rows.reshape(size, rows.shape[0] // size, rows.shape[1]))
-    return jnp.sum(parts.astype(jnp.float32), 0)
+    parts = rows.reshape(size, rows.shape[0] // size, rows.shape[1])
+    total = take(parts, me).astype(jnp.float32)
+    for step in range(1, size):
+        pairs = [(i, i ^ step) for i in range(size)]
+        came = lax.ppermute(take(parts, me ^ step), "seq", pairs)
+        total = total + came.astype(jnp.float32)
+    return total
 
 
 def row_sums(array):
@@ -749,10 +755,10 @@
     early = lax.psum_scatter(early, "dp", scatter_dimension=0, tiled=True)
     late = scattered(late)
     low = inputs(grads, first, grad_one, block)
-    low, late = lax.optimization_barrier((low, late))
     grad_tokens = exchange(low.reshape(count, block, width))
-    early, grad_tokens = lax.optimization_barrier((early, grad_tokens))
+    early, low = lax.optimization_barrier((early, low))
     early = scattered(early)
+    grad_tokens, early = lax.optimization_barrier((grad_tokens, early))
     grad_tokens = grad_tokens.astype(jnp.float32)
     o_wq, o_wk, o_wv = (early[:, i * width : (i + 1) * width] for i in range(3))
     vec = early[:, 3 * width :]

time: 472 us -> 465 us (0.985)
  waiting for transfers between devices: 73.3 us -> 65.7 us
    all_to_all x6 -> x4, waiting for transfers between devices: 49.5 us -> 19.1 us  [exchange(): return lax.all_to_all(blocks, 'seq', 0, 0, tiled=True)]
    ppermute x0 -> x6, waiting for transfers between devices: none -> 14.4 us  [scattered(): came = lax.ppermute(take(parts, me ^ step), 'seq', pairs)]
    all_to_all x6 -> x4, starting transfers between devices: 24.7 us -> 16.1 us  [exchange(): return lax.all_to_all(blocks, 'seq', 0, 0, tiled=True)]
    reduce_scatter x1, waiting for transfers between devices: 0.01 us -> 8.31 us  [whole_body(): early = lax.psum_scatter(early, 'dp', scatter_dimension=0, tiled=True)]
    ppermute x0 -> x6, starting transfers between devices: none -> 7.04 us  [scattered(): came = lax.ppermute(take(parts, me ^ step), 'seq', pairs)]
  transfers between devices with their start and end apart: 10 -> 14, of which waited for: 5 -> 6; matrix products, arithmetic and copies ran while one was open for 8% -> 7% of each run, Pallas kernels for 43% -> 43%
where the time goes in v6:
time: 465 us; the launch traced here: 460 us
  Pallas kernels  299 us (64%)
  waiting for transfers between devices  65.7 us (14%)
  local copies, waits for them, and re-layouts  32.6 us (7%)
  starting transfers between devices  23.6 us (5%)
  between operations  14.3 us (3%)
  other arithmetic  12.1 us (3%)
  blocking collectives  12 us (3%)
    pallas_call x1, Pallas kernels, unmix(): pl.pallas_call(functools.partial(unmix_kernel, scale, 256), grid=(heads,)...  95.1 us
    pallas_call x1, Pallas kernels, feed(): pl.pallas_call(feed_kernel, grid=(slots // rows,), in_specs=[flat, tall,...  70.8 us
    pallas_call x1, Pallas kernels, mix(): pl.pallas_call(functools.partial(mix_kernel, scale, 512), grid=(heads,),...  65.8 us
    pallas_call x1, Pallas kernels, feed_weights(): pl.pallas_call(feed_weights_kernel, grid=(2 * parts + 1,), in_specs=[pl.B...  29.3 us
    all_to_all x4, waiting for transfers between devices, exchange(): return lax.all_to_all(blocks, 'seq', 0, 0, tiled=True)  19.1 us
    all_gather x1, waiting for transfers between devices, whole_body(): second = lax.all_gather(second, axes, axis=0, tiled=True)  18.7 us
    all_to_all x4, starting transfers between devices, exchange(): return lax.all_to_all(blocks, 'seq', 0, 0, tiled=True)  16.1 us
    ppermute x6, waiting for transfers between devices, scattered(): came = lax.ppermute(take(parts, me ^ step), 'seq', pairs)  14.4 us
  transfers between devices with their start and end apart: 14, of which 6 were waited for; matrix products, arithmetic and copies ran while one was open for 7% of the time, Pallas kernels for 43%

profile of v6, /device:TPU:0, one launch (start us, length us, event | category | flops | bytes accessed | tf_op | source)
XLA Modules:
  0.0 459.9 jit_solution(3066861381208851233)
XLA Ops:
  7.2 0.0 all-gather.3.cloned.1.call-start
  7.2 0.7 pad_maximum_fusion.2
  8.0 0.1 reshape.122
  8.1 0.2 convolution_convert_fusion.1
  8.3 0.8 pad_maximum_fusion.1
  9.1 12.0 %all_gather.9 = bf16[96,2432]{1,0:T(8,128)(2,1)} all-gather(bf16[24,2432]{1,0:T(8,128)(2,1)S(1)} %pad_maximum_fusion.1), channel_id=1, replica_groups=mesh['dp'=8,'seq'=4] {'seq'}, dimensions={0}, use_global_device_ids=true | all-gather | bytes 583680 | tf_op jit(solution)/shard_map/all_gather | solution.py:718
  21.1 3.8 all-to-all-start
  25.1 0.0 all-gather.5.cloned.1.call-start
  25.1 2.1 reshape.119
  27.3 2.2 copy.38
  29.5 2.9 reshape.120
  32.4 0.1 concatenate.15
  32.5 0.1 reshape.121
  32.6 0.6 dynamic_slice.30
  33.2 0.7 fusion.6
  33.9 0.6 pad.4.bias
  34.5 0.9 constant_dynamic-update-slice_fusion.1
  35.5 0.8 slice_dynamic-update-slice_fusion.3
  36.2 0.8 slice_dynamic-update-slice_fusion.2
  37.0 0.8 slice_dynamic-update-slice_fusion.1
  37.8 0.8 slice_dynamic-update-slice_fusion
  38.6 0.2 fusion
  38.8 1.8 fusion.1.live
  40.5 19.1 %all-to-all-done = bf16[4,512,768]{2,1,0:T(8,128)(2,1)S(1)} async-done(((bf16[4,512,768]{2,1,0:T(8,128)(2,1)}), bf16[4,512,768]{2,1,0:T(8,128)(2,1)S(1)}, u32[]{:S(2)}, u32[]{:S(2)}) %all-to-all-start) | async-done | bytes 3145760 | tf_op jit(solution)/shard_map/all_to_all | solution.py:408
  59.6 5.1 %all-gather.3.cloned.1.call-done.w.vec.weights = bf16[768,2432]{1,0:T(8,128)(2,1)} async-done(((bf16[96,2432]{1,0:T(8,128)(2,1)}), bf16[768,2432]{1,0:T(8,128)(2,1)}) %all-gather.3.cloned.1.call-update) | async-done | bytes 3735568 | tf_op jit(solution)/shard_map/all_gather | solution.py:719
  64.7 11.9 %project.1 = (bf16[768,2048]{1,0:T(8,128)(2,1)}, bf16[768,2048]{1,0:T(8,128)(2,1)}, bf16[768,2048]{1,0:T(8,128)(2,1)}) custom-call(bf16[2048,768]{1,0:T(8,128)(2,1)} %bitcast.40, bf16[768,2432]{1,0:T(8,128)(2,1)} %all-gather.3.cloned.1.call-done.w.vec.weights, bf16[768,2432]{1,0:T(8,128)(2,1)} %all-gather.3.cloned.1.call-done.w.vec.weights), custom_call_target="tpu_custom_call" | custom-call | flops 11000000512 | tf_op jit(solution)/shard_map/project/pallas_call | solution.py:453
  76.6 3.7 all-to-all-start.1
  80.3 0.3 reduce-scatter.3.cloned.1.call-start
  80.6 65.8 %mix.1 = (bf16[12,64,2048]{2,1,0:T(8,128)(2,1)}, f32[12,1,2048]{2,1,0:T(1,128)}, bf16[12,2048,2048]{2,1,0:T(8,128)(2,1)}) custom-call(bf16[12,64,2048]{2,1,0:T(8,128)(2,1)} %bitcast.53, bf16[12,64,2048]{2,1,0:T(8,128)(2,1)} %bitcast.55, bf16[12,64,2048]{2,1,0:T(8,128)(2,1)} %bitcast.57, bf16[16,2048]{1,0:T(8,128)(2,1)} %pad.4.bias), custom_call_target="tpu_custom_call" | custom-call | flops 65000001536 | tf_op jit(solution)/shard_map/mix/pallas_call | solution.py:343
  146.3 18.7 %all-gather.5.cloned.1.call-done.vec.wo.wu.wd = bf16[768,7040]{1,0:T(8,128)(2,1)} async-done(((bf16[24,7040]{1,0:T(8,128)(2,1)}), bf16[768,7040]{1,0:T(8,128)(2,1)}) %all-gather.5.cloned.1.call-update) | async-done | bytes 10813456 | tf_op jit(solution)/shard_map/all_gather | solution.py:733
  165.0 70.8 %feed.1 = (bf16[2048,768]{1,0:T(8,128)(2,1)}, f32[2048,768]{1,0:T(8,128)}, bf16[768,2048]{1,0:T(8,128)(2,1)}, bf16[2048,4608]{1,0:T(8,128)(2,1)}, bf16[2048,4608]{1,0:T(8,128)(2,1)}, /*index=5*/f32[12,768]{1,0:T(8,128)}) custom-call(bf16[2048,768]{1,0:T(8,128)(2,1)} %bitcast.41, bf16[768,2048]{1,0:T(8,128)(2,1)} %bitcast.59, bf16[2048,768]{1,0:T(8,128)(2,1)} %bitcast.45, ...), custom_call_target="tpu_custom_call" | custom-call | flops 70000001024 | tf_op jit(solution)/shard_map/feed/pallas_call | solution.py:554
  235.8 29.3 %feed_weights.1 = bf16[768,6912]{1,0:T(8,128)(2,1)} custom-call(bf16[2048,4608]{1,0:T(8,128)(2,1)} %get-tuple-element.61.left, bf16[2048,4608]{1,0:T(8,128)(2,1)} %get-tuple-element.62.right), custom_call_target="tpu_custom_call" | custom-call | flops 25999998976 | tf_op jit(solution)/shard_map/feed_weights/pallas_call | solution.py:597
  265.1 3.7 all-to-all-start.2
  268.8 0.0 reduce-scatter.5.cloned.1.call-start
  268.9 95.1 %unmix.1 = bf16[3,12,64,2048]{3,2,1,0:T(8,128)(2,1)} custom-call(bf16[12,2048,2048]{2,1,0:T(8,128)(2,1)} %get-tuple-element.55.probs, bf16[12,64,2048]{2,1,0:T(8,128)(2,1)} %bitcast.54, bf16[12,64,2048]{2,1,0:T(8,128)(2,1)} %bitcast.56, bf16[12,64,2048]{2,1,0:T(8,128)(2,1)} %bitcast.58, bf16[12,64,2048]{2,1,0:T(8,128)(2,1)} %bitcast.60, ...), custom_call_target="tpu_custom_call" | custom-call | flops 95000002560 | tf_op jit(solution)/shard_map/unmix/pallas_call | solution.py:392
  364.0 13.4 %input_weights.1 = bf16[768,2432]{1,0:T(8,128)(2,1)} custom-call(bf16[2048,768]{1,0:T(8,128)(2,1)} %bitcast.42, bf16[2304,2048]{1,0:T(8,128)(2,1)} %bitcast.51, f32[12,768]{1,0:T(8,128)} %get-tuple-element.68.rows), custom_call_target="tpu_custom_call" | custom-call | flops 12000000000 | tf_op jit(solution)/shard_map/input_weights/pallas_call | solution.py:668
  377.5 2.2 dynamic-slice_bitcast_fusion.2
  379.7 1.8 collective-permute-start.3
  381.5 1.5 collective-permute-start.4
  383.0 0.2 collective-permute-start.5
  383.2 12.9 %inputs.1 = bf16[2048,768]{1,0:T(8,128)(2,1)} custom-call(bf16[2304,2048]{1,0:T(8,128)(2,1)} %bitcast.52, bf16[768,2432]{1,0:T(8,128)(2,1)} %all-gather.3.cloned.1.call-done.w.vec.weights, f32[2048,768]{1,0:T(8,128)} %get-tuple-element.71.grad_one), custom_call_target="tpu_custom_call" | custom-call | flops 12000000000 | tf_op jit(solution)/shard_map/inputs/pallas_call | solution.py:622
  396.1 4.9 %all-to-all-start.3 = ((bf16[4,512,768]{2,1,0:T(8,128)(2,1)}), bf16[4,512,768]{2,1,0:T(8,128)(2,1)}, u32[]{:S(2)}, u32[]{:S(2)}) async-start(bf16[4,512,768]{2,1,0:T(8,128)(2,1)} %bitcast.43), calls=%async_computation.4 | async-start | bytes 6291456 | tf_op jit(solution)/shard_map/all_to_all | solution.py:408
  401.0 1.3 fusion.3
  402.4 0.8 copy-done.2
  403.2 2.3 reshape.135
  405.5 3.8 copy.39
  409.4 4.0 reshape.136
  413.4 1.7 fusion.10
  415.0 8.3 %reduce-scatter.5.cloned.1.call-done = bf16[96,2432]{1,0:T(8,128)(2,1)} async-done(((bf16[768,2432]{1,0:T(8,128)(2,1)}), bf16[96,2432]{1,0:T(8,128)(2,1)}) %reduce-scatter.5.cloned.1.call-update) | async-done | bytes 466960 | tf_op jit(solution)/shard_map/reduce_scatter | solution.py:755
  423.4 1.0 dynamic-slice_bitcast_fusion.5
  424.4 1.5 collective-permute-start
  425.9 1.5 collective-permute-start.1
  427.4 0.5 collective-permute-start.2
  428.0 0.7 pad_maximum_fusion
  428.7 12.2 %collective-permute-done = bf16[24,2432]{1,0:T(8,128)(2,1)S(1)} collective-permute-done((bf16[24,2432]{1,0:T(8,128)(2,1)S(1)}, bf16[24,2432]{1,0:T(8,128)(2,1)S(1)}, u32[]{:S(2)}, u32[]{:S(2)}) %collective-permute-start) | collective-permute-done | bytes 116768 | tf_op jit(solution)/shard_map/ppermute | solution.py:429
  440.9 2.2 collective-permute-done.2
  443.1 1.0 fusion.5
  444.1 0.7 fusion.11
  444.8 0.1 slice_bitcast_fusion
  444.9 0.8 slice_reduce_fusion
  445.7 5.1 %convert_element_type.73 = f32[4,512,768]{2,1,0:T(8,128)} convert(bf16[4,512,768]{2,1,0:T(8,128)(2,1)} %all-to-all-done.3) | non-fusion elementwise | flops 1572864 | bytes 9437184 | tf_op jit(solution)/shard_map/convert_element_type | solution.py:762
  450.8 0.1 copy.40
  450.9 0.6 reshape.137
  451.5 1.7 copy.48
  (41 shorter events, 0.2 us)
Async XLA Ops:
  7.2 57.5 %all-gather.3.cloned.1.call-start = ((), (), s32[]{:S(2)}) async-start(), calls=%async_computation.6 | async-start | bytes 4202496 | tf_op jit(solution)/shard_map/all_gather | solution.py:719
  21.1 4.0 copy-start.4
  21.1 38.5 %all-to-all-start = ((bf16[4,512,768]{2,1,0:T(8,128)(2,1)}), bf16[4,512,768]{2,1,0:T(8,128)(2,1)S(1)}, u32[]{:S(2)}, u32[]{:S(2)}) async-start(bf16[4,512,768]{2,1,0:T(8,128)(2,1)} %param.18), calls=%async_computation | async-start | bytes 6291456 | tf_op jit(solution)/shard_map/all_to_all | solution.py:408
  25.0 7.4 %copy-start.6 = (bf16[24]{0:T(256)(128)(2,1)S(1)}, bf16[24]{0:T(256)(128)(2,1)}, u32[]{:S(2)}) copy-start(bf16[24]{0:T(256)(128)(2,1)} %param.27) | copy-start | bytes 148
  25.0 7.4 %copy-start.7 = (bf16[24]{0:T(256)(128)(2,1)S(1)}, bf16[24]{0:T(256)(128)(2,1)}, u32[]{:S(2)}) copy-start(bf16[24]{0:T(256)(128)(2,1)} %param.28) | copy-start | bytes 148
  25.0 7.4 %copy-start.8 = (bf16[24]{0:T(256)(128)(2,1)S(1)}, bf16[24]{0:T(256)(128)(2,1)}, u32[]{:S(2)}) copy-start(bf16[24]{0:T(256)(128)(2,1)} %param.29) | copy-start | bytes 148
  25.0 7.4 %copy-start.9 = (bf16[24]{0:T(256)(128)(2,1)S(1)}, bf16[24]{0:T(256)(128)(2,1)}, u32[]{:S(2)}) copy-start(bf16[24]{0:T(256)(128)(2,1)} %param.33) | copy-start | bytes 148
  25.0 7.4 %copy-start.10 = (bf16[24]{0:T(256)(128)(2,1)S(1)}, bf16[24]{0:T(256)(128)(2,1)}, u32[]{:S(2)}) copy-start(bf16[24]{0:T(256)(128)(2,1)} %param.34) | copy-start | bytes 148
  25.0 7.4 %copy-start.11 = (bf16[24]{0:T(256)(128)(2,1)S(1)}, bf16[24]{0:T(256)(128)(2,1)}, u32[]{:S(2)}) copy-start(bf16[24]{0:T(256)(128)(2,1)} %param.35) | copy-start | bytes 148
  25.0 7.4 %copy-start.12 = (bf16[96]{0:T(256)(128)(2,1)S(1)}, bf16[96]{0:T(256)(128)(2,1)}, u32[]{:S(2)}) copy-start(bf16[96]{0:T(256)(128)(2,1)} %param.31) | copy-start | bytes 580
  25.1 7.6 %copy-start.13 = (s32[4]{0:T(128)S(1)}, s32[4]{0:T(128)}, u32[]{:S(2)}) copy-start(s32[4]{0:T(128)} %param.19) | copy-start | bytes 52
  25.1 13.5 %copy-start.5 = (bf16[24,768]{1,0:T(8,128)(2,1)S(1)}, bf16[24,768]{1,0:T(8,128)(2,1)}, u32[]{:S(2)}) copy-start(bf16[24,768]{1,0:T(8,128)(2,1)} %param.26) | copy-start | bytes 110596
  25.1 140.0 %all-gather.5.cloned.1.call-start = ((), (), s32[]{:S(2)}) async-start(), calls=%async_computation.7 | async-start | bytes 11151360 | tf_op jit(solution)/shard_map/all_gather | solution.py:733
  38.8 25.9 %copy-start.3 = (bf16[24,7040]{1,0:T(8,128)(2,1)}, bf16[24,7040]{1,0:T(8,128)(2,1)S(1)}, u32[]{:S(2)}) copy-start(bf16[24,7040]{1,0:T(8,128)(2,1)S(1)} %fusion) | copy-start | bytes 1013764
  59.6 5.1 %copy-start = (bf16[4,512,768]{2,1,0:T(8,128)(2,1)}, bf16[4,512,768]{2,1,0:T(8,128)(2,1)S(1)}, u32[]{:S(2)}) copy-start(bf16[4,512,768]{2,1,0:T(8,128)(2,1)S(1)} %all-to-all-done) | copy-start | bytes 9437188
  76.6 69.8 %all-to-all-start.1 = ((bf16[4,512,768]{2,1,0:T(8,128)(2,1)}), bf16[4,512,768]{2,1,0:T(8,128)(2,1)S(1)}, u32[]{:S(2)}, u32[]{:S(2)}) async-start(bf16[4,512,768]{2,1,0:T(8,128)(2,1)} %param.20), calls=%async_computation.1 | async-start | bytes 6291456 | tf_op jit(solution)/shard_map/all_to_all | solution.py:408
  80.3 297.2 %reduce-scatter.3.cloned.1.call-start = ((), (), s32[]{:S(2)}) async-start(), calls=%async_computation.8 | async-start | bytes 11943936 | tf_op jit(solution)/shard_map/reduce_scatter | solution.py:748
  146.3 18.7 %copy-start.1 = (bf16[4,512,768]{2,1,0:T(8,128)(2,1)}, bf16[4,512,768]{2,1,0:T(8,128)(2,1)S(1)}, u32[]{:S(2)}) copy-start(bf16[4,512,768]{2,1,0:T(8,128)(2,1)S(1)} %all-to-all-done.1) | copy-start | bytes 9437188
  265.1 98.9 %all-to-all-start.2 = ((bf16[4,512,768]{2,1,0:T(8,128)(2,1)}), bf16[4,512,768]{2,1,0:T(8,128)(2,1)S(1)}, u32[]{:S(2)}, u32[]{:S(2)}) async-start(bf16[4,512,768]{2,1,0:T(8,128)(2,1)} %bitcast.44), calls=%async_computation.2 | async-start | bytes 6291456 | tf_op jit(solution)/shard_map/all_to_all | solution.py:408
  268.8 154.5 %reduce-scatter.5.cloned.1.call-start = ((), (), s32[]{:S(2)}) async-start(), calls=%async_computation.9 | async-start | bytes 4202496 | tf_op jit(solution)/shard_map/reduce_scatter | solution.py:755
  379.7 21.3 %collective-permute-start.3 = (bf16[24,6912]{1,0:T(8,128)(2,1)}, bf16[24,6912]{1,0:T(8,128)(2,1)S(1)}, u32[]{:S(2)}, u32[]{:S(2)}) collective-permute-start(bf16[24,6912]{1,0:T(8,128)(2,1)} %get-tuple-element.85), channel_id=1, source_target_pairs={{0,1},{1,0},{2,3},{3,2},{4,5},{5,4},{6,7},{7,6},{8,9},{9,8},{10,11... | collective-permute-start | bytes 995336 | tf_op jit(solution)/shard_map/ppermute | solution.py:429
  381.5 19.5 %collective-permute-start.4 = (bf16[24,6912]{1,0:T(8,128)(2,1)}, bf16[24,6912]{1,0:T(8,128)(2,1)}, u32[]{:S(2)}, u32[]{:S(2)}) collective-permute-start(bf16[24,6912]{1,0:T(8,128)(2,1)} %get-tuple-element.87), channel_id=1, source_target_pairs={{0,2},{1,3},{2,0},{3,1},{4,6},{5,7},{6,4},{7,5},{8,10},{9,11},{10,... | collective-permute-start | bytes 995336 | tf_op jit(solution)/shard_map/ppermute | solution.py:429
  383.0 18.0 %collective-permute-start.5 = (bf16[24,6912]{1,0:T(8,128)(2,1)}, bf16[24,6912]{1,0:T(8,128)(2,1)}, u32[]{:S(2)}, u32[]{:S(2)}) collective-permute-start(bf16[24,6912]{1,0:T(8,128)(2,1)} %get-tuple-element.86), channel_id=1, source_target_pairs={{0,3},{1,2},{2,1},{3,0},{4,7},{5,6},{6,5},{7,4},{8,11},{9,10},{10,... | collective-permute-start | bytes 995336 | tf_op jit(solution)/shard_map/ppermute | solution.py:429
  396.1 48.0 %all-to-all-start.3 = ((bf16[4,512,768]{2,1,0:T(8,128)(2,1)}), bf16[4,512,768]{2,1,0:T(8,128)(2,1)}, u32[]{:S(2)}, u32[]{:S(2)}) async-start(bf16[4,512,768]{2,1,0:T(8,128)(2,1)} %bitcast.43), calls=%async_computation.4 | async-start | bytes 6291456 | tf_op jit(solution)/shard_map/all_to_all | solution.py:408
  402.4 0.9 copy-start.2
  424.4 16.5 %collective-permute-start = (bf16[24,2432]{1,0:T(8,128)(2,1)S(1)}, bf16[24,2432]{1,0:T(8,128)(2,1)S(1)}, u32[]{:S(2)}, u32[]{:S(2)}) collective-permute-start(bf16[24,2432]{1,0:T(8,128)(2,1)S(1)} %get-tuple-element.93), channel_id=1, source_target_pairs={{0,1},{1,0},{2,3},{3,2},{4,5},{5,4},{6,7},{7,6},{8,9},{9,8},{10,11... | collective-permute-start | bytes 350216 | tf_op jit(solution)/shard_map/ppermute | solution.py:429
  425.9 15.0 %collective-permute-start.1 = (bf16[24,2432]{1,0:T(8,128)(2,1)S(1)}, bf16[24,2432]{1,0:T(8,128)(2,1)S(1)}, u32[]{:S(2)}, u32[]{:S(2)}) collective-permute-start(bf16[24,2432]{1,0:T(8,128)(2,1)S(1)} %get-tuple-element.95), channel_id=1, source_target_pairs={{0,2},{1,3},{2,0},{3,1},{4,6},{5,7},{6,4},{7,5},{8,10},{9,11},{10,... | collective-permute-start | bytes 350216 | tf_op jit(solution)/shard_map/ppermute | solution.py:429
  427.4 15.7 %collective-permute-start.2 = (bf16[24,2432]{1,0:T(8,128)(2,1)S(1)}, bf16[24,2432]{1,0:T(8,128)(2,1)S(1)}, u32[]{:S(2)}, u32[]{:S(2)}) collective-permute-start(bf16[24,2432]{1,0:T(8,128)(2,1)S(1)} %get-tuple-element.94), channel_id=1, source_target_pairs={{0,3},{1,2},{2,1},{3,0},{4,7},{5,6},{6,5},{7,4},{8,11},{9,10},{10,... | collective-permute-start | bytes 350216 | tf_op jit(solution)/shard_map/ppermute | solution.py:429
Sparse Core Ops, SparseCore 0:
  21.2 43.3 all-gather.2
  68.1 96.8 all-gather.4
  265.2 109.1 reduce-scatter.2
  377.6 45.6 reduce-scatter.4

commit v7 on v6

--- a/solution.py
+++ b/solution.py
@@ -728,7 +728,7 @@
     bias = jnp.where(live, 0.0, -1e30).astype(jnp.bfloat16)
     bias = jnp.pad(bias[None, :], ((0, PAD - 1), (0, 0)))
     live = live[:, None].astype(jnp.float32)
-    x, live, bias = lax.optimization_barrier((x, live, bias))
+    x, live, bias, cotangent = lax.optimization_barrier((x, live, bias, cotangent))
     second, first, x = lax.optimization_barrier((second, first, x))
     second = lax.all_gather(second, axes, axis=0, tiled=True)
 
@@ -736,7 +736,6 @@
         return array.reshape(heads, size, slots)
 
     qt, kt, vt = project(x, first, block)
-    qt, cotangent = lax.optimization_barrier((qt, cotangent))
     cot = exchange(cotangent).reshape(slots, width)
     qt, kt, vt = (by_head(a) for a in (qt, kt, vt))
     mt, total, probs = mix(qt, kt, vt, bias, scale * LOG2E)

time: 465 us -> 466 us (level)
  no operation moved by 1% of the time
where the time goes in v7:
time: 466 us; the launch traced here: 461 us
  Pallas kernels  299 us (64%)
  waiting for transfers between devices  66.1 us (14%)
  local copies, waits for them, and re-layouts  32.6 us (7%)
  starting transfers between devices  24.3 us (5%)
  between operations  14.3 us (3%)
  other arithmetic  12.1 us (3%)
  blocking collectives  12 us (3%)
    pallas_call x1, Pallas kernels, unmix(): pl.pallas_call(functools.partial(unmix_kernel, scale, 256), grid=(heads,)...  95.1 us
    pallas_call x1, Pallas kernels, feed(): pl.pallas_call(feed_kernel, grid=(slots // rows,), in_specs=[flat, tall,...  70.8 us
    pallas_call x1, Pallas kernels, mix(): pl.pallas_call(functools.partial(mix_kernel, scale, 512), grid=(heads,),...  66 us
    pallas_call x1, Pallas kernels, feed_weights(): pl.pallas_call(feed_weights_kernel, grid=(2 * parts + 1,), in_specs=[pl.B...  29.2 us
    all_gather x1, waiting for transfers between devices, whole_body(): second = lax.all_gather(second, axes, axis=0, tiled=True)  19.2 us
    all_to_all x4, waiting for transfers between devices, exchange(): return lax.all_to_all(blocks, 'seq', 0, 0, tiled=True)  19.1 us
    all_to_all x4, starting transfers between devices, exchange(): return lax.all_to_all(blocks, 'seq', 0, 0, tiled=True)  17.1 us
    ppermute x6, waiting for transfers between devices, scattered(): came = lax.ppermute(take(parts, me ^ step), 'seq', pairs)  14.4 us
  transfers between devices with their start and end apart: 14, of which 6 were waited for; matrix products, arithmetic and copies ran while one was open for 7% of the time, Pallas kernels for 43%

profile of v7, /device:TPU:0, one launch (start us, length us, event | category | flops | bytes accessed | tf_op | source)
XLA Modules:
  0.0 461.2 jit_solution(7384875363523003145)
XLA Ops:
  7.2 0.0 all-gather.3.cloned.1.call-start
  7.2 0.7 pad_maximum_fusion.2
  8.0 0.1 reshape.122
  8.1 0.2 convolution_convert_fusion.1
  8.3 0.8 pad_maximum_fusion.1
  9.1 12.0 %all_gather.9 = bf16[96,2432]{1,0:T(8,128)(2,1)} all-gather(bf16[24,2432]{1,0:T(8,128)(2,1)S(1)} %pad_maximum_fusion.1), channel_id=1, replica_groups=mesh['dp'=8,'seq'=4] {'seq'}, dimensions={0}, use_global_device_ids=true | all-gather | bytes 583680 | tf_op jit(solution)/shard_map/all_gather | solution.py:718
  21.1 3.8 all-to-all-start
  25.1 0.0 all-gather.5.cloned.1.call-start
  25.2 2.1 reshape.119
  27.3 2.2 copy.38
  29.5 2.9 reshape.120
  32.4 0.1 concatenate.15
  32.5 0.1 reshape.121
  32.6 0.6 dynamic_slice.30
  33.2 0.7 fusion.6
  33.9 0.6 pad.4.bias
  34.5 0.9 constant_dynamic-update-slice_fusion.1
  35.5 0.8 slice_dynamic-update-slice_fusion.3
  36.2 0.8 slice_dynamic-update-slice_fusion.2
  37.0 0.8 slice_dynamic-update-slice_fusion.1
  37.8 0.8 slice_dynamic-update-slice_fusion
  38.6 0.2 fusion
  38.8 1.8 fusion.1.live
  40.5 19.1 %all-to-all-done = bf16[4,512,768]{2,1,0:T(8,128)(2,1)S(1)} async-done(((bf16[4,512,768]{2,1,0:T(8,128)(2,1)}), bf16[4,512,768]{2,1,0:T(8,128)(2,1)S(1)}, u32[]{:S(2)}, u32[]{:S(2)}) %all-to-all-start) | async-done | bytes 3145760 | tf_op jit(solution)/shard_map/all_to_all | solution.py:408
  59.6 5.1 %all-gather.3.cloned.1.call-done.w.vec.weights = bf16[768,2432]{1,0:T(8,128)(2,1)} async-done(((bf16[96,2432]{1,0:T(8,128)(2,1)}), bf16[768,2432]{1,0:T(8,128)(2,1)}) %all-gather.3.cloned.1.call-update) | async-done | bytes 3735568 | tf_op jit(solution)/shard_map/all_gather | solution.py:719
  64.7 4.6 %all-to-all-start.1 = ((bf16[4,512,768]{2,1,0:T(8,128)(2,1)}), bf16[4,512,768]{2,1,0:T(8,128)(2,1)}, u32[]{:S(2)}, u32[]{:S(2)}) async-start(bf16[4,512,768]{2,1,0:T(8,128)(2,1)} %param.20), calls=%async_computation.1 | async-start | bytes 6291456 | tf_op jit(solution)/shard_map/all_to_all | solution.py:408
  69.3 0.0 reduce-scatter.3.cloned.1.call-start
  69.4 11.8 %project.1 = (bf16[768,2048]{1,0:T(8,128)(2,1)}, bf16[768,2048]{1,0:T(8,128)(2,1)}, bf16[768,2048]{1,0:T(8,128)(2,1)}) custom-call(bf16[2048,768]{1,0:T(8,128)(2,1)} %bitcast.40, bf16[768,2432]{1,0:T(8,128)(2,1)} %all-gather.3.cloned.1.call-done.w.vec.weights, bf16[768,2432]{1,0:T(8,128)(2,1)} %all-gather.3.cloned.1.call-done.w.vec.weights), custom_call_target="tpu_custom_call" | custom-call | flops 11000000512 | tf_op jit(solution)/shard_map/project/pallas_call | solution.py:453
  81.2 66.0 %mix.1 = (bf16[12,64,2048]{2,1,0:T(8,128)(2,1)}, f32[12,1,2048]{2,1,0:T(1,128)}, bf16[12,2048,2048]{2,1,0:T(8,128)(2,1)}) custom-call(bf16[12,64,2048]{2,1,0:T(8,128)(2,1)} %bitcast.52, bf16[12,64,2048]{2,1,0:T(8,128)(2,1)} %bitcast.54, bf16[12,64,2048]{2,1,0:T(8,128)(2,1)} %bitcast.56, bf16[16,2048]{1,0:T(8,128)(2,1)} %pad.4.bias), custom_call_target="tpu_custom_call" | custom-call | flops 65000001536 | tf_op jit(solution)/shard_map/mix/pallas_call | solution.py:343
  147.2 19.2 %all-gather.5.cloned.1.call-done.vec.wo.wu.wd = bf16[768,7040]{1,0:T(8,128)(2,1)} async-done(((bf16[24,7040]{1,0:T(8,128)(2,1)}), bf16[768,7040]{1,0:T(8,128)(2,1)}) %all-gather.5.cloned.1.call-update) | async-done | bytes 10813456 | tf_op jit(solution)/shard_map/all_gather | solution.py:733
  166.4 70.8 %feed.1 = (bf16[2048,768]{1,0:T(8,128)(2,1)}, f32[2048,768]{1,0:T(8,128)}, bf16[768,2048]{1,0:T(8,128)(2,1)}, bf16[2048,4608]{1,0:T(8,128)(2,1)}, bf16[2048,4608]{1,0:T(8,128)(2,1)}, /*index=5*/f32[12,768]{1,0:T(8,128)}) custom-call(bf16[2048,768]{1,0:T(8,128)(2,1)} %bitcast.41, bf16[768,2048]{1,0:T(8,128)(2,1)} %bitcast.58, bf16[2048,768]{1,0:T(8,128)(2,1)} %bitcast.7.cot, ...), custom_call_target="tpu_custom_call" | custom-call | flops 70000001024 | tf_op jit(solution)/shard_map/feed/pallas_call | solution.py:554
  237.2 29.2 %feed_weights.1 = bf16[768,6912]{1,0:T(8,128)(2,1)} custom-call(bf16[2048,4608]{1,0:T(8,128)(2,1)} %get-tuple-element.59.left, bf16[2048,4608]{1,0:T(8,128)(2,1)} %get-tuple-element.60.right), custom_call_target="tpu_custom_call" | custom-call | flops 25999998976 | tf_op jit(solution)/shard_map/feed_weights/pallas_call | solution.py:597
  266.4 3.7 all-to-all-start.2
  270.1 0.0 reduce-scatter.5.cloned.1.call-start
  270.2 95.1 %unmix.1 = bf16[3,12,64,2048]{3,2,1,0:T(8,128)(2,1)} custom-call(bf16[12,2048,2048]{2,1,0:T(8,128)(2,1)} %get-tuple-element.53.probs, bf16[12,64,2048]{2,1,0:T(8,128)(2,1)} %bitcast.53, bf16[12,64,2048]{2,1,0:T(8,128)(2,1)} %bitcast.55, bf16[12,64,2048]{2,1,0:T(8,128)(2,1)} %bitcast.57, bf16[12,64,2048]{2,1,0:T(8,128)(2,1)} %bitcast.59, ...), custom_call_target="tpu_custom_call" | custom-call | flops 95000002560 | tf_op jit(solution)/shard_map/unmix/pallas_call | solution.py:392
  365.3 13.4 %input_weights.1 = bf16[768,2432]{1,0:T(8,128)(2,1)} custom-call(bf16[2048,768]{1,0:T(8,128)(2,1)} %bitcast.42, bf16[2304,2048]{1,0:T(8,128)(2,1)} %bitcast.50, f32[12,768]{1,0:T(8,128)} %get-tuple-element.66.rows), custom_call_target="tpu_custom_call" | custom-call | flops 12000000000 | tf_op jit(solution)/shard_map/input_weights/pallas_call | solution.py:668
  378.8 2.2 dynamic-slice_bitcast_fusion.2
  380.9 1.9 collective-permute-start.3
  382.8 1.5 collective-permute-start.4
  384.3 0.2 collective-permute-start.5
  384.4 12.9 %inputs.1 = bf16[2048,768]{1,0:T(8,128)(2,1)} custom-call(bf16[2304,2048]{1,0:T(8,128)(2,1)} %bitcast.51, bf16[768,2432]{1,0:T(8,128)(2,1)} %all-gather.3.cloned.1.call-done.w.vec.weights, f32[2048,768]{1,0:T(8,128)} %get-tuple-element.69.grad_one), custom_call_target="tpu_custom_call" | custom-call | flops 12000000000 | tf_op jit(solution)/shard_map/inputs/pallas_call | solution.py:622
  397.4 4.9 %all-to-all-start.3 = ((bf16[4,512,768]{2,1,0:T(8,128)(2,1)}), bf16[4,512,768]{2,1,0:T(8,128)(2,1)}, u32[]{:S(2)}, u32[]{:S(2)}) async-start(bf16[4,512,768]{2,1,0:T(8,128)(2,1)} %bitcast.43), calls=%async_computation.4 | async-start | bytes 6291456 | tf_op jit(solution)/shard_map/all_to_all | solution.py:408
  402.3 1.3 fusion.3
  403.6 0.9 copy-done.1
  404.5 2.3 reshape.135
  406.8 3.8 copy.39
  410.6 4.0 reshape.136
  414.6 1.7 fusion.10
  416.3 8.3 %reduce-scatter.5.cloned.1.call-done = bf16[96,2432]{1,0:T(8,128)(2,1)} async-done(((bf16[768,2432]{1,0:T(8,128)(2,1)}), bf16[96,2432]{1,0:T(8,128)(2,1)}) %reduce-scatter.5.cloned.1.call-update) | async-done | bytes 466960 | tf_op jit(solution)/shard_map/reduce_scatter | solution.py:754
  424.7 1.0 dynamic-slice_bitcast_fusion.5
  425.7 1.6 collective-permute-start
  427.2 1.5 collective-permute-start.1
  428.7 0.5 collective-permute-start.2
  429.2 0.7 pad_maximum_fusion
  430.0 12.2 %collective-permute-done = bf16[24,2432]{1,0:T(8,128)(2,1)S(1)} collective-permute-done((bf16[24,2432]{1,0:T(8,128)(2,1)S(1)}, bf16[24,2432]{1,0:T(8,128)(2,1)S(1)}, u32[]{:S(2)}, u32[]{:S(2)}) %collective-permute-start) | collective-permute-done | bytes 116768 | tf_op jit(solution)/shard_map/ppermute | solution.py:429
  442.2 2.2 collective-permute-done.2
  444.4 1.0 fusion.5
  445.4 0.7 fusion.11
  446.1 0.1 slice_bitcast_fusion
  446.1 0.8 slice_reduce_fusion
  446.9 5.1 %convert_element_type.73 = f32[4,512,768]{2,1,0:T(8,128)} convert(bf16[4,512,768]{2,1,0:T(8,128)(2,1)} %all-to-all-done.3) | non-fusion elementwise | flops 1572864 | bytes 9437184 | tf_op jit(solution)/shard_map/convert_element_type | solution.py:761
  452.1 0.1 copy.40
  452.2 0.6 reshape.137
  452.8 1.7 copy.48
  (39 shorter events, 0.2 us)
Async XLA Ops:
  7.2 57.5 %all-gather.3.cloned.1.call-start = ((), (), s32[]{:S(2)}) async-start(), calls=%async_computation.6 | async-start | bytes 4202496 | tf_op jit(solution)/shard_map/all_gather | solution.py:719
  21.1 4.0 copy-start.3
  21.1 38.5 %all-to-all-start = ((bf16[4,512,768]{2,1,0:T(8,128)(2,1)}), bf16[4,512,768]{2,1,0:T(8,128)(2,1)S(1)}, u32[]{:S(2)}, u32[]{:S(2)}) async-start(bf16[4,512,768]{2,1,0:T(8,128)(2,1)} %param.18), calls=%async_computation | async-start | bytes 6291456 | tf_op jit(solution)/shard_map/all_to_all | solution.py:408
  25.0 7.4 %copy-start.5 = (bf16[24]{0:T(256)(128)(2,1)S(1)}, bf16[24]{0:T(256)(128)(2,1)}, u32[]{:S(2)}) copy-start(bf16[24]{0:T(256)(128)(2,1)} %param.27) | copy-start | bytes 148
  25.0 7.4 %copy-start.6 = (bf16[24]{0:T(256)(128)(2,1)S(1)}, bf16[24]{0:T(256)(128)(2,1)}, u32[]{:S(2)}) copy-start(bf16[24]{0:T(256)(128)(2,1)} %param.28) | copy-start | bytes 148
  25.0 7.4 %copy-start.7 = (bf16[24]{0:T(256)(128)(2,1)S(1)}, bf16[24]{0:T(256)(128)(2,1)}, u32[]{:S(2)}) copy-start(bf16[24]{0:T(256)(128)(2,1)} %param.29) | copy-start | bytes 148
  25.0 7.4 %copy-start.8 = (bf16[24]{0:T(256)(128)(2,1)S(1)}, bf16[24]{0:T(256)(128)(2,1)}, u32[]{:S(2)}) copy-start(bf16[24]{0:T(256)(128)(2,1)} %param.33) | copy-start | bytes 148
  25.0 7.4 %copy-start.9 = (bf16[24]{0:T(256)(128)(2,1)S(1)}, bf16[24]{0:T(256)(128)(2,1)}, u32[]{:S(2)}) copy-start(bf16[24]{0:T(256)(128)(2,1)} %param.34) | copy-start | bytes 148
  25.0 7.4 %copy-start.10 = (bf16[24]{0:T(256)(128)(2,1)S(1)}, bf16[24]{0:T(256)(128)(2,1)}, u32[]{:S(2)}) copy-start(bf16[24]{0:T(256)(128)(2,1)} %param.35) | copy-start | bytes 148
  25.1 7.4 %copy-start.11 = (bf16[96]{0:T(256)(128)(2,1)S(1)}, bf16[96]{0:T(256)(128)(2,1)}, u32[]{:S(2)}) copy-start(bf16[96]{0:T(256)(128)(2,1)} %param.31) | copy-start | bytes 580
  25.1 7.6 %copy-start.12 = (s32[4]{0:T(128)S(1)}, s32[4]{0:T(128)}, u32[]{:S(2)}) copy-start(s32[4]{0:T(128)} %param.19) | copy-start | bytes 52
  25.1 13.5 %copy-start.4 = (bf16[24,768]{1,0:T(8,128)(2,1)S(1)}, bf16[24,768]{1,0:T(8,128)(2,1)}, u32[]{:S(2)}) copy-start(bf16[24,768]{1,0:T(8,128)(2,1)} %param.26) | copy-start | bytes 110596
  25.1 141.3 %all-gather.5.cloned.1.call-start = ((), (), s32[]{:S(2)}) async-start(), calls=%async_computation.7 | async-start | bytes 11151360 | tf_op jit(solution)/shard_map/all_gather | solution.py:733
  38.8 25.9 %copy-start.2 = (bf16[24,7040]{1,0:T(8,128)(2,1)}, bf16[24,7040]{1,0:T(8,128)(2,1)S(1)}, u32[]{:S(2)}) copy-start(bf16[24,7040]{1,0:T(8,128)(2,1)S(1)} %fusion) | copy-start | bytes 1013764
  59.6 5.1 %copy-start = (bf16[4,512,768]{2,1,0:T(8,128)(2,1)}, bf16[4,512,768]{2,1,0:T(8,128)(2,1)S(1)}, u32[]{:S(2)}) copy-start(bf16[4,512,768]{2,1,0:T(8,128)(2,1)S(1)} %all-to-all-done) | copy-start | bytes 9437188
  64.7 82.5 %all-to-all-start.1 = ((bf16[4,512,768]{2,1,0:T(8,128)(2,1)}), bf16[4,512,768]{2,1,0:T(8,128)(2,1)}, u32[]{:S(2)}, u32[]{:S(2)}) async-start(bf16[4,512,768]{2,1,0:T(8,128)(2,1)} %param.20), calls=%async_computation.1 | async-start | bytes 6291456 | tf_op jit(solution)/shard_map/all_to_all | solution.py:408
  69.3 309.4 %reduce-scatter.3.cloned.1.call-start = ((), (), s32[]{:S(2)}) async-start(), calls=%async_computation.8 | async-start | bytes 11943936 | tf_op jit(solution)/shard_map/reduce_scatter | solution.py:747
  266.4 98.9 %all-to-all-start.2 = ((bf16[4,512,768]{2,1,0:T(8,128)(2,1)}), bf16[4,512,768]{2,1,0:T(8,128)(2,1)S(1)}, u32[]{:S(2)}, u32[]{:S(2)}) async-start(bf16[4,512,768]{2,1,0:T(8,128)(2,1)} %bitcast.44), calls=%async_computation.2 | async-start | bytes 6291456 | tf_op jit(solution)/shard_map/all_to_all | solution.py:408
  270.1 154.5 %reduce-scatter.5.cloned.1.call-start = ((), (), s32[]{:S(2)}) async-start(), calls=%async_computation.9 | async-start | bytes 4202496 | tf_op jit(solution)/shard_map/reduce_scatter | solution.py:754
  380.9 21.3 %collective-permute-start.3 = (bf16[24,6912]{1,0:T(8,128)(2,1)}, bf16[24,6912]{1,0:T(8,128)(2,1)S(1)}, u32[]{:S(2)}, u32[]{:S(2)}) collective-permute-start(bf16[24,6912]{1,0:T(8,128)(2,1)} %get-tuple-element.83), channel_id=1, source_target_pairs={{0,1},{1,0},{2,3},{3,2},{4,5},{5,4},{6,7},{7,6},{8,9},{9,8},{10,11... | collective-permute-start | bytes 995336 | tf_op jit(solution)/shard_map/ppermute | solution.py:429
  382.8 19.5 %collective-permute-start.4 = (bf16[24,6912]{1,0:T(8,128)(2,1)}, bf16[24,6912]{1,0:T(8,128)(2,1)}, u32[]{:S(2)}, u32[]{:S(2)}) collective-permute-start(bf16[24,6912]{1,0:T(8,128)(2,1)} %get-tuple-element.85), channel_id=1, source_target_pairs={{0,2},{1,3},{2,0},{3,1},{4,6},{5,7},{6,4},{7,5},{8,10},{9,11},{10,... | collective-permute-start | bytes 995336 | tf_op jit(solution)/shard_map/ppermute | solution.py:429
  384.3 18.0 %collective-permute-start.5 = (bf16[24,6912]{1,0:T(8,128)(2,1)}, bf16[24,6912]{1,0:T(8,128)(2,1)}, u32[]{:S(2)}, u32[]{:S(2)}) collective-permute-start(bf16[24,6912]{1,0:T(8,128)(2,1)} %get-tuple-element.84), channel_id=1, source_target_pairs={{0,3},{1,2},{2,1},{3,0},{4,7},{5,6},{6,5},{7,4},{8,11},{9,10},{10,... | collective-permute-start | bytes 995336 | tf_op jit(solution)/shard_map/ppermute | solution.py:429
  397.4 48.0 %all-to-all-start.3 = ((bf16[4,512,768]{2,1,0:T(8,128)(2,1)}), bf16[4,512,768]{2,1,0:T(8,128)(2,1)}, u32[]{:S(2)}, u32[]{:S(2)}) async-start(bf16[4,512,768]{2,1,0:T(8,128)(2,1)} %bitcast.43), calls=%async_computation.4 | async-start | bytes 6291456 | tf_op jit(solution)/shard_map/all_to_all | solution.py:408
  403.6 0.9 copy-start.1
  425.7 16.5 %collective-permute-start = (bf16[24,2432]{1,0:T(8,128)(2,1)S(1)}, bf16[24,2432]{1,0:T(8,128)(2,1)S(1)}, u32[]{:S(2)}, u32[]{:S(2)}) collective-permute-start(bf16[24,2432]{1,0:T(8,128)(2,1)S(1)} %get-tuple-element.91), channel_id=1, source_target_pairs={{0,1},{1,0},{2,3},{3,2},{4,5},{5,4},{6,7},{7,6},{8,9},{9,8},{10,11... | collective-permute-start | bytes 350216 | tf_op jit(solution)/shard_map/ppermute | solution.py:429
  427.2 15.0 %collective-permute-start.1 = (bf16[24,2432]{1,0:T(8,128)(2,1)S(1)}, bf16[24,2432]{1,0:T(8,128)(2,1)S(1)}, u32[]{:S(2)}, u32[]{:S(2)}) collective-permute-start(bf16[24,2432]{1,0:T(8,128)(2,1)S(1)} %get-tuple-element.93), channel_id=1, source_target_pairs={{0,2},{1,3},{2,0},{3,1},{4,6},{5,7},{6,4},{7,5},{8,10},{9,11},{10,... | collective-permute-start | bytes 350216 | tf_op jit(solution)/shard_map/ppermute | solution.py:429
  428.7 15.7 %collective-permute-start.2 = (bf16[24,2432]{1,0:T(8,128)(2,1)S(1)}, bf16[24,2432]{1,0:T(8,128)(2,1)S(1)}, u32[]{:S(2)}, u32[]{:S(2)}) collective-permute-start(bf16[24,2432]{1,0:T(8,128)(2,1)S(1)} %get-tuple-element.92), channel_id=1, source_target_pairs={{0,3},{1,2},{2,1},{3,0},{4,7},{5,6},{6,5},{7,4},{8,11},{9,10},{10,... | collective-permute-start | bytes 350216 | tf_op jit(solution)/shard_map/ppermute | solution.py:429
Sparse Core Ops, SparseCore 0:
  21.2 43.3 all-gather.2
  68.2 98.1 all-gather.4
  266.5 109.1 reduce-scatter.2
  378.9 45.7 reduce-scatter.4
